TPU v7x, 32 devices: a whole 2x2x4 slice. The times are simulated.
32 devices in a mesh: tab: 2 (over x), fsdp: 16 (over z, y, core).
Axes of the slice: x: 2, y: 2, z: 4, core: 2. Of those that a mesh axis runs over, the one named last changes fastest.
Arguments:
- features: bfloat16 [16, 2048, 100], P('fsdp', 'tab'), may hold values from -6 to 6
- feature_counts: int32 [16], P('fsdp'), may hold values from 3 to 100
- row_flags: int32 [16, 2048], P('fsdp', 'tab'), may hold values from 0 to 1, as said below
- target_bins: int32 [16, 2048], P('fsdp', 'tab'), may hold values from 0 to 4999
- emb_weight: float32 [100, 768], P(None, 'fsdp'), may hold values from -0.625 to 0.625
- qkv_weight: float32 [768, 2304], P('fsdp'), may hold values from -0.21875 to 0.21875
- out_weight: float32 [768, 768], P('fsdp'), may hold values from -0.875 to 0.875
- up_weight: float32 [768, 3072], P('fsdp'), may hold values from -0.21875 to 0.21875
- down_weight: float32 [3072, 768], P('fsdp'), may hold values from -0.109375 to 0.109375
- head_weight: float32 [768, 5000], P('fsdp'), may hold values from -0.21875 to 0.21875
- vectors: float32 [4, 768], P(None, 'fsdp')
- mom_emb: float32 [100, 768], P(None, 'fsdp'), may hold values from -2.2888184e-05 to 2.2888184e-05
- mom_qkv: float32 [768, 2304], P('fsdp'), may hold values from -2.2888184e-05 to 2.2888184e-05
- mom_out: float32 [768, 768], P('fsdp'), may hold values from -2.2888184e-05 to 2.2888184e-05
- mom_up: float32 [768, 3072], P('fsdp'), may hold values from -2.2888184e-05 to 2.2888184e-05
- mom_down: float32 [3072, 768], P('fsdp'), may hold values from -2.2888184e-05 to 2.2888184e-05
- mom_head: float32 [768, 5000], P('fsdp'), may hold values from -2.2888184e-05 to 2.2888184e-05
- mom_vectors: float32 [4, 768], P(None, 'fsdp'), may hold values from -0.00010681152 to 0.00010681152
- ema_emb: float32 [100, 768], P(None, 'fsdp'), may hold values from -0.625 to 0.625
- ema_qkv: float32 [768, 2304], P('fsdp'), may hold values from -0.21875 to 0.21875
- ema_out: float32 [768, 768], P('fsdp'), may hold values from -0.875 to 0.875
- ema_up: float32 [768, 3072], P('fsdp'), may hold values from -0.21875 to 0.21875
- ema_down: float32 [3072, 768], P('fsdp'), may hold values from -0.109375 to 0.109375
- ema_head: float32 [768, 5000], P('fsdp'), may hold values from -0.21875 to 0.21875
- ema_vectors: float32 [4, 768], P(None, 'fsdp'), may hold values from 0.5 to 1.5
Outputs:
- loss_sum: float32 [], replicated
- row_count: float32 [], replicated
- rms_sums: float32 [3], replicated
- clip_norm: float32 [], replicated
- new_mom_emb: float32 [100, 768], P(None, 'fsdp')
- new_mom_qkv: float32 [768, 2304], P('fsdp')
- new_mom_out: float32 [768, 768], P('fsdp')
- new_mom_up: float32 [768, 3072], P('fsdp')
- new_mom_down: float32 [3072, 768], P('fsdp')
- new_mom_head: float32 [768, 5000], P('fsdp')
- new_mom_vectors: float32 [4, 768], P(None, 'fsdp')
- new_emb: float32 [100, 768], P(None, 'fsdp')
- new_qkv: float32 [768, 2304], P('fsdp')
- new_out: float32 [768, 768], P('fsdp')
- new_up: float32 [768, 3072], P('fsdp')
- new_down: float32 [3072, 768], P('fsdp')
- new_head: float32 [768, 5000], P('fsdp')
- new_vectors: float32 [4, 768], P(None, 'fsdp')
- new_ema_emb: float32 [100, 768], P(None, 'fsdp')
- new_ema_qkv: float32 [768, 2304], P('fsdp')
- new_ema_out: float32 [768, 768], P('fsdp')
- new_ema_up: float32 [768, 3072], P('fsdp')
- new_ema_down: float32 [3072, 768], P('fsdp')
- new_ema_head: float32 [768, 5000], P('fsdp')
- new_ema_vectors: float32 [4, 768], P(None, 'fsdp')
Inputs may be any that keep to these rules, and one draw needn't show every extreme that they name: `row_flags`: in every table the first row is a context row and the last a query row.
All inputs are finite; a program needn't handle non-finite values.
Results may differ from a plain program's by a relative error of at most 0.012.
The roundings to bfloat16 on the way count: a program that leaves them out, or rounds other values in their place, can miss the bound.
Values may be sent and summed in bfloat16 or wider, within the bound.
No kernel may reach another device: no remote copies, remote signals or barrier semaphores. Data moves between devices by JAX's collectives and lax.ppermute only.
A program may use at most 256 MiB of HBM per device.

v0:
```python
import jax
import jax.numpy as jnp
from jax import lax
from jax.sharding import PartitionSpec as P

HEADS = 12
BINS = 5000


CLIP = 0.005
RATE = 10000.0
MOMENTUM = 0.5
AVERAGE = 0.5


def matmul(left, right):
    return jnp.dot(left, right, preferred_element_type=jnp.float32)


def matmul_tn(left, right):
    return lax.dot_general(
        left, right, (((0,), (0,)), ((), ())), preferred_element_type=jnp.float32
    )


def matmul_nt(left, right):
    return lax.dot_general(
        left, right, (((1,), (1,)), ((), ())), preferred_element_type=jnp.float32
    )


def rms_norm(stream, gain):
    return stream * lax.rsqrt(jnp.mean(stream * stream, axis=-1, keepdims=True) + 1e-06) * gain


def row_rms(stream):
    return jnp.sqrt(jnp.mean(stream * stream, axis=-1) + 1e-06)


def rms_back(stream, gain, upstream):
    result, pullback = jax.vjp(rms_norm, stream, gain)
    return pullback(upstream)


def split_heads(block):
    rows, width = block.shape
    return block.reshape(rows, HEADS, width // HEADS).transpose(1, 0, 2)


def join_heads(block):
    count, rows, size = block.shape
    return block.transpose(1, 0, 2).reshape(rows, count * size)


def masked_scores(query_h, key_h, key_live):
    scale = query_h.shape[-1] ** (-0.5)
    return jnp.where(key_live[None, :], matmul_nt(query_h, key_h) * scale, -1e30)


def attend_forward(queries, keys_h, values_h, key_live):

    def per_head(items):
        query_h, key_h, value_h = items
        scores = masked_scores(query_h, key_h, key_live)
        top = jnp.max(scores, axis=1, keepdims=True)
        expo = jnp.exp(scores - top)
        total = jnp.sum(expo, axis=1, keepdims=True)
        weights_bf = (expo / total).astype(jnp.bfloat16)
        return (matmul(weights_bf, value_h), (top + jnp.log(total))[:, 0])

    return lax.map(per_head, (queries, keys_h, values_h))


def attend_backward(queries, keys_h, values_h, key_live, grad_heads, logsum):
    scale = queries.shape[-1] ** (-0.5)

    def per_head(items):
        query_h, key_h, value_h, grad_h, lse_h, delta_h = items
        probs = jnp.exp(masked_scores(query_h, key_h, key_live) - lse_h[:, None])
        dprob = matmul_nt(grad_h, value_h)
        delta = jnp.sum(dprob * probs, axis=1)
        dscore = (probs * (dprob - delta[:, None])).astype(jnp.bfloat16)
        grad_q = matmul(dscore, key_h) * scale
        grad_k = matmul_tn(dscore, query_h) * scale
        grad_v = matmul_tn(probs.astype(jnp.bfloat16), grad_h)
        return (grad_q, grad_k, grad_v, delta)

    return lax.map(per_head, (queries, keys_h, values_h, grad_heads, logsum, logsum))


def layer_forward(weights, stream0, context_bf):
    qkv_full, out_full, up_full, down_full, head_full, gains = weights
    width = qkv_full.shape[0]
    normed = rms_norm(stream0, gains[0]).astype(jnp.bfloat16)
    project = matmul(normed, qkv_full).astype(jnp.bfloat16)
    queries = project[:, :width]
    kv_all, context_all = (
        lax.all_gather(project[:, width:], "tab", axis=0, tiled=True),
        lax.all_gather(context_bf, "tab", axis=0, tiled=True),
    )
    key_live = context_all > 0
    keys_h = split_heads(kv_all[:, :width])
    values_h = split_heads(kv_all[:, width:])
    query_heads = split_heads(queries)
    attended, logsum = attend_forward(query_heads, keys_h, values_h, key_live)
    attended_bf = join_heads(attended).astype(jnp.bfloat16)
    attn_branch = matmul(attended_bf, out_full)
    stream1 = stream0 + attn_branch
    normed2 = rms_norm(stream1, gains[1]).astype(jnp.bfloat16)
    upper = matmul(normed2, up_full)
    activ = jax.nn.gelu(upper).astype(jnp.bfloat16)
    mlp_branch = matmul(activ, down_full)
    stream2 = stream1 + mlp_branch
    kept = (
        normed,
        query_heads,
        keys_h,
        values_h,
        key_live,
        logsum,
        attended_bf,
        stream1,
        normed2,
        upper,
        activ,
    )
    return (stream2, kept, (attn_branch, mlp_branch))


def layer_backward(weights, stream0, kept, grad_stream2):
    qkv_full, out_full, up_full, down_full, head_full, gains = weights
    (
        normed,
        query_heads,
        keys_h,
        values_h,
        key_live,
        logsum,
        attended_bf,
        stream1,
        normed2,
        upper,
        activ,
    ) = kept
    grad_m = grad_stream2.astype(jnp.bfloat16)
    grad_down = matmul_tn(activ, grad_m)
    grad_z = matmul_nt(grad_m, down_full)
    gelu_value, gelu_pull = jax.vjp(jax.nn.gelu, upper)
    grad_u = gelu_pull(grad_z)[0].astype(jnp.bfloat16)
    grad_up = matmul_tn(normed2, grad_u)
    grad_b = matmul_nt(grad_u, up_full)
    back_stream, grad_gain2 = rms_back(stream1, gains[1], grad_b)
    grad_stream1 = grad_stream2 + back_stream
    grad_a = grad_stream1.astype(jnp.bfloat16)
    grad_out = matmul_tn(attended_bf, grad_a)
    grad_o = matmul_nt(grad_a, out_full).astype(jnp.bfloat16)
    grad_heads = split_heads(grad_o)
    grad_q, grad_k, grad_v, row_delta = attend_backward(
        query_heads, keys_h, values_h, key_live, grad_heads, logsum
    )
    grad_kv_all = jnp.concatenate([join_heads(grad_k), join_heads(grad_v)], axis=1)
    grad_kv = lax.psum_scatter(grad_kv_all, "tab", scatter_dimension=0, tiled=True)
    grad_p = jnp.concatenate([join_heads(grad_q), grad_kv], axis=1).astype(jnp.bfloat16)
    grad_qkv = matmul_tn(normed, grad_p)
    grad_normed = matmul_nt(grad_p, qkv_full)
    back_zero, grad_gain1 = rms_back(stream0, gains[0], grad_normed)
    grad_stream0 = grad_stream1 + back_zero
    return (grad_stream0, grad_qkv, grad_out, grad_up, grad_down, grad_gain1, grad_gain2)


def on_device(
    features,
    feature_counts,
    row_flags,
    target_bins,
    emb_weight,
    qkv_weight,
    out_weight,
    up_weight,
    down_weight,
    head_weight,
    vectors,
    mom_emb,
    mom_qkv,
    mom_out,
    mom_up,
    mom_down,
    mom_head,
    mom_vectors,
    ema_emb,
    ema_qkv,
    ema_out,
    ema_up,
    ema_down,
    ema_head,
    ema_vectors,
):
    masters = (emb_weight, qkv_weight, out_weight, up_weight, down_weight, head_weight, vectors)
    moms = (mom_emb, mom_qkv, mom_out, mom_up, mom_down, mom_head, mom_vectors)
    emas = (ema_emb, ema_qkv, ema_out, ema_up, ema_down, ema_head, ema_vectors)
    lowered = [weight.astype(jnp.bfloat16) for weight in masters]
    gathered = (
        lax.all_gather(lowered[0], "fsdp", axis=1, tiled=True),
        lax.all_gather(lowered[1], "fsdp", axis=0, tiled=True),
        lax.all_gather(lowered[2], "fsdp", axis=0, tiled=True),
        lax.all_gather(lowered[3], "fsdp", axis=0, tiled=True),
        lax.all_gather(lowered[4], "fsdp", axis=0, tiled=True),
        lax.all_gather(lowered[5], "fsdp", axis=0, tiled=True),
        lax.all_gather(lowered[6], "fsdp", axis=1, tiled=True),
    )
    gains = gathered[6].astype(jnp.float32)
    weights = (gathered[1], gathered[2], gathered[3], gathered[4], gathered[5], gains)
    feats = features[0].astype(jnp.float32)
    count = feature_counts[0]
    flags = row_flags[0]
    targets = target_bins[0]
    nfeat = feats.shape[-1]
    keep = (jnp.arange(nfeat) < count).astype(jnp.float32)
    scale = jnp.sqrt(nfeat / count.astype(jnp.float32))
    x_in = (feats * keep[None, :] * scale).astype(jnp.bfloat16)
    context = (flags == 0).astype(jnp.float32)
    label = (targets.astype(jnp.float32) + 0.5) * (2.0 / BINS) - 1.0
    label_term = context * label
    stream0 = matmul(x_in, gathered[0]) + label_term[:, None] * gains[3][None, :]
    stream2, kept, branches = layer_forward(weights, stream0, context.astype(jnp.bfloat16))
    query = (flags == 1).astype(jnp.float32)
    local_stats = jnp.stack(
        [
            jnp.sum(query * row_rms(stream2)),
            jnp.sum(query * row_rms(branches[0])),
            jnp.sum(query * row_rms(branches[1])),
        ]
    )
    normed3 = rms_norm(stream2, gains[2]).astype(jnp.bfloat16)
    logits = matmul(normed3, gathered[5])
    top = jnp.max(logits, axis=-1, keepdims=True)
    expo = jnp.exp(logits - top)
    total = jnp.sum(expo, axis=-1, keepdims=True)
    logsum = top[:, 0] + jnp.log(total[:, 0])
    onehot = (jnp.arange(logits.shape[1], dtype=jnp.int32)[None, :] == targets[:, None]).astype(
        jnp.float32
    )
    target_logit = jnp.sum(logits * onehot, axis=-1)
    loss_sum, row_count, rms_sums = lax.psum(
        (jnp.sum((logsum - target_logit) * query), jnp.sum(query), local_stats), ("tab", "fsdp")
    )
    again = (
        lax.all_gather(lowered[1], "fsdp", axis=0, tiled=True),
        lax.all_gather(lowered[2], "fsdp", axis=0, tiled=True),
        lax.all_gather(lowered[3], "fsdp", axis=0, tiled=True),
        lax.all_gather(lowered[4], "fsdp", axis=0, tiled=True),
        lax.all_gather(lowered[5], "fsdp", axis=0, tiled=True),
        lax.all_gather(lowered[6], "fsdp", axis=1, tiled=True),
    )
    back_weights = (again[0], again[1], again[2], again[3], again[4], again[5].astype(jnp.float32))
    grad_logits = ((expo / total - onehot) * (query / row_count)[:, None]).astype(jnp.bfloat16)
    grad_head = matmul_tn(normed3, grad_logits)
    grad_f = matmul_nt(grad_logits, back_weights[4])
    grad_stream2, grad_gain3 = rms_back(stream2, back_weights[5][2], grad_f)
    grad_stream0, grad_qkv, grad_out, grad_up, grad_down, grad_gain1, grad_gain2 = layer_backward(
        back_weights, stream0, kept, grad_stream2
    )
    grad_emb = matmul_tn(x_in, grad_stream0.astype(jnp.bfloat16))
    grad_label = jnp.sum(label_term[:, None] * grad_stream0, axis=0)
    grad_vectors = jnp.stack([grad_gain1, grad_gain2, grad_gain3, grad_label], axis=0)
    owned = (
        lax.psum_scatter(grad_emb, "fsdp", scatter_dimension=1, tiled=True),
        lax.psum_scatter(grad_qkv, "fsdp", scatter_dimension=0, tiled=True),
        lax.psum_scatter(grad_out, "fsdp", scatter_dimension=0, tiled=True),
        lax.psum_scatter(grad_up, "fsdp", scatter_dimension=0, tiled=True),
        lax.psum_scatter(grad_down, "fsdp", scatter_dimension=0, tiled=True),
        lax.psum_scatter(grad_head, "fsdp", scatter_dimension=0, tiled=True),
        lax.psum_scatter(grad_vectors, "fsdp", scatter_dimension=1, tiled=True),
    )
    summed = lax.psum((owned[0], owned[1], owned[2], owned[3], owned[4], owned[5], owned[6]), "tab")
    squares = sum((jnp.sum(grad * grad) for grad in summed))
    clip_norm = jnp.sqrt(lax.psum(squares, "fsdp"))
    factor = jnp.minimum(1.0, CLIP / clip_norm)
    new_moms, new_weights, new_emas = ([], [], [])
    for weight, grad, moment, average in zip(masters, summed, moms, emas):
        clipped = grad * factor
        moment_new = MOMENTUM * moment + clipped
        weight_new = weight - RATE * (clipped + MOMENTUM * moment_new)
        new_moms.append(moment_new)
        new_weights.append(weight_new)
        new_emas.append(AVERAGE * average + (1.0 - AVERAGE) * weight_new)
    return (
        loss_sum,
        row_count,
        rms_sums,
        clip_norm,
        new_moms[0],
        new_moms[1],
        new_moms[2],
        new_moms[3],
        new_moms[4],
        new_moms[5],
        new_moms[6],
        new_weights[0],
        new_weights[1],
        new_weights[2],
        new_weights[3],
        new_weights[4],
        new_weights[5],
        new_weights[6],
        new_emas[0],
        new_emas[1],
        new_emas[2],
        new_emas[3],
        new_emas[4],
        new_emas[5],
        new_emas[6],
    )


def solution(mesh):
    return jax.shard_map(
        on_device,
        mesh=mesh,
        in_specs=(
            P("fsdp", "tab", None),
            P("fsdp"),
            P("fsdp", "tab"),
            P("fsdp", "tab"),
            P(None, "fsdp"),
            P("fsdp", None),
            P("fsdp", None),
            P("fsdp", None),
            P("fsdp", None),
            P("fsdp", None),
            P(None, "fsdp"),
            P(None, "fsdp"),
            P("fsdp", None),
            P("fsdp", None),
            P("fsdp", None),
            P("fsdp", None),
            P("fsdp", None),
            P(None, "fsdp"),
            P(None, "fsdp"),
            P("fsdp", None),
            P("fsdp", None),
            P("fsdp", None),
            P("fsdp", None),
            P("fsdp", None),
            P(None, "fsdp"),
        ),
        out_specs=(
            P(),
            P(),
            P(),
            P(),
            P(None, "fsdp"),
            P("fsdp", None),
            P("fsdp", None),
            P("fsdp", None),
            P("fsdp", None),
            P("fsdp", None),
            P(None, "fsdp"),
            P(None, "fsdp"),
            P("fsdp", None),
            P("fsdp", None),
            P("fsdp", None),
            P("fsdp", None),
            P("fsdp", None),
            P(None, "fsdp"),
            P(None, "fsdp"),
            P("fsdp", None),
            P("fsdp", None),
            P("fsdp", None),
            P("fsdp", None),
            P("fsdp", None),
            P(None, "fsdp"),
        ),
        check_vma=False,
    )
```

profile of v0, /device:TPU:0, one launch (start us, length us, event | category | flops | bytes accessed | tf_op | source)
XLA Modules:
  0.0 1680.8 jit_solution(3727176526476042687)
XLA Ops:
  9.7 23.1 %all-gather = bf16[16,48,4]{1,2,0:T(4,128)(2,1)S(1)} all-gather(bf16[1,48,4]{1,2,0:T(4,128)(2,1)S(1)} %convert_bitcast_fusion), channel_id=1, replica_groups=mesh['tab'=2,'fsdp'=16] {'fsdp'}, dimensions={0}, use_global_device_ids=true | all-gather | bytes 6528 | tf_op jit(solution)/shard_map/all_gather | solution.py:209
  34.4 18.6 %all_gather.33 = bf16[100,768]{0,1:T(8,128)(2,1)S(1)} all-gather(bf16[100,48]{0,1:T(8,128)(2,1)S(1)} %convert_element_type.121), channel_id=1, replica_groups=mesh['tab'=2,'fsdp'=16] {'fsdp'}, dimensions={1}, use_global_device_ids=true | all-gather | bytes 163200 | tf_op jit(solution)/shard_map/all_gather | solution.py:203
  57.4 4.0 all-gather.8.cloned.1.call-done
  61.4 6.3 convolution_convert_fusion
  76.4 4.3 all_gather.35
  85.8 65.9 %all-gather.10.cloned.1.call-done = bf16[2048,1536]{1,0:T(8,128)(2,1)} async-done(((bf16[1024,1536]{1,0:T(8,128)(2,1)}), bf16[2048,1536]{1,0:T(8,128)(2,1)}) %all-gather.10.cloned.1.call-update) | async-done | bytes 6291472 | tf_op jit(solution)/shard_map/all_gather | solution.py:98
  151.8 5.9 fusion.85
  157.6 4.7 copy.96
  162.3 6.6 copy.99
  168.9 4.7 copy.97
  173.6 6.7 copy.100
  181.7 111.5 %while.26 = (s32[]{:T(128)}, bf16[12,1024,64]{1,2,0:T(8,128)(2,1)}, f32[12,1024]{1,0:T(8,128)S(1)}, pred[2048]{0:T(1024)(128)(4,1)S(1)}, bf16[12,1024,64]{2,1,0:...) while((s32[]{:T(128)}, bf16[12,1024,64]{1,2,0:T(8,128)(2,1)}, ...), condition=%wide.region_4.5_spmd, body=%wide.region_1.4_spmd.sunk | while | flops 562035712 | bytes 26787944 | solution.py:71
  186.4 4.5 fusion.131
  195.7 4.5 fusion.131
  205.0 4.5 fusion.131
  214.3 4.5 fusion.131
  223.5 4.5 fusion.131
  232.8 4.5 fusion.131
  242.2 4.5 fusion.131
  251.5 4.5 fusion.131
  260.8 4.5 fusion.131
  270.1 4.5 fusion.131
  279.3 4.5 fusion.131
  288.6 4.5 fusion.131
  293.2 6.1 multiply_reduce_fusion.11
  299.4 14.7 multiply_convert_fusion.2
  314.1 11.0 multiply_reduce_fusion.10
  325.1 50.7 %all-gather.18.cloned.1.call-done = bf16[768,5000]{1,0:T(8,128)(2,1)} async-done(((bf16[48,5000]{1,0:T(8,128)(2,1)}), bf16[768,5000]{1,0:T(8,128)(2,1)}) %all-gather.18.cloned.1.call-update) | async-done | bytes 7680016 | tf_op jit(solution)/shard_map/all_gather | solution.py:208
  375.8 16.2 fusion.86
  391.9 9.9 fusion.53
  404.5 39.2 %all-reduce = (f32[]{:T(128)}, f32[]{:T(128)}, f32[3]{0:T(128)}) all-reduce(f32[]{:T(128)} %get-tuple-element.191, f32[]{:T(128)} %get-tuple-element.190, f32[3]{0:T(128)S(1)} %pad_maximum_fusion.5), channel_id=1, replica_groups=mesh['tab'=2,'fsdp'=16] {'tab','fsdp'}, use_global_device_ids=true, to_apply=%region_11.12 | all-reduce | flops 5 | bytes 40 | tf_op jit(solution)/shard_map/psum | solution.py:244
  444.4 14.7 multiply_convert_fusion.1
  459.1 14.2 multiply_reduce_fusion.2
  474.1 16.7 fusion.60
  490.8 8.2 multiply_reduce_fusion.3
  503.4 4.1 copy.103
  508.8 200.4 %while.27 = (s32[]{:T(128)}, bf16[12,1024,64]{1,2,0:T(8,128)(2,1)}, f32[12,2048,64]{1,2,0:T(8,128)}, f32[12,2048,64]{1,2,0:T(8,128)}, pred[2048]{0:T(1024)(128)(...) while((s32[]{:T(128)}, bf16[12,1024,64]{1,2,0:T(8,128)(2,1)}, ...), condition=%wide.region_24.25_spmd, body=%wide.region_22.24_spmd.sunk | while | flops 1373830144 | bytes 66886776 | solution.py:88
  521.9 3.6 fusion.143
  538.6 3.6 fusion.143
  555.3 3.6 fusion.143
  588.7 3.6 fusion.143
  605.4 3.6 fusion.143
  622.1 3.6 fusion.143
  638.8 3.6 fusion.143
  655.5 3.7 fusion.143
  672.2 3.6 fusion.143
  709.2 11.5 pad_maximum_fusion
  722.6 4.4 fusion.68
  727.0 11.2 fusion.80
  739.6 10.3 fusion.87
  751.8 15.3 fusion.82
  767.2 98.9 %reduce-scatter.11.cloned.1.call-done = f32[1024,1536]{0,1:T(8,128)} async-done(((f32[2048,1536]{0,1:T(8,128)}), f32[1024,1536]{0,1:T(8,128)}) %reduce-scatter.11.cloned.1.call-update) | async-done | bytes 6291472 | tf_op jit(solution)/shard_map/reduce_scatter | solution.py:162
  871.2 7.4 fusion.63
  879.3 7.5 multiply_reduce_fusion.4
  893.2 39.6 %reduce-scatter.17.cloned.1.call-done = f32[48,768]{1,0:T(8,128)} async-done(((f32[768,768]{1,0:T(8,128)}), f32[48,768]{1,0:T(8,128)}) %reduce-scatter.17.cloned.1.call-update) | async-done | bytes 147472 | tf_op jit(solution)/shard_map/reduce_scatter | solution.py:269
  932.8 115.1 %reduce-scatter.19.cloned.1.call-done = f32[48,3072]{1,0:T(8,128)} async-done(((f32[768,3072]{1,0:T(8,128)}), f32[48,3072]{1,0:T(8,128)}) %reduce-scatter.19.cloned.1.call-update) | async-done | bytes 589840 | tf_op jit(solution)/shard_map/reduce_scatter | solution.py:270
  1048.0 115.1 %reduce-scatter.21.cloned.1.call-done = f32[192,768]{1,0:T(8,128)} async-done(((f32[3072,768]{1,0:T(8,128)}), f32[192,768]{1,0:T(8,128)}) %reduce-scatter.21.cloned.1.call-update) | async-done | bytes 589840 | tf_op jit(solution)/shard_map/reduce_scatter | solution.py:271
  1163.0 161.3 %reduce-scatter.23.cloned.1.call-done = f32[48,5000]{1,0:T(8,128)} async-done(((f32[768,5000]{1,0:T(8,128)}), f32[48,5000]{1,0:T(8,128)}) %reduce-scatter.23.cloned.1.call-update) | async-done | bytes 960016 | tf_op jit(solution)/shard_map/reduce_scatter | solution.py:272
  1324.3 93.0 %reduce-scatter.15.cloned.1.call-done = f32[48,2304]{1,0:T(8,128)} async-done(((f32[768,2304]{1,0:T(8,128)}), f32[48,2304]{1,0:T(8,128)}) %reduce-scatter.15.cloned.1.call-update) | async-done | bytes 442384 | tf_op jit(solution)/shard_map/reduce_scatter | solution.py:268
  1417.4 59.5 %reduce-scatter.25.cloned.1.call-done = f32[48,4]{1,0:T(8,128)} async-done(((f32[768,4]{1,0:T(8,128)}), f32[48,4]{1,0:T(8,128)}) %reduce-scatter.25.cloned.1.call-update) | async-done | bytes 784
  1477.8 57.8 %reduce-scatter.13.cloned.1.call-done = f32[100,48]{0,1:T(8,128)} async-done(((f32[100,768]{0,1:T(8,128)}), f32[100,48]{0,1:T(8,128)}) %reduce-scatter.13.cloned.1.call-update) | async-done | bytes 19216 | tf_op jit(solution)/shard_map/reduce_scatter | solution.py:267
  1535.6 8.9 all-reduce.1
  1545.7 69.4 %all-reduce.5.cloned.1.call-done = (f32[48,2304]{1,0:T(8,128)}, f32[48,768]{1,0:T(8,128)}, f32[48,3072]{1,0:T(8,128)}, f32[192,768]{1,0:T(8,128)}, f32[48,5000]{1,0:T(8,128)}) async-done(((f32[48,2304]{1,0:T(8,128)}, f32[48,768]{1,0:T(8,128)}, f32[48,3072]{1,0:T(8,128)}, f32[192,768]{1,0:T(8,128)}, f32[48,5000]{1,0:T(8,128)}), (f32[48,2304]{1,0:T(8,128)}, f32[48,768]{1,0:T(8,128)}, f32[48,3072]{1,0:T(8,128)}, ...) | async-done | bytes 2729488 | tf_op jit(solution)/shard_map/psum | solution.py:275
  1628.7 33.7 %psum.87 = f32[]{:T(128)} all-reduce(f32[]{:T(128)S(6)} %add.249), channel_id=1, replica_groups=mesh['tab'=2,'fsdp'=16] {'fsdp'}, use_global_device_ids=true, to_apply=%region_52.53 | all-reduce | flops 1 | bytes 8 | tf_op jit(solution)/shard_map/psum | solution.py:277
  (341 shorter events, 294.9 us)
Async XLA Ops:
  7.2 54.2 %all-gather.8.cloned.1.call-start = ((), (), s32[]{:S(2)}) async-start(), calls=%async_computation.8 | async-start | bytes 3760128 | tf_op jit(solution)/shard_map/all_gather | solution.py:204
  9.0 142.8 %all-gather.10.cloned.1.call-start = ((), (), s32[]{:S(2)}) async-start(), calls=%async_computation.9 | async-start | bytes 9437184 | tf_op jit(solution)/shard_map/all_gather | solution.py:98
  53.0 8.3 copy-start.56
  54.4 7.0 copy-start.46
  54.4 444.6 %copy-start.39 = (f32[768]{0:T(1024)}, f32[768]{0:T(1024)S(1)}, u32[]{:S(2)}) copy-start(f32[768]{0:T(1024)S(1)} %get-tuple-element.181) | copy-start | bytes 9220
  56.8 10.9 copy-start
  57.4 4.0 copy-start.48
  67.7 2.1 copy-start.7
  69.8 2.0 copy-start.29
  71.8 2.9 copy-start.14
  71.8 3.7 copy-start.8
  71.8 9.0 slice-start
  71.8 221.4 %all-gather.12.cloned.1.call-start = ((), (), s32[]{:S(2)}) async-start(), calls=%async_computation.10 | async-start | bytes 1253376 | tf_op jit(solution)/shard_map/all_gather | solution.py:205
  72.5 226.8 %all-gather.14.cloned.1.call-start = ((), (), s32[]{:S(2)}) async-start(), calls=%async_computation.11 | async-start | bytes 5013504 | tf_op jit(solution)/shard_map/all_gather | solution.py:206
  74.6 239.5 %all-gather.16.cloned.1.call-start = ((), (), s32[]{:S(2)}) async-start(), calls=%async_computation.12 | async-start | bytes 5013504 | tf_op jit(solution)/shard_map/all_gather | solution.py:207
  75.4 300.4 %all-gather.18.cloned.1.call-start = ((), (), s32[]{:S(2)}) async-start(), calls=%async_computation.13 | async-start | bytes 8355840 | tf_op jit(solution)/shard_map/all_gather | solution.py:208
  76.3 789.7 %reduce-scatter.11.cloned.1.call-start = ((), (), s32[]{:S(2)}) async-start(), calls=%async_computation.14 | async-start | bytes 18874368 | tf_op jit(solution)/shard_map/reduce_scatter | solution.py:162
  325.1 173.9 %copy-start.41 = (f32[1024]{0:T(1024)}, f32[1024]{0:T(1024)S(1)}, u32[]{:S(2)}) copy-start(f32[1024]{0:T(1024)S(1)} %fusion.77) | copy-start | bytes 12292
  375.8 16.2 copy-start.43
  391.9 9.9 copy-start.50
  444.4 14.8 copy-start.2
  473.4 17.4 %slice-start.1 = ((s8[4718592]{0:T(1024)(128)(4,1)}), s8[4194304]{0:T(1024)(128)(4,1)S(1)}, s32[]{:S(2)}) async-start(s8[4718592]{0:T(1024)(128)(4,1)} %bitcast.180), calls=%async_computation.24 | async-start | bytes 8388608
  474.0 16.7 copy-start.20
  474.0 16.7 copy-start.11
  474.0 16.7 slice-start.2
  500.8 2.5 copy-start.4
  720.7 212.1 %reduce-scatter.17.cloned.1.call-start = ((), (), s32[]{:S(2)}) async-start(), calls=%async_computation.17 | async-start | bytes 2506752 | tf_op jit(solution)/shard_map/reduce_scatter | solution.py:269
  727.0 321.0 %reduce-scatter.19.cloned.1.call-start = ((), (), s32[]{:S(2)}) async-start(), calls=%async_computation.18 | async-start | bytes 10027008 | tf_op jit(solution)/shard_map/reduce_scatter | solution.py:270
  738.2 424.8 %reduce-scatter.21.cloned.1.call-start = ((), (), s32[]{:S(2)}) async-start(), calls=%async_computation.19 | async-start | bytes 10027008 | tf_op jit(solution)/shard_map/reduce_scatter | solution.py:271
  749.9 1.9 copy-start.42
  750.0 574.4 %reduce-scatter.23.cloned.1.call-start = ((), (), s32[]{:S(2)}) async-start(), calls=%async_computation.20 | async-start | bytes 16711680 | tf_op jit(solution)/shard_map/reduce_scatter | solution.py:272
  767.1 104.1 %copy-start.1 = (f32[1024,768]{0,1:T(8,128)S(1)}, f32[1024,768]{0,1:T(8,128)}, u32[]{:S(2)}) copy-start(f32[1024,768]{0,1:T(8,128)} %copy-done) | copy-start | bytes 9437188
  767.1 104.1 %copy-start.47 = (f32[768]{0:T(1024)S(1)}, f32[768]{0:T(1024)}, u32[]{:S(2)}) copy-start(f32[768]{0:T(1024)} %copy-done.46) | copy-start | bytes 9220
  767.1 104.1 %copy-start.49 = (f32[1024]{0:T(1024)S(1)}, f32[1024]{0:T(1024)}, u32[]{:S(2)}) copy-start(f32[1024]{0:T(1024)} %copy-done.48) | copy-start | bytes 12292
  767.1 650.2 %reduce-scatter.15.cloned.1.call-start = ((), (), s32[]{:S(2)}) async-start(), calls=%async_computation.16 | async-start | bytes 7520256 | tf_op jit(solution)/shard_map/reduce_scatter | solution.py:268
  866.0 5.1 copy-start.19
  878.6 598.4 %reduce-scatter.25.cloned.1.call-start = ((), (), s32[]{:S(2)}) async-start(), calls=%async_computation.21 | async-start | bytes 417792
  879.3 7.5 copy-start.38
  879.3 7.5 copy-start.6
  879.3 7.5 copy-start.36
  886.8 3.4 copy-start.24
  886.8 3.4 copy-start.57
  890.1 773.0 %copy-start.34 = (f32[100,48]{0,1:T(8,128)S(1)}, f32[100,48]{0,1:T(8,128)}, u32[]{:S(2)}) copy-start(f32[100,48]{0,1:T(8,128)} %param.33) | copy-start | bytes 57604
  890.1 773.0 %copy-start.44 = (f32[100,48]{0,1:T(8,128)S(1)}, f32[100,48]{0,1:T(8,128)}, u32[]{:S(2)}) copy-start(f32[100,48]{0,1:T(8,128)} %param.47) | copy-start | bytes 57604
  890.2 773.0 %copy-start.45 = (f32[100,48]{0,1:T(8,128)S(1)}, f32[100,48]{0,1:T(8,128)}, u32[]{:S(2)}) copy-start(f32[100,48]{0,1:T(8,128)} %param.40) | copy-start | bytes 57604
  890.2 773.7 %copy-start.18 = (f32[48,2304]{1,0:T(8,128)S(1)}, f32[48,2304]{1,0:T(8,128)}, u32[]{:S(2)}) copy-start(f32[48,2304]{1,0:T(8,128)} %param.34) | copy-start | bytes 1327108
  890.2 645.4 %reduce-scatter.13.cloned.1.call-start = ((), (), s32[]{:S(2)}) async-start(), calls=%async_computation.15 | async-start | bytes 417792 | tf_op jit(solution)/shard_map/reduce_scatter | solution.py:267
  893.2 722.0 %all-reduce.5.cloned.1.call-start = ((), (), s32[]{:S(2)}) async-start(), calls=%async_computation.22 | async-start | bytes 5505024 | tf_op jit(solution)/shard_map/psum | solution.py:275
  1417.4 249.0 %copy-start.30 = (f32[48,768]{1,0:T(8,128)S(1)}, f32[48,768]{1,0:T(8,128)}, u32[]{:S(2)}) copy-start(f32[48,768]{1,0:T(8,128)} %param.35) | copy-start | bytes 442372
  1417.4 249.0 %copy-start.32 = (f32[48,768]{1,0:T(8,128)S(1)}, f32[48,768]{1,0:T(8,128)}, u32[]{:S(2)}) copy-start(f32[48,768]{1,0:T(8,128)} %param.49) | copy-start | bytes 442372
  1417.4 249.0 %copy-start.33 = (f32[48,768]{1,0:T(8,128)S(1)}, f32[48,768]{1,0:T(8,128)}, u32[]{:S(2)}) copy-start(f32[48,768]{1,0:T(8,128)} %param.42) | copy-start | bytes 442372
  1417.4 249.8 %copy-start.13 = (f32[48,3072]{1,0:T(8,128)S(1)}, f32[48,3072]{1,0:T(8,128)}, u32[]{:S(2)}) copy-start(f32[48,3072]{1,0:T(8,128)} %param.36) | copy-start | bytes 1769476
  1417.4 249.8 %copy-start.25 = (f32[48,3072]{1,0:T(8,128)S(1)}, f32[48,3072]{1,0:T(8,128)}, u32[]{:S(2)}) copy-start(f32[48,3072]{1,0:T(8,128)} %param.50) | copy-start | bytes 1769476
  1417.4 249.8 %copy-start.26 = (f32[48,3072]{1,0:T(8,128)S(1)}, f32[48,3072]{1,0:T(8,128)}, u32[]{:S(2)}) copy-start(f32[48,3072]{1,0:T(8,128)} %param.43) | copy-start | bytes 1769476
  1615.1 51.2 %copy-start.31 = (f32[48,768]{1,0:T(8,128)S(1)}, f32[48,768]{1,0:T(8,128)}, u32[]{:S(2)}) copy-start(f32[48,768]{1,0:T(8,128)} %get-tuple-element.232) | copy-start | bytes 442372
  1615.1 52.0 %copy-start.17 = (f32[48,3072]{1,0:T(8,128)S(1)}, f32[48,3072]{1,0:T(8,128)}, u32[]{:S(2)}) copy-start(f32[48,3072]{1,0:T(8,128)} %get-tuple-element.233) | copy-start | bytes 1769476
  1663.2 5.4 copy-start.15
  1663.2 5.4 copy-start.16
  1663.2 5.4 copy-start.27
  1663.2 5.4 copy-start.28
  1667.2 2.8 copy-start.9
  1667.2 2.7 copy-start.10
  1667.2 2.7 copy-start.22
  1667.2 3.3 copy-start.23
  (13 other events, 19.7 us)
Sparse Core Ops, SparseCore 0:
  10.9 50.4 all-gather.7
  71.9 79.8 all-gather.9
  154.6 38.3 all-gather.11
  195.7 52.4 all-gather.13
  250.9 51.9 all-gather.15
  305.6 70.1 all-gather.17
  720.9 145.1 reduce-scatter.10
  869.8 62.9 reduce-scatter.16
  937.5 110.4 reduce-scatter.18
  1051.9 111.0 reduce-scatter.20
  1167.7 156.5 reduce-scatter.22
  1328.2 89.1 reduce-scatter.14
  1421.8 55.0 reduce-scatter.24
  1480.9 54.6 reduce-scatter.12
  1538.2 76.9 all-reduce.4
where the time goes:
time: 1690 us; the launch traced here: 1680 us
  waiting for transfers between devices  931 us (55%)
  matrix products  411 us (24%)
  other arithmetic  131 us (8%)
  blocking collectives  128 us (8%)
  local copies, waits for them, and re-layouts  55.7 us (3%)
  between operations  22.7 us (1%)
    reduce_scatter x1, waiting for transfers between devices, on_device(): lax.psum_scatter(grad_head, 'fsdp', scatter_dimension=0, tiled=True)  161 us
    dot_general x41, matrix products, matmul_nt(): lax.dot_general(left, right, (((1,), (1,)), ((), ())), preferred_element_...  149 us
    dot_general x30, matrix products, matmul(): return jnp.dot(left, right, preferred_element_type=jnp.float32)  147 us
    dot_general x30, matrix products, matmul_tn(): lax.dot_general(left, right, (((0,), (0,)), ((), ())), preferred_element_...  116 us
    reduce_scatter x1, waiting for transfers between devices, on_device(): lax.psum_scatter(grad_up, 'fsdp', scatter_dimension=0, tiled=True)  115 us
    reduce_scatter x1, waiting for transfers between devices, on_device(): lax.psum_scatter(grad_down, 'fsdp', scatter_dimension=0, tiled=True)  115 us
    reduce_scatter x1, waiting for transfers between devices, layer_backward(): lax.psum_scatter(grad_kv_all, 'tab', scatter_dimension=0, tiled=True)  98.9 us
    reduce_scatter x1, waiting for transfers between devices, on_device(): lax.psum_scatter(grad_qkv, 'fsdp', scatter_dimension=0, tiled=True)  93 us
  transfers between devices with their start and end apart: 15, of which 12 were waited for; matrix products, arithmetic and copies ran while one was open for 15% of the time, Pallas kernels for 0%

commit v1 on v0

v1 whole, which is shorter than its diff:
```python
import functools

import jax
import jax.numpy as jnp
import numpy as np
from jax import lax
from jax.experimental import pallas as pl
from jax.experimental.pallas import tpu as pltpu
from jax.sharding import PartitionSpec as P

HEADS = 12
BINS = 5000
CLIP = 0.005
RATE = 10000.0
MOMENTUM = 0.5
AVERAGE = 0.5

BF = jnp.bfloat16
F32 = jnp.float32
LANES = 128
QB = 256
CB = 512
HC = 512
VMEM = 60 * 1024 * 1024
LOW = -1e30


def mm(left, right):
    return jnp.dot(left, right, preferred_element_type=F32)


def mm_tn(left, right):
    return lax.dot_general(left, right, (((0,), (0,)), ((), ())), preferred_element_type=F32)


def mm_nt(left, right):
    return lax.dot_general(left, right, (((1,), (1,)), ((), ())), preferred_element_type=F32)


def iota(shape, axis):
    return lax.broadcasted_iota(jnp.int32, shape, axis)


def block(index, size):
    return pl.ds(pl.multiple_of(index * size, size), size)


def inverse_rms(stream):
    return lax.rsqrt(jnp.mean(stream * stream, axis=-1, keepdims=True) + 1e-06)


def rms_back(stream, gain, upstream):
    scale = inverse_rms(stream)
    unit = stream * scale
    weighted = upstream * gain
    back = scale * (weighted - unit * jnp.mean(weighted * unit, axis=-1, keepdims=True))
    return back, jnp.sum(upstream * unit, axis=0, keepdims=True)


def params(*semantics):
    return pltpu.CompilerParams(vmem_limit_bytes=VMEM)


def anywhere():
    return pl.BlockSpec(memory_space=pl.ANY)


def in_vmem():
    return pl.BlockSpec(memory_space=pltpu.VMEM)


def in_smem():
    return pl.BlockSpec(memory_space=pltpu.SMEM)


def shape(dims, dtype):
    return jax.ShapeDtypeStruct(dims, dtype)


class Group:
    def __init__(self, axis_bits, rows, parts, count):
        self.steps = axis_bits
        self.rows = rows
        self.parts = parts
        self.count = count
        self.width = sum(width * blocks for width, blocks in parts)
        self.pieces = 2 ** len(axis_bits)
        self.direct = rows % 16 == 0

    def place(self, piece, core):
        across, half = core, 0
        for bit, step in enumerate(self.steps):
            if piece >> bit & 1:
                if step == "tab":
                    half ^= 1
                else:
                    across ^= step
        return across, half

    def spans(self):
        start = 0
        for part, (width, blocks) in enumerate(self.parts):
            for at in range(blocks):
                yield part, start, width, at, blocks
                start += width

    def full_shapes(self):
        return [(2, self.count * self.rows * blocks, width) for width, blocks in self.parts]

    def table(self):
        order = np.zeros((2, self.count), np.int32)
        for core in range(2):
            for piece in range(self.pieces):
                across, half = self.place(piece, core)
                order[half, across] = core * self.pieces + piece
        return order

    def to_whole(self, near, far, me, tab):
        halves = np.arange(2, dtype=np.int32)[:, None] ^ tab
        places = np.arange(self.count, dtype=np.int32)[None, :] ^ me
        index = jnp.asarray(self.table())[halves, places]
        every = jnp.take(jnp.concatenate([near, far]), index, axis=0)
        whole = [[] for _ in self.parts]
        for part, start, width, _, _ in self.spans():
            whole[part].append(every[..., start : start + width])
        return [
            jnp.stack(found, axis=2).reshape(dims) for found, dims in zip(whole, self.full_shapes())
        ]

    def to_pieces(self, wholes, me, tab):
        columns = []
        for part, _, width, at, blocks in self.spans():
            split = wholes[part].reshape(2, self.count, blocks, self.rows, width)
            columns.append(split[:, :, at])
        every = jnp.concatenate(columns, axis=-1).reshape(2 * self.count, self.rows, self.width)
        where = np.array(
            [
                self.place(piece, core)
                for core in range(2)
                for piece in range(self.pieces)
            ],
            np.int32,
        )
        index = (where[:, 1] ^ tab) * self.count + (where[:, 0] ^ me)
        found = jnp.take(every, index, axis=0)
        return found[: self.pieces], found[self.pieces :]

    def load(self, sources, wholes, sems, me, tab):
        if not self.direct:
            for source, whole, sem in zip(sources, wholes, sems):
                pltpu.make_async_copy(source, whole, sem).start()
            return
        for core in range(2):
            for piece in range(self.pieces):
                across, half = self.place(piece, core)
                shard = lax.bitwise_xor(me, jnp.int32(across))
                side = lax.bitwise_xor(tab, jnp.int32(half))
                for part, start, width, at, blocks in self.spans():
                    first = pl.multiple_of((shard * blocks + at) * self.rows, self.rows)
                    pltpu.make_async_copy(
                        sources[core].at[piece, :, pl.ds(start, width)],
                        wholes[part].at[side, pl.ds(first, self.rows), :],
                        sems[part],
                    ).start()

    def store(self, wholes, targets, sems, me, tab, parts=None):
        if not self.direct:
            for whole, target, sem in zip(wholes, targets, sems):
                pltpu.make_async_copy(whole, target, sem).start()
            return
        for core in range(2):
            for piece in range(self.pieces):
                across, half = self.place(piece, core)
                shard = lax.bitwise_xor(me, jnp.int32(across))
                side = lax.bitwise_xor(tab, jnp.int32(half))
                for part, start, width, at, blocks in self.spans():
                    first = pl.multiple_of((shard * blocks + at) * self.rows, self.rows)
                    pltpu.make_async_copy(
                        wholes[part].at[side, pl.ds(first, self.rows), :],
                        targets[core].at[piece, :, pl.ds(start, width)],
                        sems[core],
                    ).start()

    def stored(self, targets, sems):
        for target, sem in zip(targets, sems):
            pltpu.make_async_copy(target, target, sem).wait()

    def out_shapes(self):
        if self.direct:
            return [shape((self.pieces, self.rows, self.width), BF)] * 2
        return [shape(dims, BF) for dims in self.full_shapes()]

    def sources(self, near, far, me, tab):
        return [near, far] if self.direct else self.to_whole(near, far, me, tab)

    def targets(self, outs, me, tab):
        return tuple(outs) if self.direct else self.to_pieces(outs, me, tab)


def loaded(whole, sem):
    pltpu.make_async_copy(whole, whole, sem).wait()


def swap(value, step, count):
    if step == "tab":
        return lax.ppermute(value, "tab", [(0, 1), (1, 0)])
    return lax.ppermute(value, "fsdp", [(i, i ^ step) for i in range(count)])


def gather_group(group, piece):
    held = piece[None]
    for step in group.steps:
        held = jnp.concatenate([held, swap(held, step, group.count)])
    return held, swap(held, 1, group.count)


def scatter_group(group, near, far):
    held = near + swap(far, 1, group.count)
    for step in reversed(group.steps):
        half = held.shape[0] // 2
        other = swap(held[half:], step, group.count)
        held = held[:half].astype(F32) + other.astype(F32)
        if half > 1:
            held = held.astype(BF)
    return held[0]


def sort_rows(nfeat, count, table, marks, x_query, t_query, x_context, y_context):
    total, _ = table.shape
    rows = total // LANES
    flags = marks[...]
    inside = mm(flags.astype(BF), (iota((LANES, LANES), 0) <= iota((LANES, LANES), 1)).astype(F32).astype(BF))
    sums = jnp.broadcast_to(jnp.sum(flags, axis=1, keepdims=True), (rows, LANES))
    below = (iota((rows, rows), 1) < iota((rows, rows), 0)).astype(F32)
    upto = inside + mm(below.astype(BF), sums.astype(BF))
    spot = (iota((rows, LANES), 0) * LANES + iota((rows, LANES), 1)).astype(F32)
    as_query = jnp.where(flags > 0, upto - 1.0, -1.0)
    as_context = jnp.where(flags > 0, -1.0, spot - upto)
    held = count[6]
    scale = jnp.sqrt(F32(nfeat) / jnp.full((1, LANES), held, jnp.int32).astype(F32))

    def pick(rank, dest):
        hot = jnp.concatenate(
            [(rank[k : k + 1, :] == dest).astype(F32).astype(BF) for k in range(rows)], axis=1
        )
        found = mm(hot, table[...])
        kept = jnp.where(iota(found.shape, 1) < held, found * scale, 0.0).astype(BF)
        return kept, found[:, nfeat + 1 : nfeat + 2] * 64.0 + found[:, nfeat + 2 : nfeat + 3]

    def query(i, _):
        dest = (2 * (i * QB + iota((QB, LANES), 0)) + count[5]).astype(F32)
        kept, target = pick(as_query, dest)
        x_query[block(i, QB), :] = kept
        t_query[block(i, QB), :] = jnp.broadcast_to(target, (QB, LANES))
        return 0

    def context(i, _):
        dest = i * QB + iota((QB, LANES), 0)
        kept, target = pick(as_context, dest.astype(F32))
        x_context[block(i, QB), :] = kept
        label = (jnp.broadcast_to(target, (QB, LANES)) + 0.5) * (2.0 / BINS) - 1.0
        y_context[block(i, QB), :] = jnp.where(dest < count[1], label, 0.0)
        return 0

    lax.fori_loop(0, count[2], query, 0)
    lax.fori_loop(0, count[3] * (CB // QB), context, 0)


def sort_rows_call(nfeat, count, table, marks):
    total = table.shape[0]
    local = total // 2
    return pl.pallas_call(
        functools.partial(sort_rows, nfeat),
        out_shape=(
            shape((local, LANES), BF),
            shape((local, LANES), F32),
            shape((total, LANES), BF),
            shape((total, LANES), F32),
        ),
        in_specs=[in_smem(), in_vmem(), in_vmem()],
        out_specs=(in_vmem(),) * 4,
        compiler_params=params(),
        name="sort_rows",
    )(count, table, marks)


def project(group, nfeat, count, x_query, x_context, y_context, *rest):
    sources = rest[: 2 if group.direct else 1]
    (q_out, k_out, v_out, aq_out, ac_out, h_out, gains, weight, sem) = rest[len(sources) :]
    step = pl.program_id(0)
    blocks_q = pl.num_programs(0) - k_blocks(ac_out, count)
    third = q_out.shape[1] // 2

    @pl.when(step == 0)
    def _():
        group.load(sources, [weight], [sem.at[0]], count[4], count[5])
        loaded(weight, sem.at[0])
        vectors = weight[1, :, 3 * third :].astype(F32).T
        embedding = weight[0, :, 3 * third :].astype(F32).T
        high = jnp.sum(vectors[4:5, :]) + jnp.sum(embedding[nfeat : nfeat + 1, :])
        low = jnp.sum(vectors[5:6, :]) + jnp.sum(embedding[nfeat + 1 : nfeat + 2, :])
        width = vectors.shape[1]
        gains[...] = jnp.where(iota((8, width), 0) < 4, vectors[:8, :], high * 32.0 + low)

    def normed(stream):
        return (stream * inverse_rms(stream) * gains[0:1, :]).astype(BF)

    @pl.when(step < count[2])
    def _():
        stream = mm_nt(x_query[...], weight[0, :, 3 * third :])
        h_out[...] = stream
        a = normed(stream)
        aq_out[...] = a
        for side in range(2):
            q_out[:, side * third : (side + 1) * third] = mm(a, weight[side, :, :third]).astype(BF)

    @pl.when((step >= blocks_q) & (step < blocks_q + count[3]))
    def _():
        stream = mm_nt(x_context[...], weight[0, :, 3 * third :]) + y_context[:, 0:1] * gains[3:4, :]
        a = normed(stream)
        ac_out[...] = a
        for side in range(2):
            columns = slice(side * third, (side + 1) * third)
            k_out[:, columns] = mm(a, weight[side, :, third : 2 * third]).astype(BF)
            v_out[:, columns] = mm(a, weight[side, :, 2 * third : 3 * third]).astype(BF)


def k_blocks(ref, count):
    return 4


def project_call(group, nfeat, count, x_query, x_context, y_context, sources, model):
    local, total = x_query.shape[0], x_context.shape[0]
    blocks_q, blocks_c = local // QB, total // CB
    assert blocks_c == 4

    def q_map(i, c):
        return (jnp.minimum(i, c[2] - 1), 0)

    def c_map(i, c):
        return (jnp.clip(i - blocks_q, 0, c[3] - 1), 0)

    def same(i, c):
        return (0, 0)

    return pl.pallas_call(
        functools.partial(project, group, nfeat),
        grid_spec=pltpu.PrefetchScalarGridSpec(
            num_scalar_prefetch=1,
            grid=(blocks_q + blocks_c,),
            in_specs=[
                pl.BlockSpec((QB, LANES), q_map),
                pl.BlockSpec((CB, LANES), c_map),
                pl.BlockSpec((CB, LANES), c_map),
            ]
            + [anywhere()] * len(sources),
            out_specs=(
                pl.BlockSpec((QB, model), q_map),
                pl.BlockSpec((CB, model), c_map),
                pl.BlockSpec((CB, model), c_map),
                pl.BlockSpec((QB, model), q_map),
                pl.BlockSpec((CB, model), c_map),
                pl.BlockSpec((QB, model), q_map),
                pl.BlockSpec((8, model), same),
            ),
            scratch_shapes=[
                pltpu.VMEM(group.full_shapes()[0], BF),
                pltpu.SemaphoreType.DMA((1,)),
            ],
        ),
        out_shape=(
            shape((local, model), BF),
            shape((total, model), BF),
            shape((total, model), BF),
            shape((local, model), BF),
            shape((total, model), BF),
            shape((local, model), F32),
            shape((8, model), F32),
        ),
        compiler_params=params(),
        name="project",
    )(count, x_query, x_context, y_context, *sources)


def head_masks(size):
    low = (iota((1, LANES), 1) < size).astype(F32)
    return low.astype(BF), (1.0 - low).astype(BF)


def dead_rows(j, count):
    return jnp.where(j * CB + iota((CB, 1), 0) < count[1], 0.0, LOW)


def attend(size, count, q_ref, k_ref, v_ref, o_ref, lse_ref):
    scale = size ** (-0.5)
    masks = head_masks(size)

    def over_queries(i, _):
        queries = q_ref[block(i, QB), :] * BF(scale)
        heads = [queries * mask for mask in masks]

        def over_context(j, carry):
            keys, values = k_ref[block(j, CB), :], v_ref[block(j, CB), :]
            dead = dead_rows(j, count)
            found = []
            for head, (top, total, sums) in zip(heads, carry):
                scores = mm_nt(keys, head) + dead
                top_new = jnp.maximum(top, jnp.max(scores, axis=0, keepdims=True))
                fade = jnp.exp(top - top_new)
                expo = jnp.exp(scores - top_new)
                total = total * fade + jnp.sum(expo, axis=0, keepdims=True)
                sums = sums * fade + mm_tn(values, expo.astype(BF))
                found.append((top_new, total, sums))
            return tuple(found)

        start = (
            jnp.full((1, QB), 3.0 * LOW, F32),
            jnp.zeros((1, QB), F32),
            jnp.zeros((LANES, QB), F32),
        )
        ends = lax.fori_loop(0, count[3], over_context, (start, start))
        joined = jnp.concatenate(
            [
                (sums / total)[side * size : (side + 1) * size]
                for side, (_, total, sums) in enumerate(ends)
            ]
        )
        o_ref[block(i, QB), :] = joined.T.astype(BF)
        for side, (top, total, _) in enumerate(ends):
            lse_ref[side : side + 1, block(i, QB)] = top + jnp.log(total)
        return 0

    lax.fori_loop(0, count[2], over_queries, 0)


def attend_call(size, count, queries, keys, values):
    local, model = queries.shape
    total = keys.shape[0]
    pairs = model // LANES

    def column(i, c):
        return (0, i)

    return pl.pallas_call(
        functools.partial(attend, size),
        grid_spec=pltpu.PrefetchScalarGridSpec(
            num_scalar_prefetch=1,
            grid=(pairs,),
            in_specs=[
                pl.BlockSpec((local, LANES), column),
                pl.BlockSpec((total, LANES), column),
                pl.BlockSpec((total, LANES), column),
            ],
            out_specs=(
                pl.BlockSpec((local, LANES), column),
                pl.BlockSpec((None, 8, local), lambda i, c: (i, 0, 0)),
            ),
        ),
        out_shape=(shape((local, model), BF), shape((pairs, 8, local), F32)),
        compiler_params=params(),
        name="attend",
    )(count, queries, keys, values)


def attend_back(size, count, q_ref, k_ref, v_ref, do_ref, o_ref, lse_ref, dq_ref, dk_ref, dv_ref, dk_sum, dv_sum):
    scale = size ** (-0.5)
    masks = head_masks(size)

    def clear(j, _):
        dk_sum[block(j, CB), :] = jnp.zeros((CB, LANES), F32)
        dv_sum[block(j, CB), :] = jnp.zeros((CB, LANES), F32)
        return 0

    lax.fori_loop(0, count[3], clear, 0)

    def over_queries(i, _):
        rows = block(i, QB)
        queries = q_ref[rows, :] * BF(scale)
        grads = do_ref[rows, :]
        heads = [queries * mask for mask in masks]
        ups = [grads * mask for mask in masks]
        both_q = jnp.concatenate(heads)
        both_up = jnp.concatenate(ups)
        product = (grads.astype(F32) * o_ref[rows, :].astype(F32)).T
        deltas = [
            jnp.sum(product[side * size : (side + 1) * size], axis=0, keepdims=True) for side in range(2)
        ]
        logs = [lse_ref[side : side + 1, rows] for side in range(2)]

        def over_context(j, carry):
            spot = block(j, CB)
            keys, values = k_ref[spot, :], v_ref[spot, :]
            dead = dead_rows(j, count)
            probs, scores_back = [], []
            for side in range(2):
                prob = jnp.exp(mm_nt(keys, heads[side]) + dead - logs[side])
                upper = mm_nt(values, ups[side])
                scores_back.append((prob * (upper - deltas[side])).astype(BF))
                probs.append(prob.astype(BF))
            dk_sum[spot, :] += mm(jnp.concatenate(scores_back, axis=1), both_q)
            dv_sum[spot, :] += mm(jnp.concatenate(probs, axis=1), both_up)
            return tuple(held + mm_tn(keys, back) for held, back in zip(carry, scores_back))

        zero = jnp.zeros((LANES, QB), F32)
        ends = lax.fori_loop(0, count[3], over_context, (zero, zero))
        joined = jnp.concatenate(
            [end[side * size : (side + 1) * size] for side, end in enumerate(ends)]
        )
        dq_ref[rows, :] = (joined.T * scale).astype(BF)
        return 0

    lax.fori_loop(0, count[2], over_queries, 0)

    def out(j, _):
        spot = block(j, CB)
        dk_ref[spot, :] = dk_sum[spot, :].astype(BF)
        dv_ref[spot, :] = dv_sum[spot, :].astype(BF)
        return 0

    lax.fori_loop(0, count[3], out, 0)


def attend_back_call(size, count, queries, keys, values, grads, outs, logs):
    local, model = queries.shape
    total = keys.shape[0]
    pairs = model // LANES

    def column(i, c):
        return (0, i)

    narrow = pl.BlockSpec((local, LANES), column)
    wide = pl.BlockSpec((total, LANES), column)
    return pl.pallas_call(
        functools.partial(attend_back, size),
        grid_spec=pltpu.PrefetchScalarGridSpec(
            num_scalar_prefetch=1,
            grid=(pairs,),
            in_specs=[
                narrow,
                wide,
                wide,
                narrow,
                narrow,
                pl.BlockSpec((None, 8, local), lambda i, c: (i, 0, 0)),
            ],
            out_specs=(narrow, wide, wide),
            scratch_shapes=[pltpu.VMEM((total, LANES), F32)] * 2,
        ),
        out_shape=(shape((local, model), BF), shape((total, model), BF), shape((total, model), BF)),
        compiler_params=params(),
        name="attend_back",
    )(count, queries, keys, values, grads, outs, logs)


def live_rows(i, count):
    return (i * QB + iota((QB, 1), 0) < count[0]).astype(F32)


def row_total(values, live):
    return jnp.sum(jnp.sqrt(jnp.mean(values * values, axis=-1, keepdims=True) + 1e-06) * live)


def gelu_both(value):
    inner = 0.7978845608028654 * (value + 0.044715 * value * value * value)
    bend = jnp.tanh(inner)
    slope = 0.7978845608028654 * (1.0 + 3.0 * 0.044715 * value * value)
    return 0.5 * value * (1.0 + bend), 0.5 * (1.0 + bend) + 0.5 * value * (1.0 - bend * bend) * slope


def feed(group, count, o_ref, h_ref, gains, *rest):
    sources = rest[: 2 if group.direct else 3]
    (h1_out, b_out, z_out, slope_out, h2_out, f_out, stats, w_out, w_up, w_down, sem) = rest[len(sources) :]
    step = pl.program_id(0)
    half = w_out.shape[2]
    hidden = w_up.shape[2]

    @pl.when(step == 0)
    def _():
        group.load(sources, [w_out, w_up, w_down], [sem.at[k] for k in range(3)], count[4], count[5])
        stats[...] = jnp.zeros(stats.shape, F32)
        for k, whole in enumerate((w_out, w_up, w_down)):
            loaded(whole, sem.at[k])

    @pl.when(step < count[2])
    def _():
        live = live_rows(step, count)
        attended = o_ref[...]
        branch = jnp.concatenate([mm(attended, w_out[0]), mm(attended, w_out[1])], axis=1)
        stream1 = h_ref[...] + branch
        h1_out[...] = stream1
        normed = (stream1 * inverse_rms(stream1) * gains[1:2, :]).astype(BF)
        b_out[...] = normed
        for side in range(2):

            def chunk(j, _, side=side):
                value, slope = gelu_both(mm(normed, w_up[side, :, block(j, HC)]))
                z_out[:, block(j + side * (hidden // HC), HC)] = value.astype(BF)
                slope_out[:, block(j + side * (hidden // HC), HC)] = slope.astype(BF)
                return 0

            lax.fori_loop(0, hidden // HC, chunk, 0)
        active = z_out[...]
        branch2 = jnp.concatenate([mm(active, w_down[0]), mm(active, w_down[1])], axis=1)
        stream2 = stream1 + branch2
        h2_out[...] = stream2
        f_out[...] = (stream2 * inverse_rms(stream2) * gains[2:3, :]).astype(BF)
        row = iota(stats.shape, 0)
        stats[...] += (
            jnp.where(row == 0, row_total(stream2, live), 0.0)
            + jnp.where(row == 1, row_total(branch, live), 0.0)
            + jnp.where(row == 2, row_total(branch2, live), 0.0)
        )


def feed_call(group, count, attended, stream0, gains, sources):
    local, model = attended.shape
    whole = group.full_shapes()
    hidden = whole[2][1]

    def rows(i, c):
        return (jnp.minimum(i, c[2] - 1), 0)

    def same(i, c):
        return (0, 0)

    narrow = pl.BlockSpec((QB, model), rows)
    wide = pl.BlockSpec((QB, hidden), rows)
    return pl.pallas_call(
        functools.partial(feed, group),
        grid_spec=pltpu.PrefetchScalarGridSpec(
            num_scalar_prefetch=1,
            grid=(local // QB,),
            in_specs=[narrow, narrow, pl.BlockSpec((8, model), same)] + [anywhere()] * len(sources),
            out_specs=(narrow, narrow, wide, wide, narrow, narrow, pl.BlockSpec((8, LANES), same)),
            scratch_shapes=[pltpu.VMEM(dims, BF) for dims in whole] + [pltpu.SemaphoreType.DMA((3,))],
        ),
        out_shape=(
            shape((local, model), F32),
            shape((local, model), BF),
            shape((local, hidden), BF),
            shape((local, hidden), BF),
            shape((local, model), F32),
            shape((local, model), BF),
            shape((8, LANES), F32),
        ),
        compiler_params=params(),
        name="feed",
    )(count, attended, stream0, gains, *sources)


def head(count, f_ref, t_ref, gains, weight, grad, df_ref, loss, logits, back, flipped):
    chunks = weight.shape[1] // HC
    loss[...] = jnp.zeros(loss.shape, F32)
    model = f_ref.shape[1]

    def over_rows(i, _):
        rows = block(i, QB)
        normed = f_ref[rows, :]
        flipped[:, rows] = normed.astype(F32).T.astype(BF)
        target = t_ref[rows, 0:1].astype(jnp.int32)
        live = live_rows(i, count)

        def column(j):
            return j * HC + iota((QB, HC), 1)

        def first(j, carry):
            top, hit = carry
            value = mm(normed, weight[:, block(j, HC)])
            place = column(j)
            value = jnp.where(place < BINS, value, LOW)
            logits[:, block(j, HC)] = value
            top = jnp.maximum(top, jnp.max(value, axis=1, keepdims=True))
            hit = hit + jnp.sum(jnp.where(place == target, value, 0.0), axis=1, keepdims=True)
            return top, hit

        top, hit = lax.fori_loop(
            0, chunks, first, (jnp.full((QB, 1), 3.0 * LOW, F32), jnp.zeros((QB, 1), F32))
        )

        def second(j, total):
            expo = jnp.exp(logits[:, block(j, HC)] - top)
            logits[:, block(j, HC)] = expo
            return total + jnp.sum(expo, axis=1, keepdims=True)

        total = lax.fori_loop(0, chunks, second, jnp.zeros((QB, 1), F32))
        weightf = live / gains[4:5, 0:1]
        share = 1.0 / total

        def third(j, held):
            hot = (column(j) == target).astype(F32)
            found = ((logits[:, block(j, HC)] * share - hot) * weightf).astype(BF)
            back[rows, block(j, HC)] = found
            return held + mm_nt(found, weight[:, block(j, HC)])

        df_ref[rows, :] = lax.fori_loop(0, chunks, third, jnp.zeros((QB, model), F32))
        loss[...] += jnp.sum(live * (top + jnp.log(total) - hit))
        return 0

    lax.fori_loop(0, count[2], over_rows, 0)

    def over_columns(j, _):
        def add(i, held):
            return held + mm(flipped[:, block(i, QB)], back[block(i, QB), block(j, HC)])

        grad[:, block(j, HC)] = lax.fori_loop(0, count[2], add, jnp.zeros((model, HC), F32)).astype(BF)
        return 0

    lax.fori_loop(0, chunks, over_columns, 0)


def head_call(count, normed, targets, gains, weight):
    local, model = normed.shape
    bins = weight.shape[1]
    return pl.pallas_call(
        head,
        out_shape=(shape((model, bins), BF), shape((local, model), F32), shape((8, LANES), F32)),
        in_specs=[in_smem()] + [in_vmem()] * 4,
        out_specs=(in_vmem(),) * 3,
        scratch_shapes=[
            pltpu.VMEM((QB, bins), F32),
            pltpu.VMEM((local, bins), BF),
            pltpu.VMEM((model, local), BF),
        ],
        compiler_params=params(),
        name="head",
    )(count, normed, targets, gains, weight)


def feed_back(group, count, df_ref, h2_ref, h1_ref, gains, o_any, b_any, z_any, slope_any, *rest):
    sources = rest[: 2 if group.direct else 3]
    rest = rest[len(sources) :]
    targets = rest[: len(group.out_shapes())]
    (
        dh1_out,
        do_out,
        gain_out,
        w_out,
        w_up,
        w_down,
        g_out,
        g_up,
        g_down,
        o_all,
        b_all,
        z_all,
        slope_all,
        dm_all,
        da_all,
        w_sem,
        r_sem,
        g_sem,
    ) = rest[len(targets) :]
    step = pl.program_id(0)
    half = w_out.shape[2]
    hidden = w_up.shape[2]
    per_side = hidden // HC
    rows = block(step, QB)
    loads = ((o_any, o_all), (b_any, b_all), (z_any, z_all), (slope_any, slope_all))

    @pl.when(step == 0)
    def _():
        group.load(sources, [w_out, w_up, w_down], [w_sem.at[k] for k in range(3)], count[4], count[5])
        gain_out[...] = jnp.zeros(gain_out.shape, F32)

        def fetch(i, _):
            for k, (source, target) in enumerate(loads):
                pltpu.make_async_copy(
                    source.at[block(i, QB)], target.at[block(i, QB)], r_sem.at[k, i]
                ).start()
            return 0

        lax.fori_loop(0, count[2], fetch, 0)
        for k, whole in enumerate((w_out, w_up, w_down)):
            loaded(whole, w_sem.at[k])

    @pl.when(step < count[2])
    def _():
        for k, (source, target) in enumerate(loads):
            pltpu.make_async_copy(source.at[rows], target.at[rows], r_sem.at[k, step]).wait()
        back, gain3 = rms_back(h2_ref[...], gains[2:3, :], df_ref[...])
        dm = back.astype(BF)
        dm_all[rows, :] = dm

        for side in range(2):

            def chunk(j, held, side=side):
                spot = block(j + side * per_side, HC)
                upper = mm_nt(dm[:, :half], w_down[0, spot, :]) + mm_nt(dm[:, half:], w_down[1, spot, :])
                found = (upper * slope_all[rows, spot].astype(F32)).astype(BF)
                slope_all[rows, spot] = found
                return held + mm_nt(found, w_up[side, :, block(j, HC)])

            db = lax.fori_loop(
                0, per_side, chunk, jnp.zeros(back.shape, F32) if side == 0 else db
            )
        back1, gain2 = rms_back(h1_ref[...], gains[1:2, :], db)
        stream = back + back1
        dh1_out[...] = stream
        da = stream.astype(BF)
        da_all[rows, :] = da
        do_out[...] = (mm_nt(da[:, :half], w_out[0]) + mm_nt(da[:, half:], w_out[1])).astype(BF)
        row = iota(gain_out.shape, 0)
        gain_out[...] += jnp.where(row == 1, gain2, 0.0) + jnp.where(row == 2, gain3, 0.0)

    @pl.when(step == pl.num_programs(0) - 1)
    def _():
        model = 2 * half

        for side in range(2):

            def columns(j, _, side=side):
                spot = block(j + side * per_side, HC)

                def add_up(i, held):
                    return held + mm_tn(b_all[block(i, QB), :], slope_all[block(i, QB), spot])

                g_up[side, :, block(j, HC)] = lax.fori_loop(
                    0, count[2], add_up, jnp.zeros((model, HC), F32)
                ).astype(BF)

                def add_down(i, held):
                    return held + mm_tn(z_all[block(i, QB), spot], dm_all[block(i, QB), :])

                down = lax.fori_loop(0, count[2], add_down, jnp.zeros((HC, model), F32)).astype(BF)
                g_down[0, spot, :] = down[:, :half]
                g_down[1, spot, :] = down[:, half:]
                return 0

            lax.fori_loop(0, per_side, columns, 0)

        def add_out(i, held):
            return held + mm_tn(o_all[block(i, QB), :], da_all[block(i, QB), :])

        whole = lax.fori_loop(0, count[2], add_out, jnp.zeros((model, model), F32)).astype(BF)
        g_out[0] = whole[:, :half]
        g_out[1] = whole[:, half:]
        sems = [g_sem.at[k] for k in range(len(targets))]
        group.store([g_out, g_up, g_down], targets, sems, count[4], count[5])
        group.stored(targets, sems)


def feed_back_call(group, count, df, stream2, stream1, gains, attended, normed, active, slope, sources):
    local, model = df.shape
    whole = group.full_shapes()
    hidden = whole[2][1]
    outs = group.out_shapes()

    def rows(i, c):
        return (jnp.minimum(i, c[2] - 1), 0)

    def same(i, c):
        return (0, 0)

    narrow = pl.BlockSpec((QB, model), rows)
    return pl.pallas_call(
        functools.partial(feed_back, group),
        grid_spec=pltpu.PrefetchScalarGridSpec(
            num_scalar_prefetch=1,
            grid=(local // QB,),
            in_specs=[narrow, narrow, narrow, pl.BlockSpec((8, model), same)]
            + [anywhere()] * (4 + len(sources)),
            out_specs=(anywhere(),) * len(outs) + (narrow, narrow, pl.BlockSpec((8, model), same)),
            scratch_shapes=[pltpu.VMEM(dims, BF) for dims in whole] * 2
            + [
                pltpu.VMEM((local, model), BF),
                pltpu.VMEM((local, model), BF),
                pltpu.VMEM((local, hidden), BF),
                pltpu.VMEM((local, hidden), BF),
                pltpu.VMEM((local, model), BF),
                pltpu.VMEM((local, model), BF),
                pltpu.SemaphoreType.DMA((3,)),
                pltpu.SemaphoreType.DMA((4, local // QB)),
                pltpu.SemaphoreType.DMA((3,)),
            ],
        ),
        out_shape=tuple(outs)
        + (shape((local, model), F32), shape((local, model), BF), shape((8, model), F32)),
        compiler_params=params(),
        name="feed_back",
    )(count, df, stream2, stream1, gains, attended, normed, active, slope, *sources)


def project_back(
    group, count, dq, aq, xq, dh1, h0, dk, dv, ac, xc, yc, gains, gains23, *rest
):
    sources = rest[: 2 if group.direct else 1]
    rest = rest[len(sources) :]
    targets = rest[: len(group.out_shapes())]
    weight, total, emb, small, out, sem, g_sem = rest[len(targets) :]
    step = pl.program_id(0)
    steps = pl.num_programs(0)
    blocks_q = steps - 4
    third = dq.shape[1] // 2

    @pl.when(step == 0)
    def _():
        group.load(sources, [weight], [sem.at[0]], count[4], count[5])
        total[...] = jnp.zeros(total.shape, F32)
        emb[...] = jnp.zeros(emb.shape, F32)
        small[...] = gains23[...]
        loaded(weight, sem.at[0])

    row = iota(small.shape, 0)

    @pl.when(step < count[2])
    def _():
        upper = jnp.zeros(dh1.shape, F32)
        a = aq[...]
        for side in range(2):
            grad = dq[:, side * third : (side + 1) * third]
            upper += mm_nt(grad, weight[side, :, :third])
            total[side, :, :third] += mm_tn(a, grad)
        back, gain1 = rms_back(h0[...], gains[0:1, :], upper)
        stream = dh1[...] + back
        emb[...] += mm_tn(stream.astype(BF), xq[...])
        small[...] += jnp.where(row == 0, gain1, 0.0)

    @pl.when((step >= blocks_q) & (step < blocks_q + count[3]))
    def _():
        a = ac[...]
        label = yc[:, 0:1]
        stream = mm_nt(xc[...], weight[0, :, 3 * third :]) + label * gains[3:4, :]
        upper = jnp.zeros(stream.shape, F32)
        for side in range(2):
            for part, ref in enumerate((dk, dv)):
                grad = ref[:, side * third : (side + 1) * third]
                columns = slice((part + 1) * third, (part + 2) * third)
                upper += mm_nt(grad, weight[side, :, columns])
                total[side, :, columns] += mm_tn(a, grad)
        back, gain1 = rms_back(stream, gains[0:1, :], upper)
        emb[...] += mm_tn(back.astype(BF), xc[...])
        small[...] += jnp.where(row == 0, gain1, 0.0) + jnp.where(
            row == 3, jnp.sum(label * back, axis=0, keepdims=True), 0.0
        )

    @pl.when(step == steps - 1)
    def _():
        for side in range(2):
            for part in range(3):
                columns = slice(part * third, (part + 1) * third)
                out[side, :, columns] = total[side, :, columns].astype(BF)
        out[0, :, 3 * third :] = emb[...].astype(BF)
        padded = jnp.concatenate([small[...], jnp.zeros((LANES - 8, small.shape[1]), F32)])
        out[1, :, 3 * third :] = padded.T.astype(BF)
        sems = [g_sem.at[k] for k in range(len(targets))]
        group.store([out], targets, sems, count[4], count[5])
        group.stored(targets, sems)


def project_back_call(group, count, dq, aq, xq, dh1, h0, dk, dv, ac, xc, yc, gains, gains23, sources):
    local, model = dq.shape
    total = dk.shape[0]
    blocks_q, blocks_c = local // QB, total // CB
    outs = group.out_shapes()

    def q_map(i, c):
        return (jnp.minimum(i, c[2] - 1), 0)

    def c_map(i, c):
        return (jnp.clip(i - blocks_q, 0, c[3] - 1), 0)

    def same(i, c):
        return (0, 0)

    query = pl.BlockSpec((QB, model), q_map)
    context = pl.BlockSpec((CB, model), c_map)
    thin = pl.BlockSpec((CB, LANES), c_map)
    fixed = pl.BlockSpec((8, model), same)
    whole = group.full_shapes()[0]
    return pl.pallas_call(
        functools.partial(project_back, group),
        grid_spec=pltpu.PrefetchScalarGridSpec(
            num_scalar_prefetch=1,
            grid=(blocks_q + blocks_c,),
            in_specs=[
                query,
                query,
                pl.BlockSpec((QB, LANES), q_map),
                query,
                query,
                context,
                context,
                context,
                thin,
                thin,
                fixed,
                fixed,
            ]
            + [anywhere()] * len(sources),
            out_specs=(anywhere(),) * len(outs),
            scratch_shapes=[
                pltpu.VMEM(whole, BF),
                pltpu.VMEM((2, whole[1], whole[2] - LANES), F32),
                pltpu.VMEM((model, LANES), F32),
                pltpu.VMEM((8, model), F32),
                pltpu.VMEM(whole, BF),
                pltpu.SemaphoreType.DMA((1,)),
                pltpu.SemaphoreType.DMA((2,)),
            ],
        ),
        out_shape=tuple(outs),
        compiler_params=params(),
        name="project_back",
    )(count, dq, aq, xq, dh1, h0, dk, dv, ac, xc, yc, gains, gains23, *sources)


def halves(tab, mine):
    other = swap(mine, "tab", 0)
    return jnp.where(tab == 0, mine, other), jnp.where(tab == 0, other, mine)


def on_device(
    count_fsdp,
    features,
    feature_counts,
    row_flags,
    target_bins,
    emb_weight,
    qkv_weight,
    out_weight,
    up_weight,
    down_weight,
    head_weight,
    vectors,
    mom_emb,
    mom_qkv,
    mom_out,
    mom_up,
    mom_down,
    mom_head,
    mom_vectors,
    ema_emb,
    ema_qkv,
    ema_out,
    ema_up,
    ema_down,
    ema_head,
    ema_vectors,
):
    masters = (emb_weight, qkv_weight, out_weight, up_weight, down_weight, head_weight, vectors)
    moms = (mom_emb, mom_qkv, mom_out, mom_up, mom_down, mom_head, mom_vectors)
    emas = (ema_emb, ema_qkv, ema_out, ema_up, ema_down, ema_head, ema_vectors)
    me = lax.axis_index("fsdp").astype(jnp.int32)
    tab = lax.axis_index("tab").astype(jnp.int32)
    local, nfeat = features.shape[1:]
    total = 2 * local
    rows = qkv_weight.shape[0]
    model = rows * count_fsdp
    half = model // 2
    hidden_half = up_weight.shape[1] // 2
    down_blocks = down_weight.shape[0] // rows
    size = model // HEADS
    flags = row_flags[0]
    targets = target_bins[0]

    high_bits = [1 << k for k in reversed(range(1, count_fsdp.bit_length() - 1))]
    group_a = Group(high_bits[:-1] + ["tab", high_bits[-1]], rows, [(3 * half + LANES, 1)], count_fsdp)
    group_b = Group(
        high_bits + ["tab"], rows, [(half, 1), (hidden_half, 1), (half, down_blocks)], count_fsdp
    )

    def side_of(weight, width):
        return jnp.where(tab == 0, weight[:, :width], weight[:, width : 2 * width])

    queries_here = jnp.sum(flags)
    marks = jnp.stack([queries_here // 32, queries_here % 32]).astype(F32)
    first_row = (jnp.arange(rows) == 0).astype(F32)[:, None]

    def tail(block_t):
        used = block_t.shape[0]
        return jnp.concatenate(
            [block_t.T, first_row * marks[None, :], jnp.zeros((rows, LANES - 2 - used), F32)], axis=1
        )

    piece_a = jnp.concatenate(
        [side_of(qkv_weight[:, k * model : (k + 1) * model], half) for k in range(3)]
        + [jnp.where(tab == 0, tail(emb_weight), tail(vectors))],
        axis=1,
    ).astype(BF)
    down_side = side_of(down_weight, half)
    piece_b = jnp.concatenate(
        [side_of(out_weight, half), side_of(up_weight, hidden_half)]
        + [down_side[k * rows : (k + 1) * rows] for k in range(down_blocks)],
        axis=1,
    ).astype(BF)
    bins = -(-head_weight.shape[1] // HC) * HC
    spare = bins - head_weight.shape[1]
    piece_h = jnp.pad(head_weight.astype(BF), ((0, 0), (0, spare)))

    near_a, far_a = gather_group(group_a, piece_a)
    near_b, far_b = gather_group(group_b, piece_b)
    head_full = lax.all_gather(piece_h, "fsdp", axis=0, tiled=True)

    pack = jnp.concatenate(
        [
            features[0],
            jnp.stack([flags, targets // 64, targets % 64], axis=1).astype(BF),
            jnp.zeros((local, LANES - 3 - nfeat), BF),
        ],
        axis=1,
    )
    lower, upper = halves(tab, pack)
    table = jnp.concatenate([lower, upper])
    flag_rows = table[:, nfeat].astype(F32).reshape(total // LANES, LANES)
    asked = jnp.sum(flag_rows).astype(jnp.int32)
    here = (asked - tab + 1) // 2
    known = total - asked
    count = jnp.stack(
        [
            here,
            known,
            jnp.maximum((here + QB - 1) // QB, 1),
            (known + CB - 1) // CB,
            me,
            tab,
            feature_counts[0],
            jnp.int32(0),
        ]
    )
    x_query, t_query, x_context, y_context = sort_rows_call(nfeat, count, table, flag_rows)

    sources_a = group_a.sources(near_a, far_a, me, tab)
    sources_b = group_b.sources(near_b, far_b, me, tab)
    queries, keys, values, a_query, a_context, stream0, gains = project_call(
        group_a, nfeat, count, x_query, x_context, y_context, sources_a, model
    )
    attended, logs = attend_call(size, count, queries, keys, values)
    stream1, normed2, active, slope, stream2, normed3, stats = feed_call(
        group_b, count, attended, stream0, gains, sources_b
    )
    grad_head, df, loss = head_call(count, normed3, t_query, gains, head_full)
    shard_h = lax.optimization_barrier(
        lax.psum_scatter(grad_head, "fsdp", scatter_dimension=0, tiled=True)
    )
    *outs_b, dh1, grad_o, gains23 = feed_back_call(
        group_b, count, df, stream2, stream1, gains, attended, normed2, active, slope, sources_b
    )
    shard_b = scatter_group(group_b, *group_b.targets(outs_b, me, tab))
    dq, dk, dv = attend_back_call(size, count, queries, keys, values, grad_o, attended, logs)
    outs_a = project_back_call(
        group_a,
        count,
        dq,
        a_query,
        x_query,
        dh1,
        stream0,
        dk,
        dv,
        a_context,
        x_context,
        y_context,
        gains,
        gains23,
        sources_a,
    )
    shard_a = scatter_group(group_a, *group_a.targets(outs_a, me, tab))

    shard_h = shard_h[:, : head_weight.shape[1]]
    grad_h = shard_h.astype(F32) + swap(shard_h, "tab", 0).astype(F32)
    a0, a1 = halves(tab, shard_a)
    b0, b1 = halves(tab, shard_b)
    grad_qkv = jnp.concatenate(
        [side[:, k * half : (k + 1) * half] for k in range(3) for side in (a0, a1)], axis=1
    )
    grad_emb = a0[:, 3 * half : 3 * half + nfeat].T
    grad_vectors = a1[:, 3 * half : 3 * half + vectors.shape[0]].T
    grad_out = jnp.concatenate([b0[:, :half], b1[:, :half]], axis=1)
    grad_up = jnp.concatenate([side[:, half : half + hidden_half] for side in (b0, b1)], axis=1)
    start = half + hidden_half
    grad_down = jnp.concatenate(
        [
            jnp.concatenate([side[:, start + k * half : start + (k + 1) * half] for side in (b0, b1)], axis=1)
            for k in range(down_blocks)
        ]
    )
    summed = (grad_emb, grad_qkv, grad_out, grad_up, grad_down, grad_h, grad_vectors)
    keep_a = jnp.where(
        jnp.arange(shard_a.shape[1])[None, :] < 3 * half + jnp.where(tab == 0, nfeat, vectors.shape[0]),
        shard_a,
        0.0,
    )
    squares = jnp.sum(keep_a * keep_a) + jnp.sum(shard_b * shard_b) + 0.5 * jnp.sum(grad_h * grad_h)
    sums = jnp.concatenate([loss[0:1, 0:1], stats[0:3, 0:1], squares.reshape(1, 1)]).reshape(1, 5)
    sums = jnp.broadcast_to(jnp.pad(sums, ((0, 0), (0, LANES - 5))), (8, LANES))
    for step in [1] + high_bits + ["tab"]:
        sums = sums + swap(sums, step, count_fsdp)
    loss_sum = sums[0, 0]
    rms_sums = sums[0, 1:4]
    clip_norm = jnp.sqrt(sums[0, 4])
    row_count = gains[4, 0]
    factor = jnp.minimum(1.0, CLIP / clip_norm)
    new_moms, new_weights, new_emas = ([], [], [])
    for weight, grad, moment, average in zip(masters, summed, moms, emas):
        clipped = grad * factor
        moment_new = MOMENTUM * moment + clipped
        weight_new = weight - RATE * (clipped + MOMENTUM * moment_new)
        new_moms.append(moment_new)
        new_weights.append(weight_new)
        new_emas.append(AVERAGE * average + (1.0 - AVERAGE) * weight_new)
    return (loss_sum, row_count, rms_sums, clip_norm, *new_moms, *new_weights, *new_emas)


def solution(mesh):
    by_row, by_column = P("fsdp", None), P(None, "fsdp")
    weights = (by_column, by_row, by_row, by_row, by_row, by_row, by_column)
    return jax.shard_map(
        functools.partial(on_device, mesh.shape["fsdp"]),
        mesh=mesh,
        in_specs=(P("fsdp", "tab", None), P("fsdp"), P("fsdp", "tab"), P("fsdp", "tab")) + weights * 3,
        out_specs=(P(), P(), P(), P()) + weights * 3,
        check_vma=False,
    )
```

time: 1690 us -> 675 us (0.40)
  waiting for transfers between devices: 931 us -> 290 us
  matrix products: 411 us -> 0 us
  Pallas kernels: 0 us -> 186 us
  blocking collectives: 128 us -> 0 us
  starting transfers between devices: 1.2 us -> 105 us
  other arithmetic: 131 us -> 36.2 us
  local copies, waits for them, and re-layouts: 55.7 us -> 29.4 us
    reduce_scatter x6 -> x0, waiting for transfers between devices: 520 us -> none  [the longest x1 115 us: on_device(): lax.psum_scatter(grad_up, 'fsdp', scatter_dimension=0, tiled=True)]
    dot_general x101 -> x0, matrix products: 411 us -> none  [the longest x41 149 us: matmul_nt(): lax.dot_general(left, right, (((1,), (1,)), ((), ())), preferred_element_...]
    ppermute x0 -> x29, waiting for transfers between devices: none -> 290 us  [the longest x20 200 us: swap(): return lax.ppermute(value, 'fsdp', [(i, i ^ step) for i in range(count)])]
    pallas_call x0 -> x8, Pallas kernels: none -> 186 us  [the longest x1 33.6 us: feed_back_call(): pl.pallas_call(functools.partial(feed_back, group), grid_spec=pltpu.Prefe...]
    reduce_scatter x1, waiting for transfers between devices: 161 us -> 0.01 us  [on_device(): lax.psum_scatter(grad_head, 'fsdp', scatter_dimension=0, tiled=True)]
    all_gather x6 -> x1, waiting for transfers between devices: 121 us -> 0.02 us  [on_device(): head_full = lax.all_gather(piece_h, 'fsdp', axis=0, tiled=True)]
    ppermute x0 -> x29, starting transfers between devices: none -> 105 us  [the longest x20 90.2 us: swap(): return lax.ppermute(value, 'fsdp', [(i, i ^ step) for i in range(count)])]
    psum x3 -> x0, blocking collectives: 81.8 us -> none  [the longest x1 39.2 us: on_device(): lax.psum((jnp.sum((logsum - target_logit) * query), jnp.sum(query), local...]
  transfers between devices with their start and end apart: 15 -> 31, of which waited for: 12 -> 22; matrix products, arithmetic and copies ran while one was open for 15% -> 7% of each run, Pallas kernels for 0% -> 18%
where the time goes in v1:
time: 675 us; the launch traced here: 669 us
  waiting for transfers between devices  290 us (43%)
  Pallas kernels  186 us (28%)
  starting transfers between devices  105 us (16%)
  other arithmetic  36.2 us (5%)
  local copies, waits for them, and re-layouts  29.4 us (4%)
  between operations  22.9 us (3%)
    ppermute x20, waiting for transfers between devices, swap(): return lax.ppermute(value, 'fsdp', [(i, i ^ step) for i in range(count)])  200 us
    ppermute x20, starting transfers between devices, swap(): return lax.ppermute(value, 'fsdp', [(i, i ^ step) for i in range(count)])  90.2 us
    ppermute x9, waiting for transfers between devices, swap(): return lax.ppermute(value, 'tab', [(0, 1), (1, 0)])  89.8 us
    pallas_call x1, Pallas kernels, feed_back_call(): pl.pallas_call(functools.partial(feed_back, group), grid_spec=pltpu.Prefe...  33.6 us
    pallas_call x1, Pallas kernels, head_call(): pl.pallas_call(head, out_shape=(shape((model, bins), BF), shape((local, m...  30.5 us
    pallas_call x1, Pallas kernels, project_back_call(): pl.pallas_call(functools.partial(project_back, group), grid_spec=pltpu.Pr...  28 us
    pallas_call x1, Pallas kernels, attend_call(): pl.pallas_call(functools.partial(attend, size), grid_spec=pltpu.PrefetchS...  26.9 us
    pallas_call x1, Pallas kernels, attend_back_call(): pl.pallas_call(functools.partial(attend_back, size), grid_spec=pltpu.Pref...  25.5 us
  transfers between devices with their start and end apart: 31, of which 22 were waited for; matrix products, arithmetic and copies ran while one was open for 7% of the time, Pallas kernels for 18%

profile of v1, /device:TPU:0, one launch (start us, length us, event | category | flops | bytes accessed | tf_op | source)
XLA Modules:
  0.0 669.4 jit_solution(63644141535059688)
XLA Ops:
  7.3 1.3 convert_element_type.129
  13.5 4.0 collective-permute-start.6
  17.5 28.9 %collective-permute-done.6 = bf16[1,48,3456]{2,1,0:T(8,128)(2,1)S(1)} collective-permute-done((bf16[1,48,3456]{2,1,0:T(8,128)(2,1)S(1)}, bf16[1,48,3456]{2,1,0:T(8,128)(2,1)S(1)}, u32[]{:S(2)}, u32[]{:S(2)}) %collective-permute-start.6) | collective-permute-done | bytes 331808 | tf_op jit(solution)/shard_map/ppermute | solution.py:207
  46.5 1.8 collective-permute-start.7
  48.3 31.9 %collective-permute-done.7 = bf16[2,48,3456]{2,1,0:T(8,128)(2,1)S(1)} collective-permute-done((bf16[2,48,3456]{2,1,0:T(8,128)(2,1)S(1)}, bf16[2,48,3456]{2,1,0:T(8,128)(2,1)S(1)}, u32[]{:S(2)}, u32[]{:S(2)}) %collective-permute-start.7) | collective-permute-done | bytes 663584 | tf_op jit(solution)/shard_map/ppermute | solution.py:207
  80.4 4.0 collective-permute-start.8
  84.5 22.3 %collective-permute-done.8 = bf16[4,48,3456]{2,1,0:T(8,128)(2,1)S(1)} collective-permute-done((bf16[4,48,3456]{2,1,0:T(8,128)(2,1)S(1)}, bf16[4,48,3456]{2,1,0:T(8,128)(2,1)S(1)}, u32[]{:S(2)}, u32[]{:S(2)}) %collective-permute-start.8) | collective-permute-done | bytes 1327136 | tf_op jit(solution)/shard_map/ppermute | solution.py:207
  106.8 1.7 pad_maximum_fusion
  108.4 1.5 collective-permute-start.9
  116.4 44.2 %collective-permute-done.9 = bf16[8,48,3456]{2,1,0:T(8,128)(2,1)} collective-permute-done((bf16[8,48,3456]{2,1,0:T(8,128)(2,1)}, bf16[8,48,3456]{2,1,0:T(8,128)(2,1)}, u32[]{:S(2)}, u32[]{:S(2)}) %collective-permute-start.9) | collective-permute-done | bytes 2654240 | tf_op jit(solution)/shard_map/ppermute | solution.py:206
  160.6 3.4 constant_dynamic-update-slice_fusion.11.rest_0_
  164.2 9.2 %collective-permute-start.1 = (bf16[1,48,1280]{2,1,0:T(8,128)(2,1)S(1)}, bf16[1,48,1280]{2,1,0:T(8,128)(2,1)S(1)}, u32[]{:S(2)}, u32[]{:S(2)}) collective-permute-start(bf16[1,48,1280]{2,1,0:T(8,128)(2,1)S(1)} %get-tuple-element.249), channel_id=1, source_target_pairs={{0,8},{1,9},{2,10},{3,11},{4,12},{5,13},{6,14},{7,15},{8,0},{9,1},... | collective-permute-start | bytes 368648 | tf_op jit(solution)/shard_map/ppermute | solution.py:207
  173.4 4.0 collective-permute-done.1
  177.4 3.4 collective-permute-start.2
  180.8 6.2 collective-permute-done.2
  187.1 2.7 collective-permute-start.3
  189.7 10.4 %collective-permute-done.3 = bf16[4,48,1280]{2,1,0:T(8,128)(2,1)S(1)} collective-permute-done((bf16[4,48,1280]{2,1,0:T(8,128)(2,1)S(1)}, bf16[4,48,1280]{2,1,0:T(8,128)(2,1)S(1)}, u32[]{:S(2)}, u32[]{:S(2)}) %collective-permute-start.3) | collective-permute-done | bytes 491552 | tf_op jit(solution)/shard_map/ppermute | solution.py:206
  201.5 20.9 %collective-permute-done.4 = bf16[8,48,1280]{2,1,0:T(8,128)(2,1)S(1)} collective-permute-done((bf16[8,48,1280]{2,1,0:T(8,128)(2,1)S(1)}, bf16[8,48,1280]{2,1,0:T(8,128)(2,1)S(1)}, u32[]{:S(2)}, u32[]{:S(2)}) %collective-permute-start.4) | collective-permute-done | bytes 983072 | tf_op jit(solution)/shard_map/ppermute | solution.py:207
  223.2 1.2 fusion.3
  224.5 1.5 concatenate.128
  226.0 1.5 collective-permute-start
  228.1 6.6 collective-permute-done
  238.1 8.2 %sort_rows.1 = (bf16[1024,128]{1,0:T(8,128)(2,1)}, f32[1024,128]{1,0:T(8,128)}, bf16[2048,128]{1,0:T(8,128)(2,1)}, f32[2048,128]{1,0:T(8,128)}) custom-call(s32[8]{0:T(128)} %stack.40.count, bf16[2048,128]{1,0:T(8,128)(2,1)} %pad_maximum_fusion.4.table, f32[16,128]{1,0:T(8,128)} %bitcast.101), custom_call_target="tpu_custom_call" | custom-call | tf_op jit(solution)/shard_map/sort_rows/pallas_call | solution.py:272
  246.3 17.5 %project.1 = (bf16[1024,768]{1,0:T(8,128)(2,1)}, bf16[2048,768]{1,0:T(8,128)(2,1)}, bf16[2048,768]{1,0:T(8,128)(2,1)}, bf16[1024,768]{1,0:T(8,128)(2,1)}, bf16[2...) custom-call(s32[8]{0:T(128)} %stack.40.count, bf16[1024,128]{1,0:T(8,128)(2,1)} %get-tuple-element.58.x_query.xq, ...), custom_call_target="tpu_custom_call" | custom-call | tf_op jit(solution)/shard_map/project/pallas_call | solution.py:346
  263.8 26.9 %attend.1 = (bf16[1024,768]{1,0:T(8,128)(2,1)}, f32[6,8,1024]{2,1,0:T(8,128)}) custom-call(s32[8]{0:T(128)} %stack.40.count, bf16[1024,768]{1,0:T(8,128)(2,1)} %get-tuple-element.61.q_ref, bf16[2048,768]{1,0:T(8,128)(2,1)} %get-tuple-element.62.k_ref, bf16[2048,768]{1,0:T(8,128)(2,1)} %get-tuple-element.63.v_ref), custom_call_target="tpu_custom_call" | custom-call | tf_op jit(solution)/shard_map/attend/pallas_call | solution.py:444
  290.7 15.8 %feed.1 = (f32[1024,768]{1,0:T(8,128)}, bf16[1024,768]{1,0:T(8,128)(2,1)}, bf16[1024,3072]{1,0:T(8,128)(2,1)}, bf16[1024,3072]{1,0:T(8,128)(2,1)}, f32[1024,768]...) custom-call(s32[8]{0:T(128)} %stack.40.count, bf16[1024,768]{1,0:T(8,128)(2,1)} %get-tuple-element.64.o_ref.o_any, ...), custom_call_target="tpu_custom_call" | custom-call | tf_op jit(solution)/shard_map/feed/pallas_call | solution.py:628
  306.5 30.5 %head.1 = (bf16[768,5120]{1,0:T(8,128)(2,1)}, f32[1024,768]{1,0:T(8,128)}, f32[8,128]{1,0:T(8,128)}) custom-call(s32[8]{0:T(128)} %stack.40.count, bf16[1024,768]{1,0:T(8,128)(2,1)} %get-tuple-element.67.f_ref, f32[1024,128]{1,0:T(8,128)} %get-tuple-element.68.t_ref, f32[8,768]{1,0:T(8,128)} %get-tuple-element.66.gains, ...), custom_call_target="tpu_custom_call" | custom-call | tf_op jit(solution)/shard_map/head/pallas_call | solution.py:714
  337.0 33.6 %feed_back.1 = (bf16[16,48,3456]{2,1,0:T(8,128)(2,1)}, bf16[16,48,3456]{2,1,0:T(8,128)(2,1)}, f32[1024,768]{1,0:T(8,128)}, bf16[1024,768]{1,0:T(8,128)(2,1)}, f32[8,768]{1,0:T(8,128)}) custom-call(s32[8]{0:T(128)} %stack.40.count, f32[1024,768]{1,0:T(8,128)} %get-tuple-element.71.df_ref, f32[1024,768]{1,0:T(8,128)} %get-tuple-element.72.h2_ref, ...), custom_call_target="tpu_custom_call" | custom-call | tf_op jit(solution)/shard_map/feed_back/pallas_call | solution.py:855
  370.7 9.1 %collective-permute-done.16 = bf16[16,48,3456]{2,1,0:T(8,128)(2,1)} collective-permute-done((bf16[16,48,3456]{2,1,0:T(8,128)(2,1)}, bf16[16,48,3456]{2,1,0:T(8,128)(2,1)}, u32[]{:S(2)}, u32[]{:S(2)}) %collective-permute-start.16) | collective-permute-done | bytes 5308448 | tf_op jit(solution)/shard_map/ppermute | solution.py:207
  379.8 5.4 add.178
  385.3 1.5 collective-permute-start.17
  387.5 25.5 %attend_back.1 = (bf16[1024,768]{1,0:T(8,128)(2,1)}, bf16[2048,768]{1,0:T(8,128)(2,1)}, bf16[2048,768]{1,0:T(8,128)(2,1)}) custom-call(s32[8]{0:T(128)} %stack.40.count, bf16[1024,768]{1,0:T(8,128)(2,1)} %get-tuple-element.61.q_ref, bf16[2048,768]{1,0:T(8,128)(2,1)} %get-tuple-element.62.k_ref, bf16[2048,768]{1,0:T(8,128)(2,1)} %get-tuple-element.63.v_ref, ...), custom_call_target="tpu_custom_call" | custom-call | tf_op jit(solution)/shard_map/attend_back/pallas_call | solution.py:533
  413.0 28.0 %project_back.1 = (bf16[16,48,1280]{2,1,0:T(8,128)(2,1)}, bf16[16,48,1280]{2,1,0:T(8,128)(2,1)}) custom-call(s32[8]{0:T(128)} %stack.40.count, bf16[1024,768]{1,0:T(8,128)(2,1)} %get-tuple-element.79.dq, bf16[1024,768]{1,0:T(8,128)(2,1)} %get-tuple-element.80.aq, bf16[1024,128]{1,0:T(8,128)(2,1)} %get-tuple-element.58.x_query.xq, ...), custom_call_target="tpu_custom_call" | custom-call | tf_op jit(solution)/shard_map/project_back/pallas_call | solution.py:970
  441.2 4.1 collective-permute-done.11
  445.4 2.2 add.173
  447.7 1.6 collective-permute-start.12
  449.3 2.5 add_convert_fusion
  452.7 35.5 %collective-permute-done.12 = bf16[8,48,1280]{2,1,0:T(8,128)(2,1)S(1)} collective-permute-done((bf16[8,48,1280]{2,1,0:T(8,128)(2,1)S(1)}, bf16[8,48,1280]{2,1,0:T(8,128)(2,1)S(1)}, u32[]{:S(2)}, u32[]{:S(2)}) %collective-permute-start.12) | collective-permute-done | bytes 983072 | tf_op jit(solution)/shard_map/ppermute | solution.py:207
  488.4 2.2 collective-permute-start.13
  490.7 8.9 %collective-permute-done.13 = bf16[4,48,1280]{2,1,0:T(8,128)(2,1)S(1)} collective-permute-done((bf16[4,48,1280]{2,1,0:T(8,128)(2,1)S(1)}, bf16[4,48,1280]{2,1,0:T(8,128)(2,1)S(1)}, u32[]{:S(2)}, u32[]{:S(2)}) %collective-permute-start.13) | collective-permute-done | bytes 491552 | tf_op jit(solution)/shard_map/ppermute | solution.py:206
  499.7 1.2 collective-permute-start.14
  501.0 20.2 %collective-permute-done.18 = bf16[4,48,3456]{2,1,0:T(8,128)(2,1)S(1)} collective-permute-done((bf16[4,48,3456]{2,1,0:T(8,128)(2,1)S(1)}, bf16[4,48,3456]{2,1,0:T(8,128)(2,1)S(1)}, u32[]{:S(2)}, u32[]{:S(2)}) %collective-permute-start.18) | collective-permute-done | bytes 1327136 | tf_op jit(solution)/shard_map/ppermute | solution.py:207
  523.9 1.2 slice.230
  527.0 45.7 %collective-permute-start.15 = (bf16[1,48,1280]{2,1,0:T(8,128)(2,1)S(1)}, bf16[1,48,1280]{2,1,0:T(8,128)(2,1)S(1)}, u32[]{:S(2)}, u32[]{:S(2)}) collective-permute-start(bf16[1,48,1280]{2,1,0:T(8,128)(2,1)S(1)} %slice.266), channel_id=1, source_target_pairs={{0,8},{1,9},{2,10},{3,11},{4,12},{5,13},{6,14},{7,15},{8,0},{9,1},... | collective-permute-start | bytes 368648 | tf_op jit(solution)/shard_map/ppermute | solution.py:207
  572.7 1.2 add_convert_fusion.3
  574.0 12.0 %collective-permute-start.20 = (bf16[1,48,3456]{2,1,0:T(8,128)(2,1)S(1)}, bf16[1,48,3456]{2,1,0:T(8,128)(2,1)S(1)}, u32[]{:S(2)}, u32[]{:S(2)}) collective-permute-start(bf16[1,48,3456]{2,1,0:T(8,128)(2,1)S(1)} %slice.274), channel_id=1, source_target_pairs={{0,8},{1,9},{2,10},{3,11},{4,12},{5,13},{6,14},{7,15},{8,0},{9,1},... | collective-permute-start | bytes 995336 | tf_op jit(solution)/shard_map/ppermute | solution.py:207
  586.0 1.9 collective-permute-start.27
  587.9 11.6 %collective-permute-done.20 = bf16[1,48,3456]{2,1,0:T(8,128)(2,1)S(1)} collective-permute-done((bf16[1,48,3456]{2,1,0:T(8,128)(2,1)S(1)}, bf16[1,48,3456]{2,1,0:T(8,128)(2,1)S(1)}, u32[]{:S(2)}, u32[]{:S(2)}) %collective-permute-start.20) | collective-permute-done | bytes 331808 | tf_op jit(solution)/shard_map/ppermute | solution.py:207
  599.6 1.9 collective-permute-start.28
  603.7 13.9 %collective-permute-done.28 = f32[48,3456]{1,0:T(8,128)} collective-permute-done((f32[48,3456]{1,0:T(8,128)S(1)}, f32[48,3456]{1,0:T(8,128)}, u32[]{:S(2)}, u32[]{:S(2)}) %collective-permute-start.28) | collective-permute-done | bytes 663584 | tf_op jit(solution)/shard_map/ppermute | solution.py:206
  617.6 1.9 broadcast_select_fusion.1
  620.8 4.7 collective-permute-done.21
  627.0 1.4 maximum_bitcast_fusion
  629.6 1.5 slice_dynamic-update-slice_fusion.2
  631.1 3.0 collective-permute-done.23
  634.1 2.4 collective-permute-start.24
  638.1 1.4 collective-permute-start.25
  639.5 1.5 slice_dynamic-update-slice_fusion
  641.7 1.7 collective-permute-start.26
  650.0 1.4 add_multiply_fusion.6
  651.4 2.6 add_multiply_fusion.3
  654.1 2.8 add_multiply_fusion.2
  657.8 1.4 add_multiply_fusion.1
  659.2 1.9 add_multiply_fusion
  (189 shorter events, 34.6 us)
Async XLA Ops:
  7.2 3.0 copy-start.7
  7.2 3.7 copy-start.5
  7.2 299.3 %all-gather.2.cloned.1.call-start = ((), (), s32[]{:S(2)}) async-start(), calls=%async_computation.1 | async-start | bytes 8355840 | tf_op jit(solution)/shard_map/all_gather | solution.py:1092
  9.5 593.4 %reduce-scatter.2.cloned.1.call-start = ((), (), s32[]{:S(2)}) async-start(), calls=%async_computation.2 | async-start | bytes 8355840 | tf_op jit(solution)/shard_map/reduce_scatter | solution.py:1133
  13.5 33.0 %collective-permute-start.6 = (bf16[1,48,3456]{2,1,0:T(8,128)(2,1)S(1)}, bf16[1,48,3456]{2,1,0:T(8,128)(2,1)S(1)}, u32[]{:S(2)}, u32[]{:S(2)}) collective-permute-start(bf16[1,48,3456]{2,1,0:T(8,128)(2,1)S(1)} %get-tuple-element.241), channel_id=1, source_target_pairs={{0,8},{1,9},{2,10},{3,11},{4,12},{5,13},{6,14},{7,15},{8,0},{9,1},... | collective-permute-start | bytes 995336 | tf_op jit(solution)/shard_map/ppermute | solution.py:207
  46.5 33.7 %collective-permute-start.7 = (bf16[2,48,3456]{2,1,0:T(8,128)(2,1)S(1)}, bf16[2,48,3456]{2,1,0:T(8,128)(2,1)S(1)}, u32[]{:S(2)}, u32[]{:S(2)}) collective-permute-start(bf16[2,48,3456]{2,1,0:T(8,128)(2,1)S(1)} %pad_maximum_fusion.3), channel_id=1, source_target_pairs={{0,4},{1,5},{2,6},{3,7},{4,0},{5,1},{6,2},{7,3},{8,12},{9,13},{10,... | collective-permute-start | bytes 1990664 | tf_op jit(solution)/shard_map/ppermute | solution.py:207
  80.4 29.5 %copy-start.33 = (s32[1,1024]{1,0:T(1,128)S(1)}, s32[1,1024]{1,0:T(1,128)}, u32[]{:S(2)}) copy-start(s32[1,1024]{1,0:T(1,128)} %param.27) | copy-start | bytes 12292
  80.4 32.8 %copy-start.35 = (f32[4,48]{1,0:T(4,128)S(1)}, f32[4,48]{1,0:T(4,128)}, u32[]{:S(2)}) copy-start(f32[4,48]{1,0:T(4,128)} %param.35) | copy-start | bytes 2308
  80.4 26.4 %collective-permute-start.8 = (bf16[4,48,3456]{2,1,0:T(8,128)(2,1)S(1)}, bf16[4,48,3456]{2,1,0:T(8,128)(2,1)S(1)}, u32[]{:S(2)}, u32[]{:S(2)}) collective-permute-start(bf16[4,48,3456]{2,1,0:T(8,128)(2,1)S(1)} %pad_maximum_fusion.1), channel_id=1, source_target_pairs={{0,2},{1,3},{2,0},{3,1},{4,6},{5,7},{6,4},{7,5},{8,10},{9,11},{10,... | collective-permute-start | bytes 3981320 | tf_op jit(solution)/shard_map/ppermute | solution.py:207
  108.4 52.2 %collective-permute-start.9 = (bf16[8,48,3456]{2,1,0:T(8,128)(2,1)}, bf16[8,48,3456]{2,1,0:T(8,128)(2,1)}, u32[]{:S(2)}, u32[]{:S(2)}) collective-permute-start(bf16[8,48,3456]{2,1,0:T(8,128)(2,1)} %pad_maximum_fusion), channel_id=1, source_target_pairs={{0,16},{16,0},{1,17},{17,1},{2,18},{18,2},{3,19},{19,3},{4,20},{20... | collective-permute-start | bytes 7962632 | tf_op jit(solution)/shard_map/ppermute | solution.py:206
  113.3 50.8 %copy-start.26 = (f32[4,48]{0,1:T(8,128)}, f32[4,48]{0,1:T(8,128)S(1)}, u32[]{:S(2)}) copy-start(f32[4,48]{0,1:T(8,128)S(1)} %copy.95) | copy-start | bytes 2308
  116.4 47.6 %copy-start.31 = (f32[100,48]{0,1:T(8,128)S(1)}, f32[100,48]{0,1:T(8,128)}, u32[]{:S(2)}) copy-start(f32[100,48]{0,1:T(8,128)} %param.29) | copy-start | bytes 57604
  116.4 47.7 %copy-start.9 = (f32[48,2304]{1,0:T(8,128)S(1)}, f32[48,2304]{1,0:T(8,128)}, u32[]{:S(2)}) copy-start(f32[48,2304]{1,0:T(8,128)} %param.30) | copy-start | bytes 1327108
  164.0 126.7 %collective-permute-start.10 = (bf16[16,48,3456]{2,1,0:T(8,128)(2,1)}, bf16[16,48,3456]{2,1,0:T(8,128)(2,1)}, u32[]{:S(2)}, u32[]{:S(2)}) collective-permute-start(bf16[16,48,3456]{2,1,0:T(8,128)(2,1)} %constant_dynamic-update-slice_fusion.11.rest_0_), channel_id=1, source_target_pairs={{0,1},{1,0},{2,3},{3,2},{4,5},{5,4},{6,7},{7,6},{8,9},{9,8},{10,11... | collective-permute-start | bytes 15925256 | tf_op jit(solution)/shard_map/ppermute | solution.py:207
  164.2 13.2 %collective-permute-start.1 = (bf16[1,48,1280]{2,1,0:T(8,128)(2,1)S(1)}, bf16[1,48,1280]{2,1,0:T(8,128)(2,1)S(1)}, u32[]{:S(2)}, u32[]{:S(2)}) collective-permute-start(bf16[1,48,1280]{2,1,0:T(8,128)(2,1)S(1)} %get-tuple-element.249), channel_id=1, source_target_pairs={{0,8},{1,9},{2,10},{3,11},{4,12},{5,13},{6,14},{7,15},{8,0},{9,1},... | collective-permute-start | bytes 368648 | tf_op jit(solution)/shard_map/ppermute | solution.py:207
  177.4 9.6 %collective-permute-start.2 = (bf16[2,48,1280]{2,1,0:T(8,128)(2,1)S(1)}, bf16[2,48,1280]{2,1,0:T(8,128)(2,1)S(1)}, u32[]{:S(2)}, u32[]{:S(2)}) collective-permute-start(bf16[2,48,1280]{2,1,0:T(8,128)(2,1)S(1)} %pad_maximum_fusion.6), channel_id=1, source_target_pairs={{0,4},{1,5},{2,6},{3,7},{4,0},{5,1},{6,2},{7,3},{8,12},{9,13},{10,... | collective-permute-start | bytes 737288 | tf_op jit(solution)/shard_map/ppermute | solution.py:207
  187.1 35.5 %copy-start.32 = (s32[1,1024]{1,0:T(1,128)S(1)}, s32[1,1024]{1,0:T(1,128)}, u32[]{:S(2)}) copy-start(s32[1,1024]{1,0:T(1,128)} %param.28) | copy-start | bytes 12292
  187.1 13.1 %collective-permute-start.3 = (bf16[4,48,1280]{2,1,0:T(8,128)(2,1)S(1)}, bf16[4,48,1280]{2,1,0:T(8,128)(2,1)S(1)}, u32[]{:S(2)}, u32[]{:S(2)}) collective-permute-start(bf16[4,48,1280]{2,1,0:T(8,128)(2,1)S(1)} %pad_maximum_fusion.5), channel_id=1, source_target_pairs={{0,16},{16,0},{1,17},{17,1},{2,18},{18,2},{3,19},{19,3},{4,20},{20... | collective-permute-start | bytes 1474568 | tf_op jit(solution)/shard_map/ppermute | solution.py:206
  200.3 22.8 %copy-start.28 = (bf16[1,1024,100]{1,2,0:T(8,128)(2,1)S(1)}, bf16[1,1024,100]{1,2,0:T(8,128)(2,1)}, u32[]{:S(2)}) copy-start(bf16[1,1024,100]{1,2,0:T(8,128)(2,1)} %param.25) | copy-start | bytes 614404
  200.3 22.1 %collective-permute-start.4 = (bf16[8,48,1280]{2,1,0:T(8,128)(2,1)S(1)}, bf16[8,48,1280]{2,1,0:T(8,128)(2,1)S(1)}, u32[]{:S(2)}, u32[]{:S(2)}) collective-permute-start(bf16[8,48,1280]{2,1,0:T(8,128)(2,1)S(1)} %pad_maximum_fusion.2), channel_id=1, source_target_pairs={{0,2},{1,3},{2,0},{3,1},{4,6},{5,7},{6,4},{7,5},{8,10},{9,11},{10,... | collective-permute-start | bytes 2949128 | tf_op jit(solution)/shard_map/ppermute | solution.py:207
  222.5 13.4 %copy-start.2 = (bf16[16,48,1280]{2,1,0:T(8,128)(2,1)}, bf16[16,48,1280]{2,1,0:T(8,128)(2,1)S(1)}, u32[]{:S(2)}) copy-start(bf16[16,48,1280]{2,1,0:T(8,128)(2,1)S(1)} %constant_dynamic-update-slice_fusion.rest_0_) | copy-start | bytes 5898244
  222.5 23.8 %collective-permute-start.5 = (bf16[16,48,1280]{2,1,0:T(8,128)(2,1)S(1)}, bf16[16,48,1280]{2,1,0:T(8,128)(2,1)}, u32[]{:S(2)}, u32[]{:S(2)}) collective-permute-start(bf16[16,48,1280]{2,1,0:T(8,128)(2,1)S(1)} %constant_dynamic-update-slice_fusion.rest_0_), channel_id=1, source_target_pairs={{0,1},{1,0},{2,3},{3,2},{4,5},{5,4},{6,7},{7,6},{8,9},{9,8},{10,11... | collective-permute-start | bytes 5898248 | tf_op jit(solution)/shard_map/ppermute | solution.py:207
  226.0 8.8 %collective-permute-start = (bf16[1024,128]{1,0:T(8,128)(2,1)S(1)}, bf16[1024,128]{1,0:T(8,128)(2,1)S(1)}, u32[]{:S(2)}, u32[]{:S(2)}) collective-permute-start(bf16[1024,128]{1,0:T(8,128)(2,1)S(1)} %concatenate.128), channel_id=1, source_target_pairs={{0,16},{16,0},{1,17},{17,1},{2,18},{18,2},{3,19},{19,3},{4,20},{20... | collective-permute-start | bytes 786440 | tf_op jit(solution)/shard_map/ppermute | solution.py:206
  370.6 9.2 %collective-permute-start.16 = (bf16[16,48,3456]{2,1,0:T(8,128)(2,1)}, bf16[16,48,3456]{2,1,0:T(8,128)(2,1)}, u32[]{:S(2)}, u32[]{:S(2)}) collective-permute-start(bf16[16,48,3456]{2,1,0:T(8,128)(2,1)} %get-tuple-element.89), channel_id=1, source_target_pairs={{0,1},{1,0},{2,3},{3,2},{4,5},{5,4},{6,7},{7,6},{8,9},{9,8},{10,11... | collective-permute-start | bytes 15925256 | tf_op jit(solution)/shard_map/ppermute | solution.py:207
  385.1 2.4 copy-start
  385.3 63.9 %collective-permute-start.17 = (bf16[8,48,3456]{2,1,0:T(8,128)(2,1)S(1)}, bf16[8,48,3456]{2,1,0:T(8,128)(2,1)}, u32[]{:S(2)}, u32[]{:S(2)}) collective-permute-start(bf16[8,48,3456]{2,1,0:T(8,128)(2,1)S(1)} %slice.268), channel_id=1, source_target_pairs={{0,16},{16,0},{1,17},{17,1},{2,18},{18,2},{3,19},{19,3},{4,20},{20... | collective-permute-start | bytes 7962632 | tf_op jit(solution)/shard_map/ppermute | solution.py:206
  441.0 4.3 collective-permute-start.11
  445.4 3.9 copy-start.1
  447.7 40.5 %collective-permute-start.12 = (bf16[8,48,1280]{2,1,0:T(8,128)(2,1)S(1)}, bf16[8,48,1280]{2,1,0:T(8,128)(2,1)S(1)}, u32[]{:S(2)}, u32[]{:S(2)}) collective-permute-start(bf16[8,48,1280]{2,1,0:T(8,128)(2,1)S(1)} %slice.260), channel_id=1, source_target_pairs={{0,2},{1,3},{2,0},{3,1},{4,6},{5,7},{6,4},{7,5},{8,10},{9,11},{10,... | collective-permute-start | bytes 2949128 | tf_op jit(solution)/shard_map/ppermute | solution.py:207
  451.8 69.3 %collective-permute-start.18 = (bf16[4,48,3456]{2,1,0:T(8,128)(2,1)S(1)}, bf16[4,48,3456]{2,1,0:T(8,128)(2,1)S(1)}, u32[]{:S(2)}, u32[]{:S(2)}) collective-permute-start(bf16[4,48,3456]{2,1,0:T(8,128)(2,1)S(1)} %slice.270), channel_id=1, source_target_pairs={{0,2},{1,3},{2,0},{3,1},{4,6},{5,7},{6,4},{7,5},{8,10},{9,11},{10,... | collective-permute-start | bytes 3981320 | tf_op jit(solution)/shard_map/ppermute | solution.py:207
  488.4 11.1 %collective-permute-start.13 = (bf16[4,48,1280]{2,1,0:T(8,128)(2,1)S(1)}, bf16[4,48,1280]{2,1,0:T(8,128)(2,1)S(1)}, u32[]{:S(2)}, u32[]{:S(2)}) collective-permute-start(bf16[4,48,1280]{2,1,0:T(8,128)(2,1)S(1)} %slice.262), channel_id=1, source_target_pairs={{0,16},{16,0},{1,17},{17,1},{2,18},{18,2},{3,19},{19,3},{4,20},{20... | collective-permute-start | bytes 1474568 | tf_op jit(solution)/shard_map/ppermute | solution.py:206
  499.7 22.8 %copy-start.34 = (f32[4,48]{1,0:T(4,128)S(1)}, f32[4,48]{1,0:T(4,128)}, u32[]{:S(2)}) copy-start(f32[4,48]{1,0:T(4,128)} %param.42) | copy-start | bytes 2308
  499.7 23.5 %copy-start.36 = (f32[4,48]{1,0:T(4,128)S(1)}, f32[4,48]{1,0:T(4,128)}, u32[]{:S(2)}) copy-start(f32[4,48]{1,0:T(4,128)} %param.49) | copy-start | bytes 2308
  499.7 25.4 %copy-start.37 = (f32[8,128]{1,0:T(8,128)S(1)}, f32[8,128]{1,0:T(8,128)}, u32[]{:S(2)}) copy-start(f32[8,128]{1,0:T(8,128)} %get-tuple-element.70) | copy-start | bytes 12292
  499.7 27.2 %collective-permute-start.14 = (bf16[2,48,1280]{2,1,0:T(8,128)(2,1)S(1)}, bf16[2,48,1280]{2,1,0:T(8,128)(2,1)S(1)}, u32[]{:S(2)}, u32[]{:S(2)}) collective-permute-start(bf16[2,48,1280]{2,1,0:T(8,128)(2,1)S(1)} %slice.264), channel_id=1, source_target_pairs={{0,4},{1,5},{2,6},{3,7},{4,0},{5,1},{6,2},{7,3},{8,12},{9,13},{10,... | collective-permute-start | bytes 737288 | tf_op jit(solution)/shard_map/ppermute | solution.py:207
  521.5 51.2 %collective-permute-start.19 = (bf16[2,48,3456]{2,1,0:T(8,128)(2,1)S(1)}, bf16[2,48,3456]{2,1,0:T(8,128)(2,1)}, u32[]{:S(2)}, u32[]{:S(2)}) collective-permute-start(bf16[2,48,3456]{2,1,0:T(8,128)(2,1)S(1)} %slice.272), channel_id=1, source_target_pairs={{0,4},{1,5},{2,6},{3,7},{4,0},{5,1},{6,2},{7,3},{8,12},{9,13},{10,... | collective-permute-start | bytes 1990664 | tf_op jit(solution)/shard_map/ppermute | solution.py:207
  527.0 59.0 %collective-permute-start.15 = (bf16[1,48,1280]{2,1,0:T(8,128)(2,1)S(1)}, bf16[1,48,1280]{2,1,0:T(8,128)(2,1)S(1)}, u32[]{:S(2)}, u32[]{:S(2)}) collective-permute-start(bf16[1,48,1280]{2,1,0:T(8,128)(2,1)S(1)} %slice.266), channel_id=1, source_target_pairs={{0,8},{1,9},{2,10},{3,11},{4,12},{5,13},{6,14},{7,15},{8,0},{9,1},... | collective-permute-start | bytes 368648 | tf_op jit(solution)/shard_map/ppermute | solution.py:207
  574.0 25.5 %collective-permute-start.20 = (bf16[1,48,3456]{2,1,0:T(8,128)(2,1)S(1)}, bf16[1,48,3456]{2,1,0:T(8,128)(2,1)S(1)}, u32[]{:S(2)}, u32[]{:S(2)}) collective-permute-start(bf16[1,48,3456]{2,1,0:T(8,128)(2,1)S(1)} %slice.274), channel_id=1, source_target_pairs={{0,8},{1,9},{2,10},{3,11},{4,12},{5,13},{6,14},{7,15},{8,0},{9,1},... | collective-permute-start | bytes 995336 | tf_op jit(solution)/shard_map/ppermute | solution.py:207
  586.0 15.5 %collective-permute-start.27 = (f32[48,1280]{1,0:T(8,128)S(1)}, f32[48,1280]{1,0:T(8,128)S(1)}, u32[]{:S(2)}, u32[]{:S(2)}) collective-permute-start(f32[48,1280]{1,0:T(8,128)S(1)} %add_bitcast_fusion.1), channel_id=1, source_target_pairs={{0,16},{16,0},{1,17},{17,1},{2,18},{18,2},{3,19},{19,3},{4,20},{20... | collective-permute-start | bytes 737288 | tf_op jit(solution)/shard_map/ppermute | solution.py:206
  599.6 18.0 %collective-permute-start.28 = (f32[48,3456]{1,0:T(8,128)S(1)}, f32[48,3456]{1,0:T(8,128)}, u32[]{:S(2)}, u32[]{:S(2)}) collective-permute-start(f32[48,3456]{1,0:T(8,128)S(1)} %add_bitcast_fusion), channel_id=1, source_target_pairs={{0,16},{16,0},{1,17},{17,1},{2,18},{18,2},{3,19},{19,3},{4,20},{20... | collective-permute-start | bytes 1990664 | tf_op jit(solution)/shard_map/ppermute | solution.py:206
  602.8 22.7 %copy-start.4 = (bf16[48,5120]{1,0:T(8,128)(2,1)S(1)}, bf16[48,5120]{1,0:T(8,128)(2,1)}, u32[]{:S(2)}) copy-start(bf16[48,5120]{1,0:T(8,128)(2,1)} %reduce-scatter.2.cloned.1.call-done) | copy-start | bytes 1474564
  602.8 22.7 %collective-permute-start.21 = (bf16[48,5000]{1,0:T(8,128)(2,1)}, bf16[48,5000]{1,0:T(8,128)(2,1)S(1)}, u32[]{:S(2)}, u32[]{:S(2)}) collective-permute-start(bf16[48,5000]{1,0:T(8,128)(2,1)} %bitcast.97), channel_id=1, source_target_pairs={{0,16},{16,0},{1,17},{17,1},{2,18},{18,2},{3,19},{19,3},{4,20},{20... | collective-permute-start | bytes 1440008 | tf_op jit(solution)/shard_map/ppermute | solution.py:206
  619.5 27.7 %copy-start.27 = (f32[4,48]{0,1:T(8,128)S(1)}, f32[4,48]{0,1:T(8,128)}, u32[]{:S(2)}) copy-start(f32[4,48]{0,1:T(8,128)} %copy-done.26) | copy-start | bytes 2308
  628.4 1.2 collective-permute-start.22
  629.6 4.5 collective-permute-start.23
  634.1 4.0 collective-permute-start.24
  638.1 3.6 collective-permute-start.25
  641.7 3.6 collective-permute-start.26
  644.2 9.7 %copy-start.8 = (f32[48,3072]{1,0:T(8,128)S(1)}, f32[48,3072]{1,0:T(8,128)}, u32[]{:S(2)}) copy-start(f32[48,3072]{1,0:T(8,128)} %param.32) | copy-start | bytes 1769476
  653.9 2.9 copy-start.16
  654.0 2.9 copy-start.17
  654.0 2.9 copy-start.29
  654.0 2.9 copy-start.30
  654.0 3.7 copy-start.6
  654.0 3.7 copy-start.13
  654.0 3.7 copy-start.14
  654.0 3.7 copy-start.18
  654.0 3.7 copy-start.19
  654.0 3.7 copy-start.20
  654.1 3.7 copy-start.21
  654.1 3.7 copy-start.22
  654.1 3.7 copy-start.23
  654.1 3.7 copy-start.24
  654.1 3.7 copy-start.25
  (5 other events, 10.8 us)
Sparse Core Ops, SparseCore 0:
  10.9 85.8 all-gather.1
  370.8 182.4 reduce-scatter.1

commit v2 on v1

v2 whole, which is shorter than its diff:
```python
import functools

import jax
import jax.numpy as jnp
import numpy as np
from jax import lax
from jax.experimental import pallas as pl
from jax.experimental.pallas import tpu as pltpu
from jax.sharding import PartitionSpec as P

HEADS = 12
BINS = 5000
CLIP = 0.005
RATE = 10000.0
MOMENTUM = 0.5
AVERAGE = 0.5

BF = jnp.bfloat16
F32 = jnp.float32
LANES = 128
QB = 256
AB = 256
FB = 256
RB = 512
CB = 512
HC = 512
VMEM = 60 * 1024 * 1024
LOW = -1e30


def mm(left, right):
    return jnp.dot(left, right, preferred_element_type=F32)


def mm_tn(left, right):
    return lax.dot_general(left, right, (((0,), (0,)), ((), ())), preferred_element_type=F32)


def mm_nt(left, right):
    return lax.dot_general(left, right, (((1,), (1,)), ((), ())), preferred_element_type=F32)


def iota(shape, axis):
    return lax.broadcasted_iota(jnp.int32, shape, axis)


def block(index, size):
    return pl.ds(pl.multiple_of(index * size, size), size)


def inverse_rms(stream):
    return lax.rsqrt(jnp.mean(stream * stream, axis=-1, keepdims=True) + 1e-06)


def rms_back(stream, gain, upstream):
    scale = inverse_rms(stream)
    unit = stream * scale
    weighted = upstream * gain
    back = scale * (weighted - unit * jnp.mean(weighted * unit, axis=-1, keepdims=True))
    return back, jnp.sum(upstream * unit, axis=0, keepdims=True)


def params():
    return pltpu.CompilerParams(vmem_limit_bytes=VMEM)


def cost(flops):
    return pl.CostEstimate(flops=int(flops), bytes_accessed=1 << 20, transcendentals=0)


def anywhere():
    return pl.BlockSpec(memory_space=pl.ANY)


def in_vmem():
    return pl.BlockSpec(memory_space=pltpu.VMEM)


def in_smem():
    return pl.BlockSpec(memory_space=pltpu.SMEM)


def shape(dims, dtype):
    return jax.ShapeDtypeStruct(dims, dtype)


class Group:
    def __init__(self, axis_bits, rows, parts, count):
        self.steps = axis_bits
        self.rows = rows
        self.parts = parts
        self.count = count
        self.width = sum(width * blocks for width, blocks in parts)
        self.pieces = 2 ** len(axis_bits)
        self.direct = rows % 16 == 0

    def place(self, piece, core):
        across, half = core, 0
        for bit, step in enumerate(self.steps):
            if piece >> bit & 1:
                if step == "tab":
                    half ^= 1
                else:
                    across ^= step
        return across, half

    def spans(self):
        start = 0
        for part, (width, blocks) in enumerate(self.parts):
            for at in range(blocks):
                yield part, start, width, at, blocks
                start += width

    def full_shapes(self):
        return [(self.count * self.rows * blocks, 2 * width) for width, blocks in self.parts]

    def table(self):
        order = np.zeros((self.count, 2), np.int32)
        for core in range(2):
            for piece in range(self.pieces):
                across, half = self.place(piece, core)
                order[across, half] = core * self.pieces + piece
        return order

    def to_whole(self, near, far, me, tab):
        places = np.arange(self.count, dtype=np.int32)[:, None] ^ me
        sides = np.arange(2, dtype=np.int32)[None, :] ^ tab
        index = jnp.asarray(self.table())[places, sides]
        every = jnp.take(jnp.concatenate([near, far]), index, axis=0)
        every = every.transpose(0, 2, 1, 3)
        whole = [[] for _ in self.parts]
        for part, start, width, _, _ in self.spans():
            whole[part].append(every[..., start : start + width])
        return [
            jnp.stack(found, axis=1).reshape(dims) for found, dims in zip(whole, self.full_shapes())
        ]

    def to_pieces(self, wholes, me, tab):
        columns = []
        for part, _, width, at, blocks in self.spans():
            split = wholes[part].reshape(self.count, blocks, self.rows, 2, width)
            columns.append(split[:, at])
        every = jnp.concatenate(columns, axis=-1).transpose(0, 2, 1, 3)
        every = every.reshape(2 * self.count, self.rows, self.width)
        where = np.array(
            [self.place(piece, core) for core in range(2) for piece in range(self.pieces)], np.int32
        )
        index = (where[:, 0] ^ me) * 2 + (where[:, 1] ^ tab)
        found = jnp.take(every, index, axis=0)
        return found[: self.pieces], found[self.pieces :]

    def pairs(self, wholes, moved, me, tab):
        for core in range(2):
            for piece in range(self.pieces):
                across, half = self.place(piece, core)
                shard = lax.bitwise_xor(me, jnp.int32(across))
                side = lax.bitwise_xor(tab, jnp.int32(half))
                for part, start, width, at, blocks in self.spans():
                    first = pl.multiple_of((shard * blocks + at) * self.rows, self.rows)
                    column = pl.multiple_of(side * width, LANES)
                    yield (
                        wholes[part].at[pl.ds(first, self.rows), pl.ds(column, width)],
                        moved[core].at[piece, :, pl.ds(start, width)],
                        part,
                        core,
                    )

    def load(self, sources, wholes, sems, me, tab):
        if not self.direct:
            for source, whole, sem in zip(sources, wholes, sems):
                pltpu.make_async_copy(source, whole, sem).start()
            return
        for whole, piece, part, _ in self.pairs(wholes, sources, me, tab):
            pltpu.make_async_copy(piece, whole, sems[part]).start()

    def store(self, wholes, targets, sems, me, tab):
        if not self.direct:
            for whole, target, sem in zip(wholes, targets, sems):
                pltpu.make_async_copy(whole, target, sem).start()
            return
        for whole, piece, _, core in self.pairs(wholes, targets, me, tab):
            pltpu.make_async_copy(whole, piece, sems[core]).start()

    def stored(self, targets, sems):
        for target, sem in zip(targets, sems):
            pltpu.make_async_copy(target, target, sem).wait()

    def out_shapes(self):
        if self.direct:
            return [shape((self.pieces, self.rows, self.width), BF)] * 2
        return [shape(dims, BF) for dims in self.full_shapes()]

    def sources(self, near, far, me, tab):
        return [near, far] if self.direct else self.to_whole(near, far, me, tab)

    def targets(self, outs, me, tab):
        return tuple(outs) if self.direct else self.to_pieces(outs, me, tab)


def loaded(whole, sem):
    pltpu.make_async_copy(whole, whole, sem).wait()


def swap(value, step, count):
    if step == "tab":
        return lax.ppermute(value, "tab", [(0, 1), (1, 0)])
    return lax.ppermute(value, "fsdp", [(i, i ^ step) for i in range(count)])


def after(value, *others):
    return lax.optimization_barrier((value, others))[0]


def gather_step(groups, held, at, *first):
    found = [swap(value, group.steps[at], group.count) for group, value in zip(groups, held)]
    found = after(found, *first)
    return [jnp.concatenate(both) for both in zip(held, found)]


def scatter_step(groups, held, at, *first):
    size = held[0].shape[0] // 2
    found = [swap(value[size:], group.steps[at], group.count) for group, value in zip(groups, held)]
    found = after(found, *first)
    kind = F32 if size == 1 else BF
    return [
        (value[:size].astype(F32) + other.astype(F32)).astype(kind) for value, other in zip(held, found)
    ]


def sort_rows(nfeat, count, table, marks, x_query, t_query, x_context, y_context):
    total, _ = table.shape
    rows = total // LANES
    flags = marks[...]
    inside = mm(flags.astype(BF), (iota((LANES, LANES), 0) <= iota((LANES, LANES), 1)).astype(F32).astype(BF))
    sums = jnp.broadcast_to(jnp.sum(flags, axis=1, keepdims=True), (rows, LANES))
    below = (iota((rows, rows), 1) < iota((rows, rows), 0)).astype(F32)
    upto = inside + mm(below.astype(BF), sums.astype(BF))
    spot = (iota((rows, LANES), 0) * LANES + iota((rows, LANES), 1)).astype(F32)
    as_query = jnp.where(flags > 0, upto - 1.0, -1.0)
    as_context = jnp.where(flags > 0, -1.0, spot - upto)
    held = count[6]
    scale = jnp.sqrt(F32(nfeat) / jnp.full((1, LANES), held, jnp.int32).astype(F32))

    def pick(rank, dest):
        hot = jnp.concatenate(
            [(rank[k : k + 1, :] == dest).astype(F32).astype(BF) for k in range(rows)], axis=1
        )
        found = mm(hot, table[...])
        kept = jnp.where(iota(found.shape, 1) < held, found * scale, 0.0).astype(BF)
        return kept, found[:, nfeat + 1 : nfeat + 2] * 64.0 + found[:, nfeat + 2 : nfeat + 3]

    def query(i, _):
        dest = (2 * (i * QB + iota((QB, LANES), 0)) + count[5]).astype(F32)
        kept, target = pick(as_query, dest)
        x_query[block(i, QB), :] = kept
        t_query[block(i, QB), :] = jnp.broadcast_to(target, (QB, LANES))
        return 0

    def context(i, _):
        dest = i * QB + iota((QB, LANES), 0)
        kept, target = pick(as_context, dest.astype(F32))
        x_context[block(i, QB), :] = kept
        label = (jnp.broadcast_to(target, (QB, LANES)) + 0.5) * (2.0 / BINS) - 1.0
        y_context[block(i, QB), :] = jnp.where(dest < count[1], label, 0.0)
        return 0

    lax.fori_loop(0, count[2] * (RB // QB), query, 0)
    lax.fori_loop(0, count[3] * (CB // QB), context, 0)


def sort_rows_call(nfeat, count, table, marks):
    total = table.shape[0]
    local = total // 2
    return pl.pallas_call(
        functools.partial(sort_rows, nfeat),
        out_shape=(
            shape((local, LANES), BF),
            shape((local, LANES), F32),
            shape((total, LANES), BF),
            shape((total, LANES), F32),
        ),
        in_specs=[in_smem(), in_vmem(), in_vmem()],
        out_specs=(in_vmem(),) * 4,
        compiler_params=params(),
        cost_estimate=cost(7e9),
        name="sort_rows",
    )(count, table, marks)


def project(nfeat, blocks, count, x_query, x_context, y_context, weight, q_out, k_out, v_out, aq_out, ac_out, h_out, gains):
    step = pl.program_id(0)
    model = q_out.shape[1]
    embed = slice(3 * model, 3 * model + LANES)

    @pl.when(step == 0)
    def _():
        vectors = weight[:, 3 * model + LANES :].astype(F32).T
        many = jnp.sum(vectors[4:5, :]) * 32.0 + jnp.sum(vectors[5:6, :])
        gains[...] = jnp.where(iota((8, model), 0) < 4, vectors[:8, :], many)

    def normed(stream):
        return (stream * inverse_rms(stream) * gains[0:1, :]).astype(BF)

    @pl.when(step < count[2])
    def _():
        stream = mm_nt(x_query[...], weight[:, embed])
        h_out[...] = stream
        a = normed(stream)
        aq_out[...] = a
        q_out[...] = mm(a, weight[:, :model]).astype(BF)

    @pl.when((step >= blocks) & (step < blocks + count[3]))
    def _():
        stream = mm_nt(x_context[...], weight[:, embed]) + y_context[:, 0:1] * gains[3:4, :]
        a = normed(stream)
        ac_out[...] = a
        k_out[...] = mm(a, weight[:, model : 2 * model]).astype(BF)
        v_out[...] = mm(a, weight[:, 2 * model : 3 * model]).astype(BF)


def project_call(nfeat, count, x_query, x_context, y_context, weight):
    local, total = x_query.shape[0], x_context.shape[0]
    model = weight.shape[0]
    blocks_q, blocks_c = local // RB, total // CB

    def q_map(i, c):
        return (jnp.minimum(i, c[2] - 1), 0)

    def c_map(i, c):
        return (jnp.clip(i - blocks_q, 0, c[3] - 1), 0)

    def same(i, c):
        return (0, 0)

    return pl.pallas_call(
        functools.partial(project, nfeat, blocks_q),
        grid_spec=pltpu.PrefetchScalarGridSpec(
            num_scalar_prefetch=1,
            grid=(blocks_q + blocks_c,),
            in_specs=[
                pl.BlockSpec((RB, LANES), q_map),
                pl.BlockSpec((CB, LANES), c_map),
                pl.BlockSpec((CB, LANES), c_map),
                pl.BlockSpec(weight.shape, same),
            ],
            out_specs=(
                pl.BlockSpec((RB, model), q_map),
                pl.BlockSpec((CB, model), c_map),
                pl.BlockSpec((CB, model), c_map),
                pl.BlockSpec((RB, model), q_map),
                pl.BlockSpec((CB, model), c_map),
                pl.BlockSpec((RB, model), q_map),
                pl.BlockSpec((8, model), same),
            ),
        ),
        out_shape=(
            shape((local, model), BF),
            shape((total, model), BF),
            shape((total, model), BF),
            shape((local, model), BF),
            shape((total, model), BF),
            shape((local, model), F32),
            shape((8, model), F32),
        ),
        compiler_params=params(),
        cost_estimate=cost(12e9),
        name="project",
    )(count, x_query, x_context, y_context, weight)


def head_masks(size):
    low = (iota((1, LANES), 1) < size).astype(F32)
    return low.astype(BF), (1.0 - low).astype(BF)


def dead_rows(j, count):
    return jnp.where(j * CB + iota((CB, 1), 0) < count[1], 0.0, LOW)


def clear_rest(ref, count):
    def clear(i, _):
        ref[block(i, QB), :] = jnp.zeros((QB, ref.shape[1]), ref.dtype)
        return 0

    lax.fori_loop(count[7], count[2] * (RB // QB), clear, 0)


def over_blocks(count, total, body):
    for blocks in range(1, total // CB + 1):

        @pl.when(count[3] == blocks)
        def _(blocks=blocks):
            body(blocks)


def context_scores(k_ref, head, blocks, count):
    scores = mm_nt(k_ref[: blocks * CB, :], head)
    tail = scores[-CB:] + dead_rows(blocks - 1, count)
    return tail if blocks == 1 else jnp.concatenate([scores[:-CB], tail])


def attend(size, count, q_ref, k_ref, v_ref, o_ref, lse_ref, v_low, v_high):
    scale = size ** (-0.5)
    masks = head_masks(size)

    def body(blocks):
        live = slice(0, blocks * CB)
        v_low[live, :] = v_ref[live, :] * masks[0] + masks[1]
        v_high[live, :] = v_ref[live, :] * masks[1] + masks[0]

        def over_queries(i, _):
            queries = q_ref[block(i, QB), :] * BF(scale)
            heads = [queries * mask for mask in masks]
            joined = []
            spots = [slice(j * AB, (j + 1) * AB) for j in range(blocks * CB // AB)]
            dead = dead_rows(blocks - 1, count)
            scores = [[mm_nt(k_ref[spot, :], head) for spot in spots] for head in heads]
            for side, parts in enumerate(scores):
                for k in range(CB // AB):
                    at = len(spots) - CB // AB + k
                    parts[at] = parts[at] + dead[k * AB : (k + 1) * AB]
                top = functools.reduce(jnp.maximum, [jnp.max(part, axis=0, keepdims=True) for part in parts])
                sums = jnp.zeros((LANES, QB), F32)
                for spot, part in zip(spots, parts):
                    expo = jnp.exp(part - top)
                    sums = sums + mm_tn((v_low, v_high)[side][spot, :], expo.astype(BF))
                total = sums[(1 - side) * size : (1 - side) * size + 1]
                joined.append((sums * (1.0 / total))[side * size : (side + 1) * size])
                lse_ref[side : side + 1, block(i, QB)] = top + jnp.log(total)
            o_ref[block(i, QB), :] = jnp.concatenate(joined).T.astype(BF)
            return 0

        lax.fori_loop(0, count[7], over_queries, 0)

    over_blocks(count, k_ref.shape[0], body)
    clear_rest(o_ref, count)


def attend_call(size, count, queries, keys, values):
    local, model = queries.shape
    total = keys.shape[0]
    pairs = model // LANES

    def column(i, c):
        return (0, i)

    return pl.pallas_call(
        functools.partial(attend, size),
        grid_spec=pltpu.PrefetchScalarGridSpec(
            num_scalar_prefetch=1,
            grid=(pairs,),
            in_specs=[
                pl.BlockSpec((local, LANES), column),
                pl.BlockSpec((total, LANES), column),
                pl.BlockSpec((total, LANES), column),
            ],
            out_specs=(
                pl.BlockSpec((local, LANES), column),
                pl.BlockSpec((None, 8, local), lambda i, c: (i, 0, 0)),
            ),
            scratch_shapes=[pltpu.VMEM((total, LANES), BF)] * 2,
        ),
        out_shape=(shape((local, model), BF), shape((pairs, 8, local), F32)),
        compiler_params=params(),
        cost_estimate=cost(35e9),
        name="attend",
    )(count, queries, keys, values)


def attend_back(size, count, q_ref, k_ref, v_ref, do_ref, o_ref, lse_ref, dq_ref, dk_ref, dv_ref, dk_sum, dv_sum):
    scale = size ** (-0.5)
    masks = head_masks(size)

    def body(blocks):
        def over_queries(i, _):
            rows = block(i, QB)
            queries = q_ref[rows, :] * BF(scale)
            grads = do_ref[rows, :]
            heads = [queries * mask for mask in masks]
            ups = [grads * mask for mask in masks]
            both_q = jnp.concatenate(heads)
            both_up = jnp.concatenate(ups)
            product = (grads.astype(F32) * o_ref[rows, :].astype(F32)).T
            back, probs, joined = [], [], []
            live = slice(0, blocks * CB)
            for side, head in enumerate(heads):
                delta = jnp.sum(product[side * size : (side + 1) * size], axis=0, keepdims=True)
                prob = jnp.exp(context_scores(k_ref, head, blocks, count) - lse_ref[side : side + 1, rows])
                upper = mm_nt(v_ref[live, :], ups[side])
                found = (prob * (upper - delta)).astype(BF)
                joined.append(mm_tn(k_ref[live, :], found)[side * size : (side + 1) * size])
                back.append(found)
                probs.append(prob.astype(BF))
            dq_ref[rows, :] = (jnp.concatenate(joined).T * scale).astype(BF)

            dk = mm(jnp.concatenate(back, axis=1), both_q)
            dv = mm(jnp.concatenate(probs, axis=1), both_up)
            dk_sum[live, :] = jnp.where(i == 0, 0.0, dk_sum[live, :]) + dk
            dv_sum[live, :] = jnp.where(i == 0, 0.0, dv_sum[live, :]) + dv
            return 0

        lax.fori_loop(0, count[7], over_queries, 0)

    over_blocks(count, k_ref.shape[0], body)
    clear_rest(dq_ref, count)

    def out(j, _):
        spot = block(j, CB)
        dk_ref[spot, :] = dk_sum[spot, :].astype(BF)
        dv_ref[spot, :] = dv_sum[spot, :].astype(BF)
        return 0

    lax.fori_loop(0, count[3], out, 0)


def attend_back_call(size, count, queries, keys, values, grads, outs, logs):
    local, model = queries.shape
    total = keys.shape[0]
    pairs = model // LANES

    def column(i, c):
        return (0, i)

    narrow = pl.BlockSpec((local, LANES), column)
    wide = pl.BlockSpec((total, LANES), column)
    return pl.pallas_call(
        functools.partial(attend_back, size),
        grid_spec=pltpu.PrefetchScalarGridSpec(
            num_scalar_prefetch=1,
            grid=(pairs,),
            in_specs=[
                narrow,
                wide,
                wide,
                narrow,
                narrow,
                pl.BlockSpec((None, 8, local), lambda i, c: (i, 0, 0)),
            ],
            out_specs=(narrow, wide, wide),
            scratch_shapes=[pltpu.VMEM((total, LANES), F32)] * 2,
        ),
        out_shape=(shape((local, model), BF), shape((total, model), BF), shape((total, model), BF)),
        compiler_params=params(),
        cost_estimate=cost(35e9),
        name="attend_back",
    )(count, queries, keys, values, grads, outs, logs)


def live_rows(i, count, size=RB):
    return (i * size + iota((size, 1), 0) < count[0]).astype(F32)


def row_total(values, live):
    return jnp.sum(jnp.sqrt(jnp.mean(values * values, axis=-1, keepdims=True) + 1e-06) * live)


def gelu_both(value):
    inner = 0.7978845608028654 * (value + 0.044715 * value * value * value)
    bend = jnp.tanh(inner)
    slope = 0.7978845608028654 * (1.0 + 3.0 * 0.044715 * value * value)
    return 0.5 * value * (1.0 + bend), 0.5 * (1.0 + bend) + 0.5 * value * (1.0 - bend * bend) * slope


def load_feed(groups, sources, wholes, sem, count):
    first, second = groups
    split = 2
    first.load(sources[:split], wholes[:2], [sem.at[0], sem.at[1]], count[4], count[5])
    second.load(sources[split:], wholes[2:], [sem.at[2]], count[4], count[5])


def feed(groups, count, o_ref, h_ref, gains, *rest):
    sources = rest[: 4 if groups[0].direct else 3]
    (h1_out, b_out, z_out, slope_out, h2_out, f_out, stats, w_out, w_up, w_down, sem) = rest[len(sources) :]
    step = pl.program_id(0)
    hidden = w_up.shape[1]

    @pl.when(step == 0)
    def _():
        load_feed(groups, sources, [w_out, w_up, w_down], sem, count)
        stats[...] = jnp.zeros(stats.shape, F32)

    def need(k):
        @pl.when(step == 0)
        def _():
            loaded((w_out, w_up, w_down)[k], sem.at[k])

    @pl.when(step < count[2] * (RB // FB))
    def _():
        live = live_rows(step, count, FB)
        attended = o_ref[...]
        need(0)
        branch = mm(attended, w_out[...])
        stream1 = h_ref[...] + branch
        h1_out[...] = stream1
        normed = (stream1 * inverse_rms(stream1) * gains[1:2, :]).astype(BF)
        b_out[...] = normed

        need(1)

        def chunk(j, _):
            value, slope = gelu_both(mm(normed, w_up[:, block(j, HC)]))
            z_out[:, block(j, HC)] = value.astype(BF)
            slope_out[:, block(j, HC)] = slope.astype(BF)
            return 0

        lax.fori_loop(0, hidden // HC, chunk, 0, unroll=3)
        need(2)
        branch2 = mm(z_out[...], w_down[...])
        stream2 = stream1 + branch2
        h2_out[...] = stream2
        f_out[...] = (stream2 * inverse_rms(stream2) * gains[2:3, :]).astype(BF)
        row = iota(stats.shape, 0)
        stats[...] += (
            jnp.where(row == 0, row_total(stream2, live), 0.0)
            + jnp.where(row == 1, row_total(branch, live), 0.0)
            + jnp.where(row == 2, row_total(branch2, live), 0.0)
        )


def feed_call(groups, count, attended, stream0, gains, sources):
    local, model = attended.shape
    whole = [dims for group in groups for dims in group.full_shapes()]
    hidden = whole[2][0]

    def rows(i, c):
        return (jnp.minimum(i, c[2] * (RB // FB) - 1), 0)

    def same(i, c):
        return (0, 0)

    narrow = pl.BlockSpec((FB, model), rows)
    wide = pl.BlockSpec((FB, hidden), rows)
    return pl.pallas_call(
        functools.partial(feed, groups),
        grid_spec=pltpu.PrefetchScalarGridSpec(
            num_scalar_prefetch=1,
            grid=(local // FB,),
            in_specs=[narrow, narrow, pl.BlockSpec((8, model), same)] + [anywhere()] * len(sources),
            out_specs=(narrow, narrow, wide, wide, narrow, narrow, pl.BlockSpec((8, LANES), same)),
            scratch_shapes=[pltpu.VMEM(dims, BF) for dims in whole] + [pltpu.SemaphoreType.DMA((3,))],
        ),
        out_shape=(
            shape((local, model), F32),
            shape((local, model), BF),
            shape((local, hidden), BF),
            shape((local, hidden), BF),
            shape((local, model), F32),
            shape((local, model), BF),
            shape((8, LANES), F32),
        ),
        compiler_params=params(),
        cost_estimate=cost(20e9),
        name="feed",
    )(count, attended, stream0, gains, *sources)


def by_lanes(fold, held, value):
    for k in range(value.shape[1] // LANES):
        held = fold(held, value[:, k * LANES : (k + 1) * LANES])
    return held


def head(
    count, f_ref, t_ref, rows_all, weight_any, grad_any, df_any, loss, weight, grad, df_ref, logits, back, flipped, sems
):
    chunks = weight.shape[1] // HC

    def weight_copy(j):
        return pltpu.make_async_copy(
            weight_any.at[:, block(j, HC)], weight.at[:, block(j, HC)], sems.at[0, j]
        )

    def grad_copy(j):
        return pltpu.make_async_copy(
            grad.at[:, block(j, HC)], grad_any.at[:, block(j, HC)], sems.at[1, j]
        )

    def df_copy(i):
        return pltpu.make_async_copy(
            df_ref.at[block(i, RB), :], df_any.at[block(i, RB), :], sems.at[2, i]
        )

    for j in range(chunks):
        weight_copy(j).start()
    loss[...] = jnp.zeros(loss.shape, F32)
    model = f_ref.shape[1]
    lane = iota((RB, HC), 1)

    def over_rows(i, _):
        rows = block(i, RB)
        normed = f_ref[rows, :]
        flipped[:, rows] = normed.astype(F32).T.astype(BF)
        target = t_ref[rows, 0:1].astype(jnp.int32)
        live = live_rows(i, count)

        def values(j):
            @pl.when(i == 0)
            def _():
                weight_copy(j).wait()

            return mm(normed, weight[:, block(j, HC)])

        def first(j, top):
            value = values(j)
            logits[:, block(j, HC)] = value
            return by_lanes(jnp.maximum, top, value)

        top = lax.fori_loop(0, chunks - 1, first, jnp.full((RB, LANES), 3.0 * LOW, F32), unroll=9)
        value = jnp.where(lane < BINS - (chunks - 1) * HC, values(chunks - 1), LOW)
        logits[:, (chunks - 1) * HC :] = value
        top = jnp.max(by_lanes(jnp.maximum, top, value), axis=1, keepdims=True)

        def second(j, carry):
            total, hit = carry
            value = logits[:, block(j, HC)]
            expo = jnp.exp(value - top)
            logits[:, block(j, HC)] = expo
            hit = by_lanes(jnp.add, hit, jnp.where(lane == target - j * HC, value, 0.0))
            return by_lanes(jnp.add, total, expo), hit

        zero = jnp.zeros((RB, LANES), F32)
        total, hit = lax.fori_loop(0, chunks, second, (zero, zero), unroll=5)
        total = jnp.sum(total, axis=1, keepdims=True)
        hit = jnp.sum(hit, axis=1, keepdims=True)
        part = live / rows_all[0:1, 0:1]
        share = part / total

        def third(j, held):
            hot = jnp.where(lane == target - j * HC, part, 0.0)
            found = (logits[:, block(j, HC)] * share - hot).astype(BF)
            back[rows, block(j, HC)] = found
            return held + mm_nt(found, weight[:, block(j, HC)])

        df_ref[rows, :] = lax.fori_loop(0, chunks, third, jnp.zeros((RB, model), F32), unroll=5)
        df_copy(i).start()
        loss[...] += jnp.sum(live * (top + jnp.log(total) - hit))
        return 0

    lax.fori_loop(0, count[2], over_rows, 0)

    for blocks in range(1, f_ref.shape[0] // RB + 1):

        @pl.when(count[2] == blocks)
        def _(blocks=blocks):
            def over_columns(j, _):
                grad[:, block(j, HC)] = mm(
                    flipped[:, : blocks * RB], back[: blocks * RB, block(j, HC)]
                ).astype(BF)
                grad_copy(j).start()
                return 0

            lax.fori_loop(0, chunks, over_columns, 0, unroll=5)
            for i in range(blocks):
                df_copy(i).wait()

    for j in range(chunks):
        grad_copy(j).wait()


def head_call(count, normed, targets, rows_all, weight):
    local, model = normed.shape
    bins = weight.shape[1]
    return pl.pallas_call(
        head,
        out_shape=(shape((model, bins), BF), shape((local, model), F32), shape((8, LANES), F32)),
        in_specs=[in_smem()] + [in_vmem()] * 3 + [anywhere()],
        out_specs=(anywhere(), anywhere(), in_vmem()),
        scratch_shapes=[
            pltpu.VMEM((model, bins), BF),
            pltpu.VMEM((model, bins), BF),
            pltpu.VMEM((local, model), F32),
            pltpu.VMEM((RB, bins), F32),
            pltpu.VMEM((local, bins), BF),
            pltpu.VMEM((model, local), BF),
            pltpu.SemaphoreType.DMA((3, bins // HC)),
        ],
        compiler_params=params(),
        cost_estimate=cost(35e9),
        name="head",
    )(count, normed, targets, rows_all, weight)


def feed_back(groups, count, df_ref, h2_ref, h1_ref, gains, o_any, b_any, z_any, slope_any, *rest):
    sources = rest[: 4 if groups[0].direct else 3]
    rest = rest[len(sources) :]
    targets = rest[: 4 if groups[0].direct else 3]
    (
        dh1_out,
        do_out,
        gain_out,
        w_out,
        w_up,
        w_down,
        g_out,
        g_up,
        g_down,
        o_all,
        b_all,
        z_all,
        slope_all,
        dm_all,
        da_all,
        w_sem,
        r_sem,
        g_sem,
    ) = rest[len(targets) :]
    step = pl.program_id(0)
    hidden = w_up.shape[1]
    rows = block(step, RB)
    loads = ((o_any, o_all), (b_any, b_all), (z_any, z_all), (slope_any, slope_all))

    @pl.when(step == 0)
    def _():
        load_feed(groups, sources, [w_out, w_up, w_down], w_sem, count)
        gain_out[...] = jnp.zeros(gain_out.shape, F32)

        def fetch(i, _):
            for k, (source, target) in enumerate(loads):
                pltpu.make_async_copy(
                    source.at[block(i, RB)], target.at[block(i, RB)], r_sem.at[k, i]
                ).start()
            return 0

        lax.fori_loop(0, count[2], fetch, 0)

    def need(k):
        @pl.when(step == 0)
        def _():
            loaded((w_out, w_up, w_down)[k], w_sem.at[k])

    @pl.when(step < count[2])
    def _():
        back, gain3 = rms_back(h2_ref[...], gains[2:3, :], df_ref[...])
        dm = back.astype(BF)
        dm_all[rows, :] = dm
        for k, (source, target) in enumerate(loads):
            pltpu.make_async_copy(source.at[rows], target.at[rows], r_sem.at[k, step]).wait()
        need(2)
        need(1)

        def chunk(j, held):
            spot = block(j, HC)
            upper = mm_nt(dm, w_down[spot, :])
            found = (upper * slope_all[rows, spot].astype(F32)).astype(BF)
            slope_all[rows, spot] = found
            return held + mm_nt(found, w_up[:, spot])

        db = lax.fori_loop(0, hidden // HC, chunk, jnp.zeros(back.shape, F32), unroll=3)
        need(0)
        back1, gain2 = rms_back(h1_ref[...], gains[1:2, :], db)
        stream = back + back1
        dh1_out[...] = stream
        da = stream.astype(BF)
        da_all[rows, :] = da
        do_out[...] = mm_nt(da, w_out[...]).astype(BF)
        row = iota(gain_out.shape, 0)
        gain_out[...] += jnp.where(row == 1, gain2, 0.0) + jnp.where(row == 2, gain3, 0.0)

    @pl.when(step == pl.num_programs(0) - 1)
    def _():
        sems = [g_sem.at[k] for k in range(len(targets))]
        split = len(targets) * 2 // 4 if groups[0].direct else 2

        def over_row_blocks(body):
            for blocks in range(1, z_all.shape[0] // RB + 1):

                @pl.when(count[2] == blocks)
                def _(blocks=blocks):
                    body(slice(0, blocks * RB))

        @over_row_blocks
        def _(live):
            def columns(j, _):
                spot = block(j, HC)
                g_down[spot, :] = mm_tn(z_all[live, spot], dm_all[live, :]).astype(BF)
                return 0

            lax.fori_loop(0, hidden // HC, columns, 0, unroll=2)

        groups[1].store([g_down], targets[split:], sems[split:], count[4], count[5])

        @over_row_blocks
        def _(live):
            def columns(j, _):
                spot = block(j, HC)
                g_up[:, spot] = mm_tn(b_all[live, :], slope_all[live, spot]).astype(BF)
                return 0

            lax.fori_loop(0, hidden // HC, columns, 0, unroll=2)
            g_out[...] = mm_tn(o_all[live, :], da_all[live, :]).astype(BF)

        groups[0].store([g_out, g_up], targets[:split], sems[:split], count[4], count[5])
        groups[0].stored(targets, sems)


def feed_back_call(groups, count, df, stream2, stream1, gains, attended, normed, active, slope, sources):
    local, model = df.shape
    whole = [dims for group in groups for dims in group.full_shapes()]
    hidden = whole[2][0]
    outs = [found for group in groups for found in group.out_shapes()]

    def rows(i, c):
        return (jnp.minimum(i, c[2] - 1), 0)

    def same(i, c):
        return (0, 0)

    narrow = pl.BlockSpec((RB, model), rows)
    return pl.pallas_call(
        functools.partial(feed_back, groups),
        grid_spec=pltpu.PrefetchScalarGridSpec(
            num_scalar_prefetch=1,
            grid=(local // RB,),
            in_specs=[narrow, narrow, narrow, pl.BlockSpec((8, model), same)]
            + [anywhere()] * (4 + len(sources)),
            out_specs=(anywhere(),) * len(outs) + (narrow, narrow, pl.BlockSpec((8, model), same)),
            scratch_shapes=[pltpu.VMEM(dims, BF) for dims in whole] * 2
            + [
                pltpu.VMEM((local, model), BF),
                pltpu.VMEM((local, model), BF),
                pltpu.VMEM((local, hidden), BF),
                pltpu.VMEM((local, hidden), BF),
                pltpu.VMEM((local, model), BF),
                pltpu.VMEM((local, model), BF),
                pltpu.SemaphoreType.DMA((3,)),
                pltpu.SemaphoreType.DMA((4, local // RB)),
                pltpu.SemaphoreType.DMA((4,)),
            ],
        ),
        out_shape=tuple(outs)
        + (shape((local, model), F32), shape((local, model), BF), shape((8, model), F32)),
        compiler_params=params(),
        cost_estimate=cost(35e9),
        name="feed_back",
    )(count, df, stream2, stream1, gains, attended, normed, active, slope, *sources)


def project_back(
    groups, blocks, count, dq, aq, xq, dh1, h0, dk, dv, ac, xc, yc, gains, gains23, weight, *rest
):
    targets = rest[: 4 if groups[0].direct else 2]
    total, emb, small, out0, out1, g_sem = rest[len(targets) :]
    step = pl.program_id(0)
    steps = pl.num_programs(0)
    model = dq.shape[1]
    embed = slice(3 * model, 3 * model + LANES)

    @pl.when(step == 0)
    def _():
        total[...] = jnp.zeros(total.shape, F32)
        emb[...] = jnp.zeros(emb.shape, F32)
        small[...] = gains23[...]

    row = iota(small.shape, 0)

    @pl.when(step < count[2])
    def _():
        grad = dq[...]
        upper = mm_nt(grad, weight[:, :model])
        total[:, :model] += mm_tn(aq[...], grad)
        back, gain1 = rms_back(h0[...], gains[0:1, :], upper)
        stream = dh1[...] + back
        emb[...] += mm_tn(stream.astype(BF), xq[...])
        small[...] += jnp.where(row == 0, gain1, 0.0)

    @pl.when((step >= blocks) & (step < blocks + count[3]))
    def _():
        a = ac[...]
        label = yc[:, 0:1]
        stream = mm_nt(xc[...], weight[:, embed]) + label * gains[3:4, :]
        upper = jnp.zeros(stream.shape, F32)
        for part, ref in enumerate((dk, dv)):
            grad = ref[...]
            columns = slice((part + 1) * model, (part + 2) * model)
            upper += mm_nt(grad, weight[:, columns])
            total[:, columns] += mm_tn(a, grad)
        back, gain1 = rms_back(stream, gains[0:1, :], upper)
        emb[...] += mm_tn(back.astype(BF), xc[...])
        small[...] += jnp.where(row == 0, gain1, 0.0) + jnp.where(
            row == 3, jnp.sum(label * back, axis=0, keepdims=True), 0.0
        )

    @pl.when(step == steps - 1)
    def _():
        middle = out0.shape[1]
        out0[...] = total[:, :middle].astype(BF)
        out1[:, : 3 * model - middle] = total[:, middle:].astype(BF)
        out1[:, 3 * model - middle : 3 * model - middle + LANES] = emb[...].astype(BF)
        padded = jnp.concatenate([small[...], jnp.zeros((LANES - 8, small.shape[1]), F32)])
        out1[:, 3 * model - middle + LANES :] = padded.T.astype(BF)
        sems = [g_sem.at[k] for k in range(len(targets))]
        size = len(targets) // 2
        for k, (group, out) in enumerate(zip(groups, (out0, out1))):
            some = slice(k * size, (k + 1) * size)
            group.store([out], targets[some], sems[some], count[4], count[5])
        group.stored(targets, sems)


def project_back_call(groups, count, dq, aq, xq, dh1, h0, dk, dv, ac, xc, yc, gains, gains23, weight):
    local, model = dq.shape
    total = dk.shape[0]
    blocks_q, blocks_c = local // RB, total // CB
    outs = [found for group in groups for found in group.out_shapes()]

    def q_map(i, c):
        return (jnp.minimum(i, c[2] - 1), 0)

    def c_map(i, c):
        return (jnp.clip(i - blocks_q, 0, c[3] - 1), 0)

    def same(i, c):
        return (0, 0)

    query = pl.BlockSpec((RB, model), q_map)
    context = pl.BlockSpec((CB, model), c_map)
    thin = pl.BlockSpec((CB, LANES), c_map)
    fixed = pl.BlockSpec((8, model), same)
    return pl.pallas_call(
        functools.partial(project_back, groups, blocks_q),
        grid_spec=pltpu.PrefetchScalarGridSpec(
            num_scalar_prefetch=1,
            grid=(blocks_q + blocks_c,),
            in_specs=[
                query,
                query,
                pl.BlockSpec((RB, LANES), q_map),
                query,
                query,
                context,
                context,
                context,
                thin,
                thin,
                fixed,
                fixed,
                pl.BlockSpec(weight.shape, same),
            ],
            out_specs=(anywhere(),) * len(outs),
            scratch_shapes=[
                pltpu.VMEM((model, 3 * model), F32),
                pltpu.VMEM((model, LANES), F32),
                pltpu.VMEM((8, model), F32),
                pltpu.VMEM(groups[0].full_shapes()[0], BF),
                pltpu.VMEM(groups[1].full_shapes()[0], BF),
                pltpu.SemaphoreType.DMA((4,)),
            ],
        ),
        out_shape=tuple(outs),
        compiler_params=params(),
        cost_estimate=cost(20e9),
        name="project_back",
    )(count, dq, aq, xq, dh1, h0, dk, dv, ac, xc, yc, gains, gains23, weight)


def halves(tab, mine):
    other = swap(mine, "tab", 0)
    return jnp.where(tab == 0, mine, other), jnp.where(tab == 0, other, mine)


def on_device(
    count_fsdp,
    features,
    feature_counts,
    row_flags,
    target_bins,
    emb_weight,
    qkv_weight,
    out_weight,
    up_weight,
    down_weight,
    head_weight,
    vectors,
    mom_emb,
    mom_qkv,
    mom_out,
    mom_up,
    mom_down,
    mom_head,
    mom_vectors,
    ema_emb,
    ema_qkv,
    ema_out,
    ema_up,
    ema_down,
    ema_head,
    ema_vectors,
):
    masters = (emb_weight, qkv_weight, out_weight, up_weight, down_weight, head_weight, vectors)
    moms = (mom_emb, mom_qkv, mom_out, mom_up, mom_down, mom_head, mom_vectors)
    emas = (ema_emb, ema_qkv, ema_out, ema_up, ema_down, ema_head, ema_vectors)
    me = lax.axis_index("fsdp").astype(jnp.int32)
    tab = lax.axis_index("tab").astype(jnp.int32)
    local, nfeat = features.shape[1:]
    total = 2 * local
    rows = qkv_weight.shape[0]
    model = rows * count_fsdp
    half = model // 2
    hidden_half = up_weight.shape[1] // 2
    size = model // HEADS
    flags = row_flags[0]
    targets = target_bins[0]

    high_bits = [1 << k for k in reversed(range(1, count_fsdp.bit_length() - 1))]
    x_last = high_bits + ["tab"]
    y_last = high_bits[:-1] + ["tab", high_bits[-1]]
    wide = 3 * model
    quarter = (wide + 2 * LANES) // 4
    groups_a = [Group(order, rows, [(quarter, 1)], count_fsdp) for order in (x_last, y_last)]
    groups_b = [
        Group(x_last, rows, [(half, 1), (hidden_half, 1)], count_fsdp),
        Group(y_last, down_weight.shape[0], [(half, 1)], count_fsdp),
    ]

    def side_of(weight, width):
        return jnp.where(tab == 0, weight[:, :width], weight[:, width : 2 * width])

    queries_here = jnp.sum(flags)
    marks = jnp.stack([queries_here // 32, queries_here % 32]).astype(F32)
    first_row = (jnp.arange(rows) == 0).astype(F32)[:, None]

    def tail(block_t):
        used = block_t.shape[0]
        return jnp.concatenate(
            [block_t.T, first_row * marks[None, :], jnp.zeros((rows, LANES - 2 - used), F32)], axis=1
        )

    piece_a = jnp.concatenate([qkv_weight, tail(emb_weight), tail(vectors)], axis=1).astype(BF)
    pieces_b = [
        [side_of(out_weight, half), side_of(up_weight, hidden_half)],
        [side_of(down_weight, half)],
    ]
    held_b = [jnp.concatenate(found, axis=1).astype(BF)[None] for found in pieces_b]
    bins = -(-head_weight.shape[1] // HC) * HC
    spare = bins - head_weight.shape[1]
    piece_h = jnp.pad(head_weight.astype(BF), ((0, 0), (0, spare)))

    whole_a = lax.all_gather(piece_a, "fsdp", axis=0, tiled=True)

    pack = jnp.concatenate(
        [
            features[0],
            jnp.stack([flags, targets // 64, targets % 64], axis=1).astype(BF),
            jnp.zeros((local, LANES - 3 - nfeat), BF),
        ],
        axis=1,
    )
    lower, upper = halves(tab, pack)
    table = jnp.concatenate([lower, upper])
    flag_rows = table[:, nfeat].astype(F32).reshape(total // LANES, LANES)
    asked = jnp.sum(flag_rows).astype(jnp.int32)
    here = (asked - tab + 1) // 2
    known = total - asked
    count = jnp.stack(
        [
            here,
            known,
            jnp.maximum((here + RB - 1) // RB, 1),
            (known + CB - 1) // CB,
            me,
            tab,
            feature_counts[0],
            jnp.maximum((here + QB - 1) // QB, 1),
        ]
    )
    x_query, t_query, x_context, y_context = sort_rows_call(nfeat, count, table, flag_rows)

    last = len(high_bits)
    for at in range(last):
        held_b = gather_step(groups_b, held_b, at, *([x_query] if at == last - 2 else []))
        if at == last - 2:
            head_full = lax.all_gather(after(piece_h, held_b), "fsdp", axis=0, tiled=True)
    x_query = after(x_query, held_b)
    queries, keys, values, a_query, a_context, stream0, gains = project_call(
        nfeat, count, x_query, x_context, y_context, whole_a
    )
    row_count = gains[4:5, :LANES]
    row_count = row_count + swap(row_count, "tab", 0)
    attended, logs = attend_call(size, count, queries, keys, values)
    held_b = gather_step(groups_b, held_b, last, attended)
    far_b = [swap(held, 1, count_fsdp) for held in held_b]
    sources_b = [
        found
        for group, near, far in zip(groups_b, held_b, far_b)
        for found in group.sources(near, far, me, tab)
    ]
    stream1, normed2, active, slope, stream2, normed3, stats = feed_call(
        groups_b, count, attended, stream0, gains, sources_b
    )
    grad_head, df, loss = head_call(count, normed3, t_query, row_count, head_full)
    shard_h = lax.optimization_barrier(
        lax.psum_scatter(grad_head, "fsdp", scatter_dimension=0, tiled=True)
    )
    *outs_b, dh1, grad_o, gains23 = feed_back_call(
        groups_b, count, df, stream2, stream1, gains, attended, normed2, active, slope, sources_b
    )

    def core_step(groups, outs):
        size_of = len(outs) // 2 if groups[0].direct else len(groups[0].parts)
        pairs = [
            group.targets(found, me, tab) for group, found in zip(groups, (outs[:size_of], outs[size_of:]))
        ]
        return [near + swap(far, 1, count_fsdp) for near, far in pairs]

    grads_b = core_step(groups_b, outs_b)
    grad_o = after(grad_o, grads_b)
    dq, dk, dv = attend_back_call(size, count, queries, keys, values, grad_o, attended, logs)
    grads_b = scatter_step(groups_b, grads_b, last, dq)
    dq = after(dq, grads_b)
    outs_a = project_back_call(
        groups_a,
        count,
        dq,
        a_query,
        x_query,
        dh1,
        stream0,
        dk,
        dv,
        a_context,
        x_context,
        y_context,
        gains,
        gains23,
        whole_a,
    )
    grads_b = scatter_step(groups_b, grads_b, last - 1, outs_a)
    grads_a = core_step(groups_a, outs_a)
    for at in reversed(range(last + 1)):
        grads_a = scatter_step(groups_a, grads_a, at)
        if at < last - 1:
            grads_b = scatter_step(groups_b, grads_b, at)
    shards_a = [found[0] for found in grads_a]
    shards_b = [found[0] for found in grads_b]

    shard_h = shard_h[:, : head_weight.shape[1]]
    grad_h = shard_h.astype(F32) + swap(shard_h, "tab", 0).astype(F32)
    split_a = [halves(tab, found) for found in shards_a]
    split_b = [halves(tab, found) for found in shards_b]
    whole_grad = jnp.concatenate([side for found in split_a for side in found], axis=1)
    grad_qkv = whole_grad[:, :wide]
    grad_emb = whole_grad[:, wide : wide + nfeat].T
    grad_vectors = whole_grad[:, wide + LANES : wide + LANES + vectors.shape[0]].T
    grad_out = jnp.concatenate([side[:, :half] for side in split_b[0]], axis=1)
    grad_up = jnp.concatenate([side[:, half:] for side in split_b[0]], axis=1)
    grad_down = jnp.concatenate(split_b[1], axis=1)
    summed = (grad_emb, grad_qkv, grad_out, grad_up, grad_down, grad_h, grad_vectors)
    place = jnp.arange(quarter)[None, :] + (2 + tab) * quarter - wide
    real = (place < nfeat) | ((place >= LANES) & (place < LANES + vectors.shape[0]))
    keep_a = jnp.where(real, shards_a[1], 0.0)
    squares = 0.5 * jnp.sum(grad_h * grad_h)
    for found in (shards_a[0], keep_a, *shards_b):
        squares = squares + jnp.sum(found * found)
    sums = jnp.concatenate([loss[0:1, 0:1], stats[0:3, 0:1], squares.reshape(1, 1)]).reshape(1, 5)
    sums = jnp.broadcast_to(jnp.pad(sums, ((0, 0), (0, LANES - 5))), (8, LANES))
    for step in [1] + high_bits + ["tab"]:
        sums = sums + swap(sums, step, count_fsdp)
    loss_sum = sums[0, 0]
    rms_sums = sums[0, 1:4]
    clip_norm = jnp.sqrt(sums[0, 4])
    row_count = row_count[0, 0]
    factor = jnp.minimum(1.0, CLIP / clip_norm)
    new_moms, new_weights, new_emas = ([], [], [])
    for weight, grad, moment, average in zip(masters, summed, moms, emas):
        clipped = grad * factor
        moment_new = MOMENTUM * moment + clipped
        weight_new = weight - RATE * (clipped + MOMENTUM * moment_new)
        new_moms.append(moment_new)
        new_weights.append(weight_new)
        new_emas.append(AVERAGE * average + (1.0 - AVERAGE) * weight_new)
    return (loss_sum, row_count, rms_sums, clip_norm, *new_moms, *new_weights, *new_emas)


def solution(mesh):
    by_row, by_column = P("fsdp", None), P(None, "fsdp")
    weights = (by_column, by_row, by_row, by_row, by_row, by_row, by_column)
    return jax.shard_map(
        functools.partial(on_device, mesh.shape["fsdp"]),
        mesh=mesh,
        in_specs=(P("fsdp", "tab", None), P("fsdp"), P("fsdp", "tab"), P("fsdp", "tab")) + weights * 3,
        out_specs=(P(), P(), P(), P()) + weights * 3,
        check_vma=False,
    )
```

time: 675 us -> 468 us (0.69)
  waiting for transfers between devices: 290 us -> 131 us
  starting transfers between devices: 105 us -> 73.9 us
  Pallas kernels: 186 us -> 160 us
  other arithmetic: 36.2 us -> 45.3 us
    ppermute x20 -> x28, waiting for transfers between devices: 200 us -> 86.8 us  [swap(): return lax.ppermute(value, 'fsdp', [(i, i ^ step) for i in range(count)])]
    ppermute x9 -> x14, waiting for transfers between devices: 89.8 us -> 43.8 us  [swap(): return lax.ppermute(value, 'tab', [(0, 1), (1, 0)])]
    ppermute x20 -> x28, starting transfers between devices: 90.2 us -> 54.4 us  [swap(): return lax.ppermute(value, 'fsdp', [(i, i ^ step) for i in range(count)])]
    pallas_call x1, Pallas kernels: 26.9 us -> 14.6 us  [attend_call(): pl.pallas_call(functools.partial(attend, size), grid_spec=pltpu.PrefetchS...]
    ppermute x9 -> x14, starting transfers between devices: 15.1 us -> 19.4 us  [swap(): return lax.ppermute(value, 'tab', [(0, 1), (1, 0)])]
    unnamed x98 -> x80, local copies, waits for them, and re-layouts: 14 us -> 11.5 us
  transfers between devices with their start and end apart: 31 -> 45, of which waited for: 22 -> 23; matrix products, arithmetic and copies ran while one was open for 7% -> 10% of each run, Pallas kernels for 18% -> 23%
where the time goes in v2:
time: 468 us; the launch traced here: 463 us
  Pallas kernels  160 us (34%)
  waiting for transfers between devices  131 us (28%)
  starting transfers between devices  73.9 us (16%)
  other arithmetic  45.3 us (10%)
  local copies, waits for them, and re-layouts  28.9 us (6%)
  between operations  24.1 us (5%)
    ppermute x28, waiting for transfers between devices, swap(): return lax.ppermute(value, 'fsdp', [(i, i ^ step) for i in range(count)])  86.8 us
    ppermute x28, starting transfers between devices, swap(): return lax.ppermute(value, 'fsdp', [(i, i ^ step) for i in range(count)])  54.4 us
    ppermute x14, waiting for transfers between devices, swap(): return lax.ppermute(value, 'tab', [(0, 1), (1, 0)])  43.8 us
    pallas_call x1, Pallas kernels, feed_back_call(): pl.pallas_call(functools.partial(feed_back, groups), grid_spec=pltpu.Pref...  28.7 us
    pallas_call x1, Pallas kernels, head_call(): pl.pallas_call(head, out_shape=(shape((model, bins), BF), shape((local, m...  27 us
    pallas_call x1, Pallas kernels, project_back_call(): pl.pallas_call(functools.partial(project_back, groups, blocks_q), grid_sp...  25.1 us
    pallas_call x1, Pallas kernels, attend_back_call(): pl.pallas_call(functools.partial(attend_back, size), grid_spec=pltpu.Pref...  21.4 us
    ppermute x14, starting transfers between devices, swap(): return lax.ppermute(value, 'tab', [(0, 1), (1, 0)])  19.4 us
  transfers between devices with their start and end apart: 45, of which 23 were waited for; matrix products, arithmetic and copies ran while one was open for 10% of the time, Pallas kernels for 23%

profile of v2, /device:TPU:0, one launch (start us, length us, event | category | flops | bytes accessed | tf_op | source)
XLA Modules:
  0.0 463.1 jit_solution(761627295962989816)
XLA Ops:
  7.3 1.4 fusion.21
  17.7 4.0 collective-permute-start.1
  24.3 1.9 collective-permute-start
  27.7 17.0 %collective-permute-done.2 = bf16[1,192,384]{2,1,0:T(8,128)(2,1)S(1)} collective-permute-done((bf16[1,192,384]{2,1,0:T(8,128)(2,1)S(1)}, bf16[1,192,384]{2,1,0:T(8,128)(2,1)S(1)}, u32[]{:S(2)}, u32[]{:S(2)}) %collective-permute-start.2) | collective-permute-done | bytes 147488 | tf_op jit(solution)/shard_map/ppermute | solution.py:207
  45.6 1.4 collective-permute-start.4
  50.4 8.3 %sort_rows.1 = (bf16[1024,128]{1,0:T(8,128)(2,1)}, f32[1024,128]{1,0:T(8,128)}, bf16[2048,128]{1,0:T(8,128)(2,1)}, f32[2048,128]{1,0:T(8,128)}) custom-call(s32[8]{0:T(128)} %stack.44.count, bf16[2048,128]{1,0:T(8,128)(2,1)} %pad_maximum_fusion.3.table, f32[16,128]{1,0:T(8,128)} %bitcast.88), custom_call_target="tpu_custom_call" | custom-call | flops 7000000000 | bytes 1048576 | tf_op jit(solution)/shard_map/sort_rows/pallas_call | solution.py:274
  58.7 17.5 %collective-permute-done.4 = bf16[2,192,384]{2,1,0:T(8,128)(2,1)S(1)} collective-permute-done((bf16[2,192,384]{2,1,0:T(8,128)(2,1)S(1)}, bf16[2,192,384]{2,1,0:T(8,128)(2,1)S(1)}, u32[]{:S(2)}, u32[]{:S(2)}) %collective-permute-start.4) | collective-permute-done | bytes 294944 | tf_op jit(solution)/shard_map/ppermute | solution.py:207
  76.4 1.3 collective-permute-start.5
  77.7 1.5 collective-permute-start.6
  80.7 8.1 %collective-permute-done.6 = bf16[4,192,384]{2,1,0:T(8,128)(2,1)S(1)} collective-permute-done((bf16[4,192,384]{2,1,0:T(8,128)(2,1)S(1)}, bf16[4,192,384]{2,1,0:T(8,128)(2,1)S(1)}, u32[]{:S(2)}, u32[]{:S(2)}) %collective-permute-start.6) | collective-permute-done | bytes 589856 | tf_op jit(solution)/shard_map/ppermute | solution.py:206
  88.7 2.6 collective-permute-done.5
  94.5 1.5 collective-permute-start.8
  97.0 15.9 %project.1 = (bf16[1024,768]{1,0:T(8,128)(2,1)}, bf16[2048,768]{1,0:T(8,128)(2,1)}, bf16[2048,768]{1,0:T(8,128)(2,1)}, bf16[1024,768]{1,0:T(8,128)(2,1)}, bf16[2...) custom-call(s32[8]{0:T(128)} %stack.44.count, bf16[1024,128]{1,0:T(8,128)(2,1)} %get-tuple-element.97.x_query.xq, ...), custom_call_target="tpu_custom_call" | custom-call | flops 12000000000 | bytes 1048576 | tf_op jit(solution)/shard_map/project/pallas_call | solution.py:335
  112.9 14.6 %attend.1 = (bf16[1024,768]{1,0:T(8,128)(2,1)}, f32[6,8,1024]{2,1,0:T(8,128)}) custom-call(s32[8]{0:T(128)} %stack.44.count, bf16[1024,768]{1,0:T(8,128)(2,1)} %get-tuple-element.100.q_ref, bf16[2048,768]{1,0:T(8,128)(2,1)} %get-tuple-element.101.k_ref, bf16[2048,768]{1,0:T(8,128)(2,1)} %get-tuple-element.102.v_ref), custom_call_target="tpu_custom_call" | custom-call | flops 35000000512 | bytes 1048576 | tf_op jit(solution)/shard_map/attend/pallas_call | solution.py:447
  127.5 2.1 collective-permute-done.8
  129.6 2.6 constant_dynamic-update-slice_fusion.rest_0_
  132.7 1.4 copy-done.26
  135.3 1.5 collective-permute-start.11
  136.8 2.0 collective-permute-done.11
  141.2 1.4 copy-done.33
  142.6 19.1 %feed.1 = (f32[1024,768]{1,0:T(8,128)}, bf16[1024,768]{1,0:T(8,128)(2,1)}, bf16[1024,3072]{1,0:T(8,128)(2,1)}, bf16[1024,3072]{1,0:T(8,128)(2,1)}, f32[1024,768]...) custom-call(s32[8]{0:T(128)} %stack.44.count, bf16[1024,768]{1,0:T(8,128)(2,1)} %get-tuple-element.103.o_ref.o_any, ...), custom_call_target="tpu_custom_call" | custom-call | flops 20000000000 | bytes 1048576 | tf_op jit(solution)/shard_map/feed/pallas_call | solution.py:633
  161.7 27.0 %head.1 = (bf16[768,5120]{1,0:T(8,128)(2,1)}, f32[1024,768]{1,0:T(8,128)}, f32[8,128]{1,0:T(8,128)}) custom-call(s32[8]{0:T(128)} %stack.44.count, bf16[1024,768]{1,0:T(8,128)(2,1)} %get-tuple-element.108.f_ref, f32[1024,128]{1,0:T(8,128)} %get-tuple-element.109.t_ref, f32[1,128]{1,0:T(1,128)} %slice_add_fusion.rows_all, ...), custom_call_target="tpu_custom_call" | custom-call | flops 35000000512 | bytes 1048576 | tf_op jit(solution)/shard_map/head/pallas_call | solution.py:763
  188.7 28.7 %feed_back.1 = (bf16[16,48,1920]{2,1,0:T(8,128)(2,1)}, bf16[16,48,1920]{2,1,0:T(8,128)(2,1)}, bf16[16,192,384]{2,1,0:T(8,128)(2,1)}, bf16[16,192,384]{2,1,0:T(8,...) custom-call(s32[8]{0:T(128)} %stack.44.count, ...), custom_call_target="tpu_custom_call" | custom-call | flops 35000000512 | bytes 1048576 | tf_op jit(solution)/shard_map/feed_back/pallas_call | solution.py:909
  218.0 8.6 %collective-permute-done.14 = bf16[16,192,384]{2,1,0:T(8,128)(2,1)} collective-permute-done((bf16[16,192,384]{2,1,0:T(8,128)(2,1)}, bf16[16,192,384]{2,1,0:T(8,128)(2,1)}, u32[]{:S(2)}, u32[]{:S(2)}) %collective-permute-start.14) | collective-permute-done | bytes 2359328 | tf_op jit(solution)/shard_map/ppermute | solution.py:207
  226.6 3.2 add.240
  231.1 1.3 collective-permute-start.16
  232.3 1.6 copy-done.7
  233.9 2.7 add.239
  239.0 21.4 %attend_back.1 = (bf16[1024,768]{1,0:T(8,128)(2,1)}, bf16[2048,768]{1,0:T(8,128)(2,1)}, bf16[2048,768]{1,0:T(8,128)(2,1)}) custom-call(s32[8]{0:T(128)} %stack.44.count, bf16[1024,768]{1,0:T(8,128)(2,1)} %get-tuple-element.100.q_ref, bf16[2048,768]{1,0:T(8,128)(2,1)} %get-tuple-element.101.k_ref, bf16[2048,768]{1,0:T(8,128)(2,1)} %get-tuple-element.102.v_ref, ...), custom_call_target="tpu_custom_call" | custom-call | flops 35000000512 | bytes 1048576 | tf_op jit(solution)/shard_map/attend_back/pallas_call | solution.py:526
  260.5 11.7 %collective-permute-done.15 = bf16[8,48,1920]{2,1,0:T(8,128)(2,1)} collective-permute-done((bf16[8,48,1920]{2,1,0:T(8,128)(2,1)}, bf16[8,48,1920]{2,1,0:T(8,128)(2,1)}, u32[]{:S(2)}, u32[]{:S(2)}) %collective-permute-start.15) | collective-permute-done | bytes 1474592 | tf_op jit(solution)/shard_map/ppermute | solution.py:206
  272.2 1.9 add_convert_fusion
  274.3 1.9 add_convert_fusion.1
  277.8 1.6 collective-permute-start.28
  279.4 25.1 %project_back.1 = (bf16[16,48,640]{2,1,0:T(8,128)(2,1)}, bf16[16,48,640]{2,1,0:T(8,128)(2,1)}, bf16[16,48,640]{2,1,0:T(8,128)(2,1)}, bf16[16,48,640]{2,1,0:T(8,128)(2,1)}) custom-call(s32[8]{0:T(128)} %stack.44.count, bf16[1024,768]{1,0:T(8,128)(2,1)} %get-tuple-element.130.dq, bf16[1024,768]{1,0:T(8,128)(2,1)} %get-tuple-element.131.aq, ...), custom_call_target="tpu_custom_call" | custom-call | flops 20000000000 | bytes 1048576 | tf_op jit(solution)/shard_map/project_back/pallas_call | solution.py:1018
  305.4 2.7 collective-permute-start.29
  310.6 1.5 collective-permute-start.18
  314.4 15.8 %collective-permute-done.30 = bf16[2,192,384]{2,1,0:T(8,128)(2,1)S(1)} collective-permute-done((bf16[2,192,384]{2,1,0:T(8,128)(2,1)S(1)}, bf16[2,192,384]{2,1,0:T(8,128)(2,1)S(1)}, u32[]{:S(2)}, u32[]{:S(2)}) %collective-permute-start.30) | collective-permute-done | bytes 294944 | tf_op jit(solution)/shard_map/ppermute | solution.py:207
  331.0 22.1 %collective-permute-start.31 = (bf16[1,48,1920]{2,1,0:T(8,128)(2,1)}, bf16[1,48,1920]{2,1,0:T(8,128)(2,1)S(1)}, u32[]{:S(2)}, u32[]{:S(2)}) collective-permute-start(bf16[1,48,1920]{2,1,0:T(8,128)(2,1)} %slice.247), channel_id=1, source_target_pairs={{0,8},{1,9},{2,10},{3,11},{4,12},{5,13},{6,14},{7,15},{8,0},{9,1},... | collective-permute-start | bytes 552968 | tf_op jit(solution)/shard_map/ppermute | solution.py:207
  355.8 11.3 %collective-permute-done.32 = bf16[1,192,384]{2,1,0:T(8,128)(2,1)S(1)} collective-permute-done((bf16[1,192,384]{2,1,0:T(8,128)(2,1)}, bf16[1,192,384]{2,1,0:T(8,128)(2,1)S(1)}, u32[]{:S(2)}, u32[]{:S(2)}) %collective-permute-start.32) | collective-permute-done | bytes 147488 | tf_op jit(solution)/shard_map/ppermute | solution.py:207
  368.9 1.9 collective-permute-start.22
  371.2 1.9 collective-permute-start.41
  373.5 4.4 collective-permute-done.22
  378.2 2.0 collective-permute-start.24
  380.2 8.8 %collective-permute-done.41 = f32[192,384]{1,0:T(8,128)S(1)} collective-permute-done((f32[192,384]{1,0:T(8,128)S(1)}, f32[192,384]{1,0:T(8,128)S(1)}, u32[]{:S(2)}, u32[]{:S(2)}) %collective-permute-start.41) | collective-permute-done | bytes 294944 | tf_op jit(solution)/shard_map/ppermute | solution.py:206
  390.0 3.0 collective-permute-start.26
  393.7 2.0 collective-permute-done.25
  396.4 1.8 collective-permute-start.39
  398.5 1.8 collective-permute-start.38
  400.3 2.4 collective-permute-done.39
  402.7 1.3 broadcast_select_fusion.8
  404.0 6.3 %collective-permute-done.38 = f32[48,640]{1,0:T(8,128)S(1)} collective-permute-done((f32[48,640]{1,0:T(8,128)S(1)}, f32[48,640]{1,0:T(8,128)S(1)}, u32[]{:S(2)}, u32[]{:S(2)}) %collective-permute-start.38) | collective-permute-done | bytes 122912 | tf_op jit(solution)/shard_map/ppermute | solution.py:206
  410.3 1.3 broadcast_select_fusion.6
  411.6 1.9 multiply_reduce_fusion
  418.7 2.1 collective-permute-start.34
  420.8 2.4 collective-permute-done.34
  423.2 6.6 %collective-permute-start.35 = (f32[8,128]{1,0:T(8,128)S(1)}, f32[8,128]{1,0:T(8,128)S(1)}, u32[]{:S(2)}, u32[]{:S(2)}) collective-permute-start(f32[8,128]{1,0:T(8,128)S(1)} %fusion.22), channel_id=1, source_target_pairs={{0,4},{1,5},{2,6},{3,7},{4,0},{5,1},{6,2},{7,3},{8,12},{9,13},{10,... | collective-permute-start | bytes 12296 | tf_op jit(solution)/shard_map/ppermute | solution.py:207
  429.8 1.6 collective-permute-done.35
  432.5 2.5 collective-permute-done.36
  435.0 1.4 collective-permute-start.37
  443.8 1.4 add_multiply_fusion.6
  445.3 2.0 add_multiply_fusion.4
  447.3 2.4 add_multiply_fusion.2
  449.7 1.4 add_multiply_fusion.1
  453.0 1.9 add_multiply_fusion
  (221 shorter events, 55.3 us)
Async XLA Ops:
  7.2 14.5 %copy-start.11 = (f32[192,768]{1,0:T(8,128)S(1)}, f32[192,768]{1,0:T(8,128)}, u32[]{:S(2)}) copy-start(f32[192,768]{1,0:T(8,128)} %param.33) | copy-start | bytes 1769476
  7.2 15.2 %copy-start.24 = (bf16[1,1024,100]{1,2,0:T(8,128)(2,1)S(1)}, bf16[1,1024,100]{1,2,0:T(8,128)(2,1)}, u32[]{:S(2)}) copy-start(bf16[1,1024,100]{1,2,0:T(8,128)(2,1)} %param.25) | copy-start | bytes 614404
  7.2 15.6 %copy-start.28 = (s32[1,1024]{1,0:T(1,128)S(1)}, s32[1,1024]{1,0:T(1,128)}, u32[]{:S(2)}) copy-start(s32[1,1024]{1,0:T(1,128)} %param.28) | copy-start | bytes 12292
  7.2 89.7 %all-gather.3.cloned.1.call-start = ((), (), s32[]{:S(2)}) async-start(), calls=%async_computation.1 | async-start | bytes 4177920 | tf_op jit(solution)/shard_map/all_gather | solution.py:1137
  14.9 146.9 %all-gather.5.cloned.1.call-start = ((), (), s32[]{:S(2)}) async-start(), calls=%async_computation.2 | async-start | bytes 8355840 | tf_op jit(solution)/shard_map/all_gather | solution.py:1171
  17.7 9.1 %copy-start.4 = (f32[48,5000]{1,0:T(8,128)S(1)}, f32[48,5000]{1,0:T(8,128)}, u32[]{:S(2)}) copy-start(f32[48,5000]{1,0:T(8,128)} %param.34) | copy-start | bytes 2880004
  17.7 27.1 %collective-permute-start.1 = (bf16[1,48,1920]{2,1,0:T(8,128)(2,1)}, bf16[1,48,1920]{2,1,0:T(8,128)(2,1)S(1)}, u32[]{:S(2)}, u32[]{:S(2)}) collective-permute-start(bf16[1,48,1920]{2,1,0:T(8,128)(2,1)} %get-tuple-element.297), channel_id=1, source_target_pairs={{0,8},{1,9},{2,10},{3,11},{4,12},{5,13},{6,14},{7,15},{8,0},{9,1},... | collective-permute-start | bytes 552968 | tf_op jit(solution)/shard_map/ppermute | solution.py:207
  22.4 22.3 %collective-permute-start.2 = (bf16[1,192,384]{2,1,0:T(8,128)(2,1)S(1)}, bf16[1,192,384]{2,1,0:T(8,128)(2,1)S(1)}, u32[]{:S(2)}, u32[]{:S(2)}) collective-permute-start(bf16[1,192,384]{2,1,0:T(8,128)(2,1)S(1)} %get-tuple-element.279), channel_id=1, source_target_pairs={{0,8},{1,9},{2,10},{3,11},{4,12},{5,13},{6,14},{7,15},{8,0},{9,1},... | collective-permute-start | bytes 442376 | tf_op jit(solution)/shard_map/ppermute | solution.py:207
  24.3 22.7 %collective-permute-start = (bf16[1024,128]{1,0:T(8,128)(2,1)S(1)}, bf16[1024,128]{1,0:T(8,128)(2,1)S(1)}, u32[]{:S(2)}, u32[]{:S(2)}) collective-permute-start(bf16[1024,128]{1,0:T(8,128)(2,1)S(1)} %concatenate.75), channel_id=1, source_target_pairs={{0,16},{16,0},{1,17},{17,1},{2,18},{18,2},{3,19},{19,3},{4,20},{20... | collective-permute-start | bytes 786440 | tf_op jit(solution)/shard_map/ppermute | solution.py:206
  44.8 31.4 %collective-permute-start.3 = (bf16[2,48,1920]{2,1,0:T(8,128)(2,1)S(1)}, bf16[2,48,1920]{2,1,0:T(8,128)(2,1)S(1)}, u32[]{:S(2)}, u32[]{:S(2)}) collective-permute-start(bf16[2,48,1920]{2,1,0:T(8,128)(2,1)S(1)} %pad_maximum_fusion.8), channel_id=1, source_target_pairs={{0,4},{1,5},{2,6},{3,7},{4,0},{5,1},{6,2},{7,3},{8,12},{9,13},{10,... | collective-permute-start | bytes 1105928 | tf_op jit(solution)/shard_map/ppermute | solution.py:207
  45.6 30.5 %collective-permute-start.4 = (bf16[2,192,384]{2,1,0:T(8,128)(2,1)S(1)}, bf16[2,192,384]{2,1,0:T(8,128)(2,1)S(1)}, u32[]{:S(2)}, u32[]{:S(2)}) collective-permute-start(bf16[2,192,384]{2,1,0:T(8,128)(2,1)S(1)} %pad_maximum_fusion.9), channel_id=1, source_target_pairs={{0,4},{1,5},{2,6},{3,7},{4,0},{5,1},{6,2},{7,3},{8,12},{9,13},{10,... | collective-permute-start | bytes 884744 | tf_op jit(solution)/shard_map/ppermute | solution.py:207
  76.3 321.9 %reduce-scatter.2.cloned.1.call-start = ((), (), s32[]{:S(2)}) async-start(), calls=%async_computation.3 | async-start | bytes 8355840 | tf_op jit(solution)/shard_map/reduce_scatter | solution.py:1191
  76.4 14.9 %collective-permute-start.5 = (bf16[4,48,1920]{2,1,0:T(8,128)(2,1)S(1)}, bf16[4,48,1920]{2,1,0:T(8,128)(2,1)S(1)}, u32[]{:S(2)}, u32[]{:S(2)}) collective-permute-start(bf16[4,48,1920]{2,1,0:T(8,128)(2,1)S(1)} %pad_maximum_fusion.2), channel_id=1, source_target_pairs={{0,2},{1,3},{2,0},{3,1},{4,6},{5,7},{6,4},{7,5},{8,10},{9,11},{10,... | collective-permute-start | bytes 2211848 | tf_op jit(solution)/shard_map/ppermute | solution.py:207
  77.7 11.0 %collective-permute-start.6 = (bf16[4,192,384]{2,1,0:T(8,128)(2,1)S(1)}, bf16[4,192,384]{2,1,0:T(8,128)(2,1)S(1)}, u32[]{:S(2)}, u32[]{:S(2)}) collective-permute-start(bf16[4,192,384]{2,1,0:T(8,128)(2,1)S(1)} %pad_maximum_fusion.4), channel_id=1, source_target_pairs={{0,16},{16,0},{1,17},{17,1},{2,18},{18,2},{3,19},{19,3},{4,20},{20... | collective-permute-start | bytes 1769480 | tf_op jit(solution)/shard_map/ppermute | solution.py:206
  92.5 37.1 %collective-permute-start.7 = (bf16[8,48,1920]{2,1,0:T(8,128)(2,1)}, bf16[8,48,1920]{2,1,0:T(8,128)(2,1)}, u32[]{:S(2)}, u32[]{:S(2)}) collective-permute-start(bf16[8,48,1920]{2,1,0:T(8,128)(2,1)} %pad_maximum_fusion), channel_id=1, source_target_pairs={{0,16},{16,0},{1,17},{17,1},{2,18},{18,2},{3,19},{19,3},{4,20},{20... | collective-permute-start | bytes 4423688 | tf_op jit(solution)/shard_map/ppermute | solution.py:206
  94.5 35.1 %collective-permute-start.8 = (bf16[8,192,384]{2,1,0:T(8,128)(2,1)}, bf16[8,192,384]{2,1,0:T(8,128)(2,1)S(1)}, u32[]{:S(2)}, u32[]{:S(2)}) collective-permute-start(bf16[8,192,384]{2,1,0:T(8,128)(2,1)} %pad_maximum_fusion.1), channel_id=1, source_target_pairs={{0,2},{1,3},{2,0},{3,1},{4,6},{5,7},{6,4},{7,5},{8,10},{9,11},{10,... | collective-permute-start | bytes 3538952 | tf_op jit(solution)/shard_map/ppermute | solution.py:207
  127.5 4.7 %copy-start.25 = (bf16[16,192,384]{2,1,0:T(8,128)(2,1)S(1)}, bf16[16,192,384]{2,1,0:T(8,128)(2,1)}, u32[]{:S(2)}) copy-start(bf16[16,192,384]{2,1,0:T(8,128)(2,1)} %get-tuple-element.278) | copy-start | bytes 7077892
  132.3 8.9 %collective-permute-start.9 = (bf16[16,48,1920]{2,1,0:T(8,128)(2,1)}, bf16[16,48,1920]{2,1,0:T(8,128)(2,1)}, u32[]{:S(2)}, u32[]{:S(2)}) collective-permute-start(bf16[16,48,1920]{2,1,0:T(8,128)(2,1)} %constant_dynamic-update-slice_fusion.rest_0_), channel_id=1, source_target_pairs={{0,1},{1,0},{2,3},{3,2},{4,5},{5,4},{6,7},{7,6},{8,9},{9,8},{10,11... | collective-permute-start | bytes 8847368 | tf_op jit(solution)/shard_map/ppermute | solution.py:207
  134.1 7.1 %collective-permute-start.10 = (bf16[16,192,384]{2,1,0:T(8,128)(2,1)S(1)}, bf16[16,192,384]{2,1,0:T(8,128)(2,1)S(1)}, u32[]{:S(2)}, u32[]{:S(2)}) collective-permute-start(bf16[16,192,384]{2,1,0:T(8,128)(2,1)S(1)} %constant_dynamic-update-slice_fusion.5.rest_2_), channel_id=1, source_target_pairs={{0,1},{1,0},{2,3},{3,2},{4,5},{5,4},{6,7},{7,6},{8,9},{9,8},{10,11... | collective-permute-start | bytes 7077896 | tf_op jit(solution)/shard_map/ppermute | solution.py:207
  135.3 3.5 collective-permute-start.11
  217.4 14.9 %collective-permute-start.13 = (bf16[16,48,1920]{2,1,0:T(8,128)(2,1)}, bf16[16,48,1920]{2,1,0:T(8,128)(2,1)S(1)}, u32[]{:S(2)}, u32[]{:S(2)}) collective-permute-start(bf16[16,48,1920]{2,1,0:T(8,128)(2,1)} %get-tuple-element.122), channel_id=1, source_target_pairs={{0,1},{1,0},{2,3},{3,2},{4,5},{5,4},{6,7},{7,6},{8,9},{9,8},{10,11... | collective-permute-start | bytes 8847368 | tf_op jit(solution)/shard_map/ppermute | solution.py:207
  217.6 9.0 %collective-permute-start.14 = (bf16[16,192,384]{2,1,0:T(8,128)(2,1)}, bf16[16,192,384]{2,1,0:T(8,128)(2,1)}, u32[]{:S(2)}, u32[]{:S(2)}) collective-permute-start(bf16[16,192,384]{2,1,0:T(8,128)(2,1)} %get-tuple-element.124), channel_id=1, source_target_pairs={{0,1},{1,0},{2,3},{3,2},{4,5},{5,4},{6,7},{7,6},{8,9},{9,8},{10,11... | collective-permute-start | bytes 7077896 | tf_op jit(solution)/shard_map/ppermute | solution.py:207
  226.6 7.3 %copy-start.6 = (bf16[16,48,1920]{2,1,0:T(8,128)(2,1)S(1)}, bf16[16,48,1920]{2,1,0:T(8,128)(2,1)}, u32[]{:S(2)}) copy-start(bf16[16,48,1920]{2,1,0:T(8,128)(2,1)} %get-tuple-element.121) | copy-start | bytes 8847364
  231.1 29.4 %collective-permute-start.16 = (bf16[8,192,384]{2,1,0:T(8,128)(2,1)}, bf16[8,192,384]{2,1,0:T(8,128)(2,1)}, u32[]{:S(2)}, u32[]{:S(2)}) collective-permute-start(bf16[8,192,384]{2,1,0:T(8,128)(2,1)} %slice.221), channel_id=1, source_target_pairs={{0,2},{1,3},{2,0},{3,1},{4,6},{5,7},{6,4},{7,5},{8,10},{9,11},{10,... | collective-permute-start | bytes 3538952 | tf_op jit(solution)/shard_map/ppermute | solution.py:207
  237.8 34.4 %collective-permute-start.15 = (bf16[8,48,1920]{2,1,0:T(8,128)(2,1)}, bf16[8,48,1920]{2,1,0:T(8,128)(2,1)}, u32[]{:S(2)}, u32[]{:S(2)}) collective-permute-start(bf16[8,48,1920]{2,1,0:T(8,128)(2,1)} %slice.220), channel_id=1, source_target_pairs={{0,16},{16,0},{1,17},{17,1},{2,18},{18,2},{3,19},{19,3},{4,20},{20... | collective-permute-start | bytes 4423688 | tf_op jit(solution)/shard_map/ppermute | solution.py:206
  277.0 28.2 %collective-permute-start.27 = (bf16[4,48,1920]{2,1,0:T(8,128)(2,1)S(1)}, bf16[4,48,1920]{2,1,0:T(8,128)(2,1)S(1)}, u32[]{:S(2)}, u32[]{:S(2)}) collective-permute-start(bf16[4,48,1920]{2,1,0:T(8,128)(2,1)S(1)} %slice.240), channel_id=1, source_target_pairs={{0,2},{1,3},{2,0},{3,1},{4,6},{5,7},{6,4},{7,5},{8,10},{9,11},{10,... | collective-permute-start | bytes 2211848 | tf_op jit(solution)/shard_map/ppermute | solution.py:207
  277.8 27.3 %collective-permute-start.28 = (bf16[4,192,384]{2,1,0:T(8,128)(2,1)}, bf16[4,192,384]{2,1,0:T(8,128)(2,1)}, u32[]{:S(2)}, u32[]{:S(2)}) collective-permute-start(bf16[4,192,384]{2,1,0:T(8,128)(2,1)} %slice.241), channel_id=1, source_target_pairs={{0,16},{16,0},{1,17},{17,1},{2,18},{18,2},{3,19},{19,3},{4,20},{20... | collective-permute-start | bytes 1769480 | tf_op jit(solution)/shard_map/ppermute | solution.py:206
  279.4 25.8 %copy-start.3 = (bf16[8,48,1920]{2,1,0:T(8,128)(2,1)S(1)}, bf16[8,48,1920]{2,1,0:T(8,128)(2,1)}, u32[]{:S(2)}) copy-start(bf16[8,48,1920]{2,1,0:T(8,128)(2,1)} %copy-done.2) | copy-start | bytes 4423684
  304.5 5.0 %collective-permute-start.17 = (bf16[16,48,640]{2,1,0:T(8,128)(2,1)}, bf16[16,48,640]{2,1,0:T(8,128)(2,1)S(1)}, u32[]{:S(2)}, u32[]{:S(2)}) collective-permute-start(bf16[16,48,640]{2,1,0:T(8,128)(2,1)} %get-tuple-element.138), channel_id=1, source_target_pairs={{0,1},{1,0},{2,3},{3,2},{4,5},{5,4},{6,7},{7,6},{8,9},{9,8},{10,11... | collective-permute-start | bytes 2949128 | tf_op jit(solution)/shard_map/ppermute | solution.py:207
  304.6 7.5 %collective-permute-start.19 = (bf16[16,48,640]{2,1,0:T(8,128)(2,1)}, bf16[16,48,640]{2,1,0:T(8,128)(2,1)S(1)}, u32[]{:S(2)}, u32[]{:S(2)}) collective-permute-start(bf16[16,48,640]{2,1,0:T(8,128)(2,1)} %get-tuple-element.140), channel_id=1, source_target_pairs={{0,1},{1,0},{2,3},{3,2},{4,5},{5,4},{6,7},{7,6},{8,9},{9,8},{10,11... | collective-permute-start | bytes 2949128 | tf_op jit(solution)/shard_map/ppermute | solution.py:207
  305.2 4.3 copy-start.16
  305.4 24.8 %collective-permute-start.29 = (bf16[2,48,1920]{2,1,0:T(8,128)(2,1)S(1)}, bf16[2,48,1920]{2,1,0:T(8,128)(2,1)S(1)}, u32[]{:S(2)}, u32[]{:S(2)}) collective-permute-start(bf16[2,48,1920]{2,1,0:T(8,128)(2,1)S(1)} %slice.243), channel_id=1, source_target_pairs={{0,4},{1,5},{2,6},{3,7},{4,0},{5,1},{6,2},{7,3},{8,12},{9,13},{10,... | collective-permute-start | bytes 1105928 | tf_op jit(solution)/shard_map/ppermute | solution.py:207
  309.4 20.8 %collective-permute-start.30 = (bf16[2,192,384]{2,1,0:T(8,128)(2,1)S(1)}, bf16[2,192,384]{2,1,0:T(8,128)(2,1)S(1)}, u32[]{:S(2)}, u32[]{:S(2)}) collective-permute-start(bf16[2,192,384]{2,1,0:T(8,128)(2,1)S(1)} %slice.245), channel_id=1, source_target_pairs={{0,4},{1,5},{2,6},{3,7},{4,0},{5,1},{6,2},{7,3},{8,12},{9,13},{10,... | collective-permute-start | bytes 884744 | tf_op jit(solution)/shard_map/ppermute | solution.py:207
  310.6 56.5 %collective-permute-start.18 = (bf16[8,48,640]{2,1,0:T(8,128)(2,1)}, bf16[8,48,640]{2,1,0:T(8,128)(2,1)S(1)}, u32[]{:S(2)}, u32[]{:S(2)}) collective-permute-start(bf16[8,48,640]{2,1,0:T(8,128)(2,1)} %slice.224), channel_id=1, source_target_pairs={{0,16},{16,0},{1,17},{17,1},{2,18},{18,2},{3,19},{19,3},{4,20},{20... | collective-permute-start | bytes 1474568 | tf_op jit(solution)/shard_map/ppermute | solution.py:206
  312.4 42.1 %copy-start.32 = (f32[8,128]{1,0:T(8,128)S(1)}, f32[8,128]{1,0:T(8,128)}, u32[]{:S(2)}) copy-start(f32[8,128]{1,0:T(8,128)} %get-tuple-element.112) | copy-start | bytes 12292
  313.2 53.9 %collective-permute-start.20 = (bf16[8,48,640]{2,1,0:T(8,128)(2,1)}, bf16[8,48,640]{2,1,0:T(8,128)(2,1)}, u32[]{:S(2)}, u32[]{:S(2)}) collective-permute-start(bf16[8,48,640]{2,1,0:T(8,128)(2,1)} %slice.225), channel_id=1, source_target_pairs={{0,2},{1,3},{2,0},{3,1},{4,6},{5,7},{6,4},{7,5},{8,10},{9,11},{10,... | collective-permute-start | bytes 1474568 | tf_op jit(solution)/shard_map/ppermute | solution.py:207
  331.0 36.0 %collective-permute-start.31 = (bf16[1,48,1920]{2,1,0:T(8,128)(2,1)}, bf16[1,48,1920]{2,1,0:T(8,128)(2,1)S(1)}, u32[]{:S(2)}, u32[]{:S(2)}) collective-permute-start(bf16[1,48,1920]{2,1,0:T(8,128)(2,1)} %slice.247), channel_id=1, source_target_pairs={{0,8},{1,9},{2,10},{3,11},{4,12},{5,13},{6,14},{7,15},{8,0},{9,1},... | collective-permute-start | bytes 552968 | tf_op jit(solution)/shard_map/ppermute | solution.py:207
  353.9 13.2 %collective-permute-start.32 = (bf16[1,192,384]{2,1,0:T(8,128)(2,1)}, bf16[1,192,384]{2,1,0:T(8,128)(2,1)S(1)}, u32[]{:S(2)}, u32[]{:S(2)}) collective-permute-start(bf16[1,192,384]{2,1,0:T(8,128)(2,1)} %slice.249), channel_id=1, source_target_pairs={{0,8},{1,9},{2,10},{3,11},{4,12},{5,13},{6,14},{7,15},{8,0},{9,1},... | collective-permute-start | bytes 442376 | tf_op jit(solution)/shard_map/ppermute | solution.py:207
  367.2 6.3 %collective-permute-start.21 = (bf16[4,48,640]{2,1,0:T(8,128)(2,1)S(1)}, bf16[4,48,640]{2,1,0:T(8,128)(2,1)S(1)}, u32[]{:S(2)}, u32[]{:S(2)}) collective-permute-start(bf16[4,48,640]{2,1,0:T(8,128)(2,1)S(1)} %slice.227), channel_id=1, source_target_pairs={{0,2},{1,3},{2,0},{3,1},{4,6},{5,7},{6,4},{7,5},{8,10},{9,11},{10,... | collective-permute-start | bytes 737288 | tf_op jit(solution)/shard_map/ppermute | solution.py:207
  368.9 9.0 %collective-permute-start.22 = (bf16[4,48,640]{2,1,0:T(8,128)(2,1)S(1)}, bf16[4,48,640]{2,1,0:T(8,128)(2,1)S(1)}, u32[]{:S(2)}, u32[]{:S(2)}) collective-permute-start(bf16[4,48,640]{2,1,0:T(8,128)(2,1)S(1)} %slice.229), channel_id=1, source_target_pairs={{0,16},{16,0},{1,17},{17,1},{2,18},{18,2},{3,19},{19,3},{4,20},{20... | collective-permute-start | bytes 737288 | tf_op jit(solution)/shard_map/ppermute | solution.py:206
  370.9 22.1 %collective-permute-start.40 = (f32[48,1920]{1,0:T(8,128)S(1)}, f32[48,1920]{1,0:T(8,128)S(1)}, u32[]{:S(2)}, u32[]{:S(2)}) collective-permute-start(f32[48,1920]{1,0:T(8,128)S(1)} %add_bitcast_fusion), channel_id=1, source_target_pairs={{0,16},{16,0},{1,17},{17,1},{2,18},{18,2},{3,19},{19,3},{4,20},{20... | collective-permute-start | bytes 1105928 | tf_op jit(solution)/shard_map/ppermute | solution.py:206
  371.2 17.9 %collective-permute-start.41 = (f32[192,384]{1,0:T(8,128)S(1)}, f32[192,384]{1,0:T(8,128)S(1)}, u32[]{:S(2)}, u32[]{:S(2)}) collective-permute-start(f32[192,384]{1,0:T(8,128)S(1)} %add_bitcast_fusion.1), channel_id=1, source_target_pairs={{0,16},{16,0},{1,17},{17,1},{2,18},{18,2},{3,19},{19,3},{4,20},{20... | collective-permute-start | bytes 884744 | tf_op jit(solution)/shard_map/ppermute | solution.py:206
  378.0 11.8 %collective-permute-start.23 = (bf16[2,48,640]{2,1,0:T(8,128)(2,1)S(1)}, bf16[2,48,640]{2,1,0:T(8,128)(2,1)S(1)}, u32[]{:S(2)}, u32[]{:S(2)}) collective-permute-start(bf16[2,48,640]{2,1,0:T(8,128)(2,1)S(1)} %slice.231), channel_id=1, source_target_pairs={{0,4},{1,5},{2,6},{3,7},{4,0},{5,1},{6,2},{7,3},{8,12},{9,13},{10,... | collective-permute-start | bytes 368648 | tf_op jit(solution)/shard_map/ppermute | solution.py:207
  378.2 32.1 %copy-start.31 = (pred[640]{0:T(1024)(128)(4,1)S(1)}, pred[640]{0:T(1024)(128)(4,1)}, u32[]{:S(2)}) copy-start(pred[640]{0:T(1024)(128)(4,1)} %fusion.16) | copy-start | bytes 1924
  378.2 11.6 %collective-permute-start.24 = (bf16[2,48,640]{2,1,0:T(8,128)(2,1)S(1)}, bf16[2,48,640]{2,1,0:T(8,128)(2,1)S(1)}, u32[]{:S(2)}, u32[]{:S(2)}) collective-permute-start(bf16[2,48,640]{2,1,0:T(8,128)(2,1)S(1)} %slice.233), channel_id=1, source_target_pairs={{0,4},{1,5},{2,6},{3,7},{4,0},{5,1},{6,2},{7,3},{8,12},{9,13},{10,... | collective-permute-start | bytes 368648 | tf_op jit(solution)/shard_map/ppermute | solution.py:207
  389.8 46.6 %copy-start.29 = (f32[4,48]{1,0:T(4,128)S(1)}, f32[4,48]{1,0:T(4,128)}, u32[]{:S(2)}) copy-start(f32[4,48]{1,0:T(4,128)} %param.42) | copy-start | bytes 2308
  389.8 46.6 %copy-start.27 = (f32[4,48]{1,0:T(4,128)S(1)}, f32[4,48]{1,0:T(4,128)}, u32[]{:S(2)}) copy-start(f32[4,48]{1,0:T(4,128)} %param.35) | copy-start | bytes 2308
  389.8 47.2 %copy-start.30 = (f32[4,48]{1,0:T(4,128)S(1)}, f32[4,48]{1,0:T(4,128)}, u32[]{:S(2)}) copy-start(f32[4,48]{1,0:T(4,128)} %param.49) | copy-start | bytes 2308
  389.9 5.8 %collective-permute-start.25 = (bf16[1,48,640]{2,1,0:T(8,128)(2,1)S(1)}, bf16[1,48,640]{2,1,0:T(8,128)(2,1)S(1)}, u32[]{:S(2)}, u32[]{:S(2)}) collective-permute-start(bf16[1,48,640]{2,1,0:T(8,128)(2,1)S(1)} %slice.235), channel_id=1, source_target_pairs={{0,8},{1,9},{2,10},{3,11},{4,12},{5,13},{6,14},{7,15},{8,0},{9,1},... | collective-permute-start | bytes 184328 | tf_op jit(solution)/shard_map/ppermute | solution.py:207
  390.0 6.4 %collective-permute-start.26 = (bf16[1,48,640]{2,1,0:T(8,128)(2,1)S(1)}, bf16[1,48,640]{2,1,0:T(8,128)(2,1)S(1)}, u32[]{:S(2)}, u32[]{:S(2)}) collective-permute-start(bf16[1,48,640]{2,1,0:T(8,128)(2,1)S(1)} %slice.237), channel_id=1, source_target_pairs={{0,8},{1,9},{2,10},{3,11},{4,12},{5,13},{6,14},{7,15},{8,0},{9,1},... | collective-permute-start | bytes 184328 | tf_op jit(solution)/shard_map/ppermute | solution.py:207
  396.4 6.3 %collective-permute-start.39 = (f32[48,640]{1,0:T(8,128)S(1)}, f32[48,640]{1,0:T(8,128)S(1)}, u32[]{:S(2)}, u32[]{:S(2)}) collective-permute-start(f32[48,640]{1,0:T(8,128)S(1)} %add_bitcast_fusion.3), channel_id=1, source_target_pairs={{0,16},{16,0},{1,17},{17,1},{2,18},{18,2},{3,19},{19,3},{4,20},{20... | collective-permute-start | bytes 368648 | tf_op jit(solution)/shard_map/ppermute | solution.py:206
  398.2 13.4 %collective-permute-start.12 = (bf16[48,5000]{1,0:T(8,128)(2,1)}, bf16[48,5000]{1,0:T(8,128)(2,1)S(1)}, u32[]{:S(2)}, u32[]{:S(2)}) collective-permute-start(bf16[48,5000]{1,0:T(8,128)(2,1)} %bitcast.85), channel_id=1, source_target_pairs={{0,16},{16,0},{1,17},{17,1},{2,18},{18,2},{3,19},{19,3},{4,20},{20... | collective-permute-start | bytes 1440008 | tf_op jit(solution)/shard_map/ppermute | solution.py:206
  398.5 11.8 %collective-permute-start.38 = (f32[48,640]{1,0:T(8,128)S(1)}, f32[48,640]{1,0:T(8,128)S(1)}, u32[]{:S(2)}, u32[]{:S(2)}) collective-permute-start(f32[48,640]{1,0:T(8,128)S(1)} %add_bitcast_fusion.2), channel_id=1, source_target_pairs={{0,16},{16,0},{1,17},{17,1},{2,18},{18,2},{3,19},{19,3},{4,20},{20... | collective-permute-start | bytes 368648 | tf_op jit(solution)/shard_map/ppermute | solution.py:206
  404.0 43.3 %copy-start.10 = (f32[48,3072]{1,0:T(8,128)S(1)}, f32[48,3072]{1,0:T(8,128)}, u32[]{:S(2)}) copy-start(f32[48,3072]{1,0:T(8,128)} %param.32) | copy-start | bytes 1769476
  404.0 43.3 %copy-start.17 = (f32[48,3072]{1,0:T(8,128)S(1)}, f32[48,3072]{1,0:T(8,128)}, u32[]{:S(2)}) copy-start(f32[48,3072]{1,0:T(8,128)} %param.46) | copy-start | bytes 1769476
  417.5 1.2 collective-permute-start.33
  418.7 4.5 collective-permute-start.34
  423.2 8.1 %collective-permute-start.35 = (f32[8,128]{1,0:T(8,128)S(1)}, f32[8,128]{1,0:T(8,128)S(1)}, u32[]{:S(2)}, u32[]{:S(2)}) collective-permute-start(f32[8,128]{1,0:T(8,128)S(1)} %fusion.22), channel_id=1, source_target_pairs={{0,4},{1,5},{2,6},{3,7},{4,0},{5,1},{6,2},{7,3},{8,12},{9,13},{10,... | collective-permute-start | bytes 12296 | tf_op jit(solution)/shard_map/ppermute | solution.py:207
  431.4 3.6 collective-permute-start.36
  435.0 4.2 collective-permute-start.37
  445.2 4.5 copy-start.12
  445.2 4.5 copy-start.18
  445.2 4.5 copy-start.19
  449.7 3.1 copy-start.14
  (15 other events, 27.1 us)
Sparse Core Ops, SparseCore 0:
  15.0 63.4 all-gather.2
  81.3 78.6 all-gather.4
  218.2 132.8 reduce-scatter.1

commit v3 on v2

--- a/solution.py
+++ b/solution.py
@@ -211,20 +211,25 @@
     return lax.optimization_barrier((value, others))[0]
 
 
-def gather_step(groups, held, at, *first):
-    found = [swap(value, group.steps[at], group.count) for group, value in zip(groups, held)]
-    found = after(found, *first)
-    return [jnp.concatenate(both) for both in zip(held, found)]
-
-
-def scatter_step(groups, held, at, *first):
-    size = held[0].shape[0] // 2
-    found = [swap(value[size:], group.steps[at], group.count) for group, value in zip(groups, held)]
-    found = after(found, *first)
-    kind = F32 if size == 1 else BF
-    return [
-        (value[:size].astype(F32) + other.astype(F32)).astype(kind) for value, other in zip(held, found)
-    ]
+def gather_all(group, piece):
+    held = piece[None]
+    for step in group.steps:
+        held = jnp.concatenate([held, swap(held, step, group.count)])
+    return held, swap(held, 1, group.count)
+
+
+def added(pair, part):
+    return pair[0][part].astype(F32) + pair[1][part].astype(F32)
+
+
+def scatter_send(group, pair, at):
+    size = pair[0].shape[0] // 2
+    return swap(added(pair, slice(size, None)).astype(BF), group.steps[at], group.count)
+
+
+def scatter_keep(pair, found):
+    size = pair[0].shape[0] // 2
+    return added(pair, slice(0, size)).astype(BF), found
 
 
 def sort_rows(nfeat, count, table, marks, x_query, t_query, x_context, y_context):
@@ -294,7 +299,7 @@
 
     @pl.when(step == 0)
     def _():
-        vectors = weight[:, 3 * model + LANES :].astype(F32).T
+        vectors = weight[:, 3 * model + LANES : 3 * model + 2 * LANES].astype(F32).T
         many = jnp.sum(vectors[4:5, :]) * 32.0 + jnp.sum(vectors[5:6, :])
         gains[...] = jnp.where(iota((8, model), 0) < 4, vectors[:8, :], many)
 
@@ -341,7 +346,7 @@
                 pl.BlockSpec((RB, LANES), q_map),
                 pl.BlockSpec((CB, LANES), c_map),
                 pl.BlockSpec((CB, LANES), c_map),
-                pl.BlockSpec(weight.shape, same),
+                pl.BlockSpec((model, 3 * model + 2 * LANES), same),
             ],
             out_specs=(
                 pl.BlockSpec((RB, model), q_map),
@@ -561,22 +566,24 @@
     return 0.5 * value * (1.0 + bend), 0.5 * (1.0 + bend) + 0.5 * value * (1.0 - bend * bend) * slope
 
 
-def load_feed(groups, sources, wholes, sem, count):
-    first, second = groups
-    split = 2
-    first.load(sources[:split], wholes[:2], [sem.at[0], sem.at[1]], count[4], count[5])
-    second.load(sources[split:], wholes[2:], [sem.at[2]], count[4], count[5])
-
-
-def feed(groups, count, o_ref, h_ref, gains, *rest):
-    sources = rest[: 4 if groups[0].direct else 3]
+def load_feed(group, sources, wholes, sem, count):
+    w_out, w_up, w_down = wholes
+    start = sources[0].shape[1] - w_up.shape[1]
+    out = sources[0].at[:, pl.ds(start - w_out.shape[1], w_out.shape[1])]
+    pltpu.make_async_copy(out, w_out, sem.at[0]).start()
+    pltpu.make_async_copy(sources[0].at[:, pl.ds(start, w_up.shape[1])], w_up, sem.at[1]).start()
+    group.load(sources[1:], [w_down], [sem.at[2]], count[4], count[5])
+
+
+def feed(down_group, count, o_ref, h_ref, gains, *rest):
+    sources = rest[: 3 if down_group.direct else 2]
     (h1_out, b_out, z_out, slope_out, h2_out, f_out, stats, w_out, w_up, w_down, sem) = rest[len(sources) :]
     step = pl.program_id(0)
     hidden = w_up.shape[1]
 
     @pl.when(step == 0)
     def _():
-        load_feed(groups, sources, [w_out, w_up, w_down], sem, count)
+        load_feed(down_group, sources, [w_out, w_up, w_down], sem, count)
         stats[...] = jnp.zeros(stats.shape, F32)
 
     def need(k):
@@ -617,10 +624,10 @@
         )
 
 
-def feed_call(groups, count, attended, stream0, gains, sources):
+def feed_call(down_group, count, attended, stream0, gains, sources):
     local, model = attended.shape
-    whole = [dims for group in groups for dims in group.full_shapes()]
-    hidden = whole[2][0]
+    hidden = down_group.full_shapes()[0][0]
+    whole = [(model, model), (model, hidden), (hidden, model)]
 
     def rows(i, c):
         return (jnp.minimum(i, c[2] * (RB // FB) - 1), 0)
@@ -631,7 +638,7 @@
     narrow = pl.BlockSpec((FB, model), rows)
     wide = pl.BlockSpec((FB, hidden), rows)
     return pl.pallas_call(
-        functools.partial(feed, groups),
+        functools.partial(feed, down_group),
         grid_spec=pltpu.PrefetchScalarGridSpec(
             num_scalar_prefetch=1,
             grid=(local // FB,),
@@ -660,10 +667,12 @@
     return held
 
 
-def head(
-    count, f_ref, t_ref, rows_all, weight_any, grad_any, df_any, loss, weight, grad, df_ref, logits, back, flipped, sems
-):
+def head(group, count, f_ref, t_ref, rows_all, weight_any, *rest):
+    sources = rest[: 2 if group.direct else 1]
+    (grad_any, df_any, loss, weight, grad, df_ref, logits, back, flipped, sems) = rest[len(sources) :]
     chunks = weight.shape[1] // HC
+    plain = weight_any.shape[1] // HC
+    moved = weight.at[:, pl.ds(plain * HC, (chunks - plain) * HC)]
 
     def weight_copy(j):
         return pltpu.make_async_copy(
@@ -680,8 +689,9 @@
             df_ref.at[block(i, RB), :], df_any.at[block(i, RB), :], sems.at[2, i]
         )
 
-    for j in range(chunks):
+    for j in range(plain):
         weight_copy(j).start()
+    group.load(sources, [moved], [sems.at[0, plain]], count[4], count[5])
     loss[...] = jnp.zeros(loss.shape, F32)
     model = f_ref.shape[1]
     lane = iota((RB, HC), 1)
@@ -693,22 +703,28 @@
         target = t_ref[rows, 0:1].astype(jnp.int32)
         live = live_rows(i, count)
 
-        def values(j):
-            @pl.when(i == 0)
+        def first(j, top):
+            @pl.when((i == 0) & (j < plain))
             def _():
                 weight_copy(j).wait()
 
-            return mm(normed, weight[:, block(j, HC)])
-
-        def first(j, top):
-            value = values(j)
+            value = mm(normed, weight[:, block(j, HC)])
             logits[:, block(j, HC)] = value
             return by_lanes(jnp.maximum, top, value)
 
-        top = lax.fori_loop(0, chunks - 1, first, jnp.full((RB, LANES), 3.0 * LOW, F32), unroll=9)
-        value = jnp.where(lane < BINS - (chunks - 1) * HC, values(chunks - 1), LOW)
-        logits[:, (chunks - 1) * HC :] = value
-        top = jnp.max(by_lanes(jnp.maximum, top, value), axis=1, keepdims=True)
+        top = lax.fori_loop(0, plain, first, jnp.full((RB, LANES), 3.0 * LOW, F32), unroll=plain)
+
+        @pl.when(i == 0)
+        def _():
+            loaded(moved, sems.at[0, plain])
+
+        for j in range(plain, chunks):
+            value = mm(normed, weight[:, j * HC : (j + 1) * HC])
+            if (j + 1) * HC > BINS:
+                value = jnp.where(lane < BINS - j * HC, value, LOW)
+            logits[:, j * HC : (j + 1) * HC] = value
+            top = by_lanes(jnp.maximum, top, value)
+        top = jnp.max(top, axis=1, keepdims=True)
 
         def second(j, carry):
             total, hit = carry
@@ -757,13 +773,13 @@
         grad_copy(j).wait()
 
 
-def head_call(count, normed, targets, rows_all, weight):
+def head_call(group, count, normed, targets, rows_all, weight, sources):
     local, model = normed.shape
-    bins = weight.shape[1]
+    bins = weight.shape[1] + group.full_shapes()[0][1]
     return pl.pallas_call(
-        head,
+        functools.partial(head, group),
         out_shape=(shape((model, bins), BF), shape((local, model), F32), shape((8, LANES), F32)),
-        in_specs=[in_smem()] + [in_vmem()] * 3 + [anywhere()],
+        in_specs=[in_smem()] + [in_vmem()] * 3 + [anywhere()] * (1 + len(sources)),
         out_specs=(anywhere(), anywhere(), in_vmem()),
         scratch_shapes=[
             pltpu.VMEM((model, bins), BF),
@@ -777,13 +793,101 @@
         compiler_params=params(),
         cost_estimate=cost(35e9),
         name="head",
-    )(count, normed, targets, rows_all, weight)
-
-
-def feed_back(groups, count, df_ref, h2_ref, h1_ref, gains, o_any, b_any, z_any, slope_any, *rest):
-    sources = rest[: 4 if groups[0].direct else 3]
+    )(count, normed, targets, rows_all, weight, *sources)
+
+
+def over_row_blocks(count, total, body):
+    for blocks in range(1, total // RB + 1):
+
+        @pl.when(count[2] == blocks)
+        def _(blocks=blocks):
+            body(slice(0, blocks * RB))
+
+
+def down_back(group, count, df_any, h2_any, gains, z_any, *rest):
+    targets = rest[: len(group.out_shapes())]
+    (dh2_out, dm_out, gain_out, df_all, h2_all, dh2_all, z_all, dm_all, g_down, r_sem, o_sem, g_sem) = rest[
+        len(targets) :
+    ]
+    hidden = z_all.shape[1]
+    loads = ((df_any, df_all), (h2_any, h2_all), (z_any, z_all))
+    stores = ((dh2_all, dh2_out), (dm_all, dm_out))
+    gain_out[...] = jnp.zeros(gain_out.shape, F32)
+
+    def fetch(i, _):
+        for k, (source, target) in enumerate(loads):
+            pltpu.make_async_copy(source.at[block(i, RB)], target.at[block(i, RB)], r_sem.at[k, i]).start()
+        return 0
+
+    lax.fori_loop(0, count[2], fetch, 0)
+
+    def over_rows(i, _):
+        rows = block(i, RB)
+        for k, (source, target) in enumerate(loads[:2]):
+            pltpu.make_async_copy(source.at[rows], target.at[rows], r_sem.at[k, i]).wait()
+        back, gain3 = rms_back(h2_all[rows, :], gains[2:3, :], df_all[rows, :])
+        dh2_all[rows, :] = back
+        dm_all[rows, :] = back.astype(BF)
+        gain_out[...] += jnp.where(iota(gain_out.shape, 0) == 2, gain3, 0.0)
+        for k, (source, target) in enumerate(stores):
+            pltpu.make_async_copy(source.at[rows], target.at[rows], o_sem.at[k, i]).start()
+        pltpu.make_async_copy(z_any.at[rows], z_all.at[rows], r_sem.at[2, i]).wait()
+        return 0
+
+    lax.fori_loop(0, count[2], over_rows, 0)
+    sems = [g_sem.at[k] for k in range(len(targets))]
+
+    def body(live):
+        def columns(j, _):
+            spot = block(j, HC)
+            g_down[spot, :] = mm_tn(z_all[live, spot], dm_all[live, :]).astype(BF)
+            return 0
+
+        lax.fori_loop(0, hidden // HC, columns, 0, unroll=3)
+
+    over_row_blocks(count, z_all.shape[0], body)
+    group.store([g_down], targets, sems, count[4], count[5])
+
+    def finish(i, _):
+        rows = block(i, RB)
+        for k, (source, target) in enumerate(stores):
+            pltpu.make_async_copy(source.at[rows], target.at[rows], o_sem.at[k, i]).wait()
+        return 0
+
+    lax.fori_loop(0, count[2], finish, 0)
+    group.stored(targets, sems)
+
+
+def down_back_call(group, count, df, stream2, gains, active):
+    local, model = df.shape
+    hidden = active.shape[1]
+    outs = group.out_shapes()
+    return pl.pallas_call(
+        functools.partial(down_back, group),
+        in_specs=[in_smem(), anywhere(), anywhere(), in_vmem(), anywhere()],
+        out_specs=(anywhere(),) * len(outs) + (anywhere(), anywhere(), in_vmem()),
+        scratch_shapes=[
+            pltpu.VMEM((local, model), F32),
+            pltpu.VMEM((local, model), F32),
+            pltpu.VMEM((local, model), F32),
+            pltpu.VMEM((local, hidden), BF),
+            pltpu.VMEM((local, model), BF),
+            pltpu.VMEM((hidden, model), BF),
+            pltpu.SemaphoreType.DMA((3, local // RB)),
+            pltpu.SemaphoreType.DMA((2, local // RB)),
+            pltpu.SemaphoreType.DMA((2,)),
+        ],
+        out_shape=tuple(outs) + (shape((local, model), F32), shape((local, model), BF), shape((8, model), F32)),
+        compiler_params=params(),
+        cost_estimate=cost(10e9),
+        name="down_back",
+    )(count, df, stream2, gains, active)
+
+
+def feed_back(down_group, group, count, dh2_ref, dm_ref, h1_ref, gains, gain3, o_any, b_any, slope_any, *rest):
+    sources = rest[: 3 if down_group.direct else 2]
     rest = rest[len(sources) :]
-    targets = rest[: 4 if groups[0].direct else 3]
+    targets = rest[: len(group.out_shapes())]
     (
         dh1_out,
         do_out,
@@ -793,12 +897,9 @@
         w_down,
         g_out,
         g_up,
-        g_down,
         o_all,
         b_all,
-        z_all,
         slope_all,
-        dm_all,
         da_all,
         w_sem,
         r_sem,
@@ -807,12 +908,12 @@
     step = pl.program_id(0)
     hidden = w_up.shape[1]
     rows = block(step, RB)
-    loads = ((o_any, o_all), (b_any, b_all), (z_any, z_all), (slope_any, slope_all))
+    loads = ((slope_any, slope_all), (o_any, o_all), (b_any, b_all))
 
     @pl.when(step == 0)
     def _():
-        load_feed(groups, sources, [w_out, w_up, w_down], w_sem, count)
-        gain_out[...] = jnp.zeros(gain_out.shape, F32)
+        load_feed(down_group, sources, [w_out, w_up, w_down], w_sem, count)
+        gain_out[...] = gain3[...]
 
         def fetch(i, _):
             for k, (source, target) in enumerate(loads):
@@ -830,9 +931,7 @@
 
     @pl.when(step < count[2])
     def _():
-        back, gain3 = rms_back(h2_ref[...], gains[2:3, :], df_ref[...])
-        dm = back.astype(BF)
-        dm_all[rows, :] = dm
+        dm = dm_ref[...]
         for k, (source, target) in enumerate(loads):
             pltpu.make_async_copy(source.at[rows], target.at[rows], r_sem.at[k, step]).wait()
         need(2)
@@ -845,59 +944,38 @@
             slope_all[rows, spot] = found
             return held + mm_nt(found, w_up[:, spot])
 
-        db = lax.fori_loop(0, hidden // HC, chunk, jnp.zeros(back.shape, F32), unroll=3)
+        db = lax.fori_loop(0, hidden // HC, chunk, jnp.zeros(h1_ref.shape, F32), unroll=3)
         need(0)
         back1, gain2 = rms_back(h1_ref[...], gains[1:2, :], db)
-        stream = back + back1
+        stream = dh2_ref[...] + back1
         dh1_out[...] = stream
         da = stream.astype(BF)
         da_all[rows, :] = da
         do_out[...] = mm_nt(da, w_out[...]).astype(BF)
-        row = iota(gain_out.shape, 0)
-        gain_out[...] += jnp.where(row == 1, gain2, 0.0) + jnp.where(row == 2, gain3, 0.0)
+        gain_out[...] += jnp.where(iota(gain_out.shape, 0) == 1, gain2, 0.0)
 
     @pl.when(step == pl.num_programs(0) - 1)
     def _():
         sems = [g_sem.at[k] for k in range(len(targets))]
-        split = len(targets) * 2 // 4 if groups[0].direct else 2
-
-        def over_row_blocks(body):
-            for blocks in range(1, z_all.shape[0] // RB + 1):
-
-                @pl.when(count[2] == blocks)
-                def _(blocks=blocks):
-                    body(slice(0, blocks * RB))
-
-        @over_row_blocks
-        def _(live):
-            def columns(j, _):
-                spot = block(j, HC)
-                g_down[spot, :] = mm_tn(z_all[live, spot], dm_all[live, :]).astype(BF)
-                return 0
-
-            lax.fori_loop(0, hidden // HC, columns, 0, unroll=2)
-
-        groups[1].store([g_down], targets[split:], sems[split:], count[4], count[5])
-
-        @over_row_blocks
-        def _(live):
+
+        def body(live):
             def columns(j, _):
                 spot = block(j, HC)
                 g_up[:, spot] = mm_tn(b_all[live, :], slope_all[live, spot]).astype(BF)
                 return 0
 
-            lax.fori_loop(0, hidden // HC, columns, 0, unroll=2)
+            lax.fori_loop(0, hidden // HC, columns, 0, unroll=3)
             g_out[...] = mm_tn(o_all[live, :], da_all[live, :]).astype(BF)
 
-        groups[0].store([g_out, g_up], targets[:split], sems[:split], count[4], count[5])
-        groups[0].stored(targets, sems)
-
-
-def feed_back_call(groups, count, df, stream2, stream1, gains, attended, normed, active, slope, sources):
-    local, model = df.shape
-    whole = [dims for group in groups for dims in group.full_shapes()]
-    hidden = whole[2][0]
-    outs = [found for group in groups for found in group.out_shapes()]
+        over_row_blocks(count, slope_all.shape[0], body)
+        group.store([g_out, g_up], targets, sems, count[4], count[5])
+        group.stored(targets, sems)
+
+
+def feed_back_call(down_group, group, count, dh2, dm, stream1, gains, gain3, attended, normed, slope, sources):
+    local, model = dh2.shape
+    hidden = slope.shape[1]
+    outs = group.out_shapes()
 
     def rows(i, c):
         return (jnp.minimum(i, c[2] - 1), 0)
@@ -906,39 +984,41 @@
         return (0, 0)
 
     narrow = pl.BlockSpec((RB, model), rows)
+    fixed = pl.BlockSpec((8, model), same)
     return pl.pallas_call(
-        functools.partial(feed_back, groups),
+        functools.partial(feed_back, down_group, group),
         grid_spec=pltpu.PrefetchScalarGridSpec(
             num_scalar_prefetch=1,
             grid=(local // RB,),
-            in_specs=[narrow, narrow, narrow, pl.BlockSpec((8, model), same)]
-            + [anywhere()] * (4 + len(sources)),
-            out_specs=(anywhere(),) * len(outs) + (narrow, narrow, pl.BlockSpec((8, model), same)),
-            scratch_shapes=[pltpu.VMEM(dims, BF) for dims in whole] * 2
-            + [
+            in_specs=[narrow, narrow, narrow, fixed, fixed] + [anywhere()] * (3 + len(sources)),
+            out_specs=(anywhere(),) * len(outs) + (narrow, narrow, fixed),
+            scratch_shapes=[
+                pltpu.VMEM((model, model), BF),
+                pltpu.VMEM((model, hidden), BF),
+                pltpu.VMEM((hidden, model), BF),
+                pltpu.VMEM((model, model), BF),
+                pltpu.VMEM((model, hidden), BF),
                 pltpu.VMEM((local, model), BF),
                 pltpu.VMEM((local, model), BF),
                 pltpu.VMEM((local, hidden), BF),
-                pltpu.VMEM((local, hidden), BF),
-                pltpu.VMEM((local, model), BF),
                 pltpu.VMEM((local, model), BF),
                 pltpu.SemaphoreType.DMA((3,)),
-                pltpu.SemaphoreType.DMA((4, local // RB)),
-                pltpu.SemaphoreType.DMA((4,)),
+                pltpu.SemaphoreType.DMA((3, local // RB)),
+                pltpu.SemaphoreType.DMA((2,)),
             ],
         ),
         out_shape=tuple(outs)
         + (shape((local, model), F32), shape((local, model), BF), shape((8, model), F32)),
         compiler_params=params(),
-        cost_estimate=cost(35e9),
+        cost_estimate=cost(25e9),
         name="feed_back",
-    )(count, df, stream2, stream1, gains, attended, normed, active, slope, *sources)
+    )(count, dh2, dm, stream1, gains, gain3, attended, normed, slope, *sources)
 
 
 def project_back(
     groups, blocks, count, dq, aq, xq, dh1, h0, dk, dv, ac, xc, yc, gains, gains23, weight, *rest
 ):
-    targets = rest[: 4 if groups[0].direct else 2]
+    targets = rest[: sum(len(group.out_shapes()) for group in groups)]
     total, emb, small, out0, out1, g_sem = rest[len(targets) :]
     step = pl.program_id(0)
     steps = pl.num_programs(0)
@@ -1033,7 +1113,7 @@
                 thin,
                 fixed,
                 fixed,
-                pl.BlockSpec(weight.shape, same),
+                pl.BlockSpec((model, 3 * model + 2 * LANES), same),
             ],
             out_specs=(anywhere(),) * len(outs),
             scratch_shapes=[
@@ -1106,6 +1186,10 @@
     wide = 3 * model
     quarter = (wide + 2 * LANES) // 4
     groups_a = [Group(order, rows, [(quarter, 1)], count_fsdp) for order in (x_last, y_last)]
+    bins = -(-head_weight.shape[1] // HC) * HC
+    plain = bins // HC * 7 // 10 * HC
+    gather_d = Group(x_last, down_weight.shape[0], [(half, 1)], count_fsdp)
+    gather_h = Group(x_last, rows, [((bins - plain) // 2, 1)], count_fsdp)
     groups_b = [
         Group(x_last, rows, [(half, 1), (hidden_half, 1)], count_fsdp),
         Group(y_last, down_weight.shape[0], [(half, 1)], count_fsdp),
@@ -1124,17 +1208,16 @@
             [block_t.T, first_row * marks[None, :], jnp.zeros((rows, LANES - 2 - used), F32)], axis=1
         )
 
-    piece_a = jnp.concatenate([qkv_weight, tail(emb_weight), tail(vectors)], axis=1).astype(BF)
-    pieces_b = [
-        [side_of(out_weight, half), side_of(up_weight, hidden_half)],
-        [side_of(down_weight, half)],
-    ]
-    held_b = [jnp.concatenate(found, axis=1).astype(BF)[None] for found in pieces_b]
-    bins = -(-head_weight.shape[1] // HC) * HC
+    piece_a = jnp.concatenate(
+        [qkv_weight, tail(emb_weight), tail(vectors), out_weight, up_weight], axis=1
+    ).astype(BF)
     spare = bins - head_weight.shape[1]
-    piece_h = jnp.pad(head_weight.astype(BF), ((0, 0), (0, spare)))
+    piece_h = jnp.pad(head_weight[:, plain:], ((0, 0), (0, spare)))
+    piece_h = side_of(piece_h, (bins - plain) // 2).astype(BF)
 
     whole_a = lax.all_gather(piece_a, "fsdp", axis=0, tiled=True)
+    moved_d = gather_all(gather_d, side_of(down_weight, half).astype(BF))
+    moved_h = gather_all(gather_h, piece_h)
 
     pack = jnp.concatenate(
         [
@@ -1164,48 +1247,56 @@
     )
     x_query, t_query, x_context, y_context = sort_rows_call(nfeat, count, table, flag_rows)
 
-    last = len(high_bits)
-    for at in range(last):
-        held_b = gather_step(groups_b, held_b, at, *([x_query] if at == last - 2 else []))
-        if at == last - 2:
-            head_full = lax.all_gather(after(piece_h, held_b), "fsdp", axis=0, tiled=True)
-    x_query = after(x_query, held_b)
+    head_plain = after(head_weight[:, :plain].astype(BF), x_query)
+    head_plain = lax.all_gather(head_plain, "fsdp", axis=0, tiled=True)
+    x_query = after(x_query, moved_d, moved_h)
     queries, keys, values, a_query, a_context, stream0, gains = project_call(
         nfeat, count, x_query, x_context, y_context, whole_a
     )
     row_count = gains[4:5, :LANES]
     row_count = row_count + swap(row_count, "tab", 0)
     attended, logs = attend_call(size, count, queries, keys, values)
-    held_b = gather_step(groups_b, held_b, last, attended)
-    far_b = [swap(held, 1, count_fsdp) for held in held_b]
-    sources_b = [
-        found
-        for group, near, far in zip(groups_b, held_b, far_b)
-        for found in group.sources(near, far, me, tab)
-    ]
+    sources_b = [whole_a, *gather_d.sources(*moved_d, me, tab)]
     stream1, normed2, active, slope, stream2, normed3, stats = feed_call(
-        groups_b, count, attended, stream0, gains, sources_b
+        gather_d, count, attended, stream0, gains, sources_b
     )
-    grad_head, df, loss = head_call(count, normed3, t_query, row_count, head_full)
+    grad_head, df, loss = head_call(
+        gather_h,
+        count,
+        normed3,
+        t_query,
+        row_count,
+        head_plain,
+        gather_h.sources(*moved_h, me, tab),
+    )
     shard_h = lax.optimization_barrier(
         lax.psum_scatter(grad_head, "fsdp", scatter_dimension=0, tiled=True)
     )
-    *outs_b, dh1, grad_o, gains23 = feed_back_call(
-        groups_b, count, df, stream2, stream1, gains, attended, normed2, active, slope, sources_b
+    group_up, group_down = groups_b
+    last = len(high_bits)
+
+    def core_step(group, outs):
+        near, far = group.targets(outs, me, tab)
+        return near, swap(far, 1, count_fsdp)
+
+    *outs_down, dh2, dm, gain3 = down_back_call(group_down, count, df, stream2, gains, active)
+    down = core_step(group_down, outs_down)
+    *outs_up, dh1, grad_o, gains23 = feed_back_call(
+        gather_d, group_up, count, dh2, dm, stream1, gains, gain3, attended, normed2, slope, sources_b
     )
-
-    def core_step(groups, outs):
-        size_of = len(outs) // 2 if groups[0].direct else len(groups[0].parts)
-        pairs = [
-            group.targets(found, me, tab) for group, found in zip(groups, (outs[:size_of], outs[size_of:]))
-        ]
-        return [near + swap(far, 1, count_fsdp) for near, far in pairs]
-
-    grads_b = core_step(groups_b, outs_b)
-    grad_o = after(grad_o, grads_b)
+    up = core_step(group_up, outs_up)
+    down = after(down, grad_o)
+    sent = scatter_send(group_down, down, last)
+    down = scatter_keep(down, sent)
+    grad_o = after(grad_o, down[0])
     dq, dk, dv = attend_back_call(size, count, queries, keys, values, grad_o, attended, logs)
-    grads_b = scatter_step(groups_b, grads_b, last, dq)
-    dq = after(dq, grads_b)
+    up = after(up, dq)
+    down = after(down, dq)
+    sent = scatter_send(group_up, up, last)
+    up = scatter_keep(up, sent)
+    sent = scatter_send(group_down, down, last - 1)
+    down = scatter_keep(down, sent)
+    dq = after(dq, up[0], down[0])
     outs_a = project_back_call(
         groups_a,
         count,
@@ -1223,20 +1314,42 @@
         gains23,
         whole_a,
     )
-    grads_b = scatter_step(groups_b, grads_b, last - 1, outs_a)
-    grads_a = core_step(groups_a, outs_a)
+    size_a = len(groups_a[0].out_shapes())
+    low_a = core_step(groups_a[0], outs_a[:size_a])
+    high_a = core_step(groups_a[1], outs_a[size_a:])
+    up, down = after((up, down), outs_a)
     for at in reversed(range(last + 1)):
-        grads_a = scatter_step(groups_a, grads_a, at)
+        sent_low = scatter_send(groups_a[0], low_a, at)
+        sent_high = scatter_send(groups_a[1], high_a, at)
+        if at < last:
+            sent = scatter_send(group_up, up, at)
+            up = scatter_keep(up, sent)
         if at < last - 1:
-            grads_b = scatter_step(groups_b, grads_b, at)
-    shards_a = [found[0] for found in grads_a]
-    shards_b = [found[0] for found in grads_b]
+            sent = scatter_send(group_down, down, at)
+            down = scatter_keep(down, sent)
+        low_a = scatter_keep(low_a, sent_low)
+        high_a = scatter_keep(high_a, sent_high)
+        if at == last - 1:
+            low_a, shard_h = lax.optimization_barrier((low_a, shard_h))
+    shards_a = [added(pair, 0).astype(BF) for pair in (low_a, high_a)]
+    shards_b = [added(pair, 0).astype(BF) for pair in (up, down)]
 
     shard_h = shard_h[:, : head_weight.shape[1]]
     grad_h = shard_h.astype(F32) + swap(shard_h, "tab", 0).astype(F32)
+    place = jnp.arange(quarter)[None, :] + (2 + tab) * quarter - wide
+    real = (place < nfeat) | ((place >= LANES) & (place < LANES + vectors.shape[0]))
+    keep_a = jnp.where(real, shards_a[1].astype(F32), 0.0)
+    squares = 0.5 * jnp.sum(grad_h * grad_h)
+    for found in (shards_a[0], keep_a, *shards_b):
+        found = found.astype(F32)
+        squares = squares + jnp.sum(found * found)
+    sums = jnp.concatenate([loss[0:1, 0:1], stats[0:3, 0:1], squares.reshape(1, 1)]).reshape(1, 5)
+    sums = jnp.broadcast_to(jnp.pad(sums, ((0, 0), (0, LANES - 5))), (8, LANES))
+    for step in [1] + high_bits + ["tab"]:
+        sums = sums + swap(sums, step, count_fsdp)
     split_a = [halves(tab, found) for found in shards_a]
     split_b = [halves(tab, found) for found in shards_b]
-    whole_grad = jnp.concatenate([side for found in split_a for side in found], axis=1)
+    whole_grad = jnp.concatenate([side for found in split_a for side in found], axis=1).astype(F32)
     grad_qkv = whole_grad[:, :wide]
     grad_emb = whole_grad[:, wide : wide + nfeat].T
     grad_vectors = whole_grad[:, wide + LANES : wide + LANES + vectors.shape[0]].T
@@ -1244,16 +1357,6 @@
     grad_up = jnp.concatenate([side[:, half:] for side in split_b[0]], axis=1)
     grad_down = jnp.concatenate(split_b[1], axis=1)
     summed = (grad_emb, grad_qkv, grad_out, grad_up, grad_down, grad_h, grad_vectors)
-    place = jnp.arange(quarter)[None, :] + (2 + tab) * quarter - wide
-    real = (place < nfeat) | ((place >= LANES) & (place < LANES + vectors.shape[0]))
-    keep_a = jnp.where(real, shards_a[1], 0.0)
-    squares = 0.5 * jnp.sum(grad_h * grad_h)
-    for found in (shards_a[0], keep_a, *shards_b):
-        squares = squares + jnp.sum(found * found)
-    sums = jnp.concatenate([loss[0:1, 0:1], stats[0:3, 0:1], squares.reshape(1, 1)]).reshape(1, 5)
-    sums = jnp.broadcast_to(jnp.pad(sums, ((0, 0), (0, LANES - 5))), (8, LANES))
-    for step in [1] + high_bits + ["tab"]:
-        sums = sums + swap(sums, step, count_fsdp)
     loss_sum = sums[0, 0]
     rms_sums = sums[0, 1:4]
     clip_norm = jnp.sqrt(sums[0, 4])
@@ -1261,7 +1364,7 @@
     factor = jnp.minimum(1.0, CLIP / clip_norm)
     new_moms, new_weights, new_emas = ([], [], [])
     for weight, grad, moment, average in zip(masters, summed, moms, emas):
-        clipped = grad * factor
+        clipped = grad.astype(F32) * factor
         moment_new = MOMENTUM * moment + clipped
         weight_new = weight - RATE * (clipped + MOMENTUM * moment_new)
         new_moms.append(moment_new)

time: 468 us -> 441 us (0.942)
  local copies, waits for them, and re-layouts: 28.9 us -> 12.6 us
  other arithmetic: 45.3 us -> 37.9 us
    convert_element_type x13 -> x17, other arithmetic: 6.81 us -> 16.5 us  [the longest x8 11.3 us: scatter_send(): added(pair, slice(size, None)).astype(BF)]
    add x4 -> x1, other arithmetic: 6.36 us -> 0.01 us  [on_device(): moment_new = MOMENTUM * moment + clipped]
    unnamed x80 -> x86, local copies, waits for them, and re-layouts: 11.5 us -> 5.36 us
    slice x16 -> x2, local copies, waits for them, and re-layouts: 6.55 us -> 0.78 us  [the longest x1 0.77 us: on_device(): head_plain = after(head_weight[:, :plain].astype(BF), x_query)]
    pallas_call x3 -> x4, Pallas kernels: 74.8 us -> 75.9 us  [the longest x1 24.1 us: head_call(): pl.pallas_call(functools.partial(head, group), out_shape=(shape((model, b...]
  transfers between devices with their start and end apart: 45 -> 45, of which waited for: 23 -> 26; matrix products, arithmetic and copies ran while one was open for 10% -> 7% of each run, Pallas kernels for 23% -> 29%
where the time goes in v3:
time: 441 us; the launch traced here: 436 us
  Pallas kernels  162 us (37%)
  waiting for transfers between devices  127 us (29%)
  starting transfers between devices  71.8 us (16%)
  other arithmetic  37.9 us (9%)
  between operations  24.2 us (5%)
  local copies, waits for them, and re-layouts  12.6 us (3%)
    ppermute x28, waiting for transfers between devices, swap(): return lax.ppermute(value, 'fsdp', [(i, i ^ step) for i in range(count)])  82.8 us
    ppermute x28, starting transfers between devices, swap(): return lax.ppermute(value, 'fsdp', [(i, i ^ step) for i in range(count)])  54.9 us
    ppermute x14, waiting for transfers between devices, swap(): return lax.ppermute(value, 'tab', [(0, 1), (1, 0)])  41.6 us
    pallas_call x1, Pallas kernels, project_back_call(): pl.pallas_call(functools.partial(project_back, groups, blocks_q), grid_sp...  25.2 us
    pallas_call x1, Pallas kernels, head_call(): pl.pallas_call(functools.partial(head, group), out_shape=(shape((model, b...  24.1 us
    pallas_call x1, Pallas kernels, feed_back_call(): pl.pallas_call(functools.partial(feed_back, down_group, group), grid_spec...  23.8 us
    pallas_call x1, Pallas kernels, attend_back_call(): pl.pallas_call(functools.partial(attend_back, size), grid_spec=pltpu.Pref...  21.7 us
    pallas_call x1, Pallas kernels, feed_call(): pl.pallas_call(functools.partial(feed, down_group), grid_spec=pltpu.Prefe...  18.6 us
  transfers between devices with their start and end apart: 45, of which 26 were waited for; matrix products, arithmetic and copies ran while one was open for 7% of the time, Pallas kernels for 29%

profile of v3, /device:TPU:0, one launch (start us, length us, event | category | flops | bytes accessed | tf_op | source)
XLA Modules:
  0.0 435.6 jit_solution(15017411419020834047)
XLA Ops:
  7.3 1.4 fusion.45
  15.7 4.0 collective-permute-start.1
  21.6 1.6 collective-permute-start
  24.5 2.2 collective-permute-done.1
  27.5 1.9 collective-permute-done
  32.7 16.9 %collective-permute-done.2 = bf16[2,192,384]{2,1,0:T(8,128)(2,1)S(1)} collective-permute-done((bf16[2,192,384]{2,1,0:T(8,128)(2,1)S(1)}, bf16[2,192,384]{2,1,0:T(8,128)(2,1)S(1)}, u32[]{:S(2)}, u32[]{:S(2)}) %collective-permute-start.2) | collective-permute-done | bytes 294944 | tf_op jit(solution)/shard_map/ppermute | solution.py:207
  51.0 8.3 %sort_rows.1 = (bf16[1024,128]{1,0:T(8,128)(2,1)}, f32[1024,128]{1,0:T(8,128)}, bf16[2048,128]{1,0:T(8,128)(2,1)}, f32[2048,128]{1,0:T(8,128)}) custom-call(s32[8]{0:T(128)} %stack.44.count, bf16[2048,128]{1,0:T(8,128)(2,1)} %pad_maximum_fusion.1.table, f32[16,128]{1,0:T(8,128)} %bitcast.76), custom_call_target="tpu_custom_call" | custom-call | flops 7000000000 | bytes 1048576 | tf_op jit(solution)/shard_map/sort_rows/pallas_call | solution.py:279
  59.4 3.0 collective-permute-done.3
  63.0 7.2 %collective-permute-start.6 = (bf16[1,48,768]{2,1,0:T(8,128)(2,1)S(1)}, bf16[1,48,768]{2,1,0:T(8,128)(2,1)S(1)}, u32[]{:S(2)}, u32[]{:S(2)}) collective-permute-start(bf16[1,48,768]{2,1,0:T(8,128)(2,1)S(1)} %get-tuple-element.271), channel_id=1, source_target_pairs={{0,8},{1,9},{2,10},{3,11},{4,12},{5,13},{6,14},{7,15},{8,0},{9,1},... | collective-permute-start | bytes 221192 | tf_op jit(solution)/shard_map/ppermute | solution.py:207
  70.2 8.2 %collective-permute-done.6 = bf16[1,48,768]{2,1,0:T(8,128)(2,1)S(1)} collective-permute-done((bf16[1,48,768]{2,1,0:T(8,128)(2,1)S(1)}, bf16[1,48,768]{2,1,0:T(8,128)(2,1)S(1)}, u32[]{:S(2)}, u32[]{:S(2)}) %collective-permute-start.6) | collective-permute-done | bytes 73760 | tf_op jit(solution)/shard_map/ppermute | solution.py:207
  78.4 2.3 collective-permute-start.7
  81.0 6.1 %collective-permute-done.4 = bf16[8,192,384]{2,1,0:T(8,128)(2,1)S(1)} collective-permute-done((bf16[8,192,384]{2,1,0:T(8,128)(2,1)S(1)}, bf16[8,192,384]{2,1,0:T(8,128)(2,1)S(1)}, u32[]{:S(2)}, u32[]{:S(2)}) %collective-permute-start.4) | collective-permute-done | bytes 1179680 | tf_op jit(solution)/shard_map/ppermute | solution.py:206
  87.4 6.4 %collective-permute-done.7 = bf16[2,48,768]{2,1,0:T(8,128)(2,1)S(1)} collective-permute-done((bf16[2,48,768]{2,1,0:T(8,128)(2,1)S(1)}, bf16[2,48,768]{2,1,0:T(8,128)(2,1)S(1)}, u32[]{:S(2)}, u32[]{:S(2)}) %collective-permute-start.7) | collective-permute-done | bytes 147488 | tf_op jit(solution)/shard_map/ppermute | solution.py:207
  93.8 1.7 collective-permute-start.8
  95.5 5.1 %collective-permute-done.8 = bf16[4,48,768]{2,1,0:T(8,128)(2,1)S(1)} collective-permute-done((bf16[4,48,768]{2,1,0:T(8,128)(2,1)S(1)}, bf16[4,48,768]{2,1,0:T(8,128)(2,1)S(1)}, u32[]{:S(2)}, u32[]{:S(2)}) %collective-permute-start.8) | collective-permute-done | bytes 294944 | tf_op jit(solution)/shard_map/ppermute | solution.py:207
  101.9 10.4 %collective-permute-done.9 = bf16[8,48,768]{2,1,0:T(8,128)(2,1)S(1)} collective-permute-done((bf16[8,48,768]{2,1,0:T(8,128)(2,1)S(1)}, bf16[8,48,768]{2,1,0:T(8,128)(2,1)S(1)}, u32[]{:S(2)}, u32[]{:S(2)}) %collective-permute-start.9) | collective-permute-done | bytes 589856 | tf_op jit(solution)/shard_map/ppermute | solution.py:206
  112.4 2.8 collective-permute-done.10.rest_1_
  115.3 15.9 %project.1 = (bf16[1024,768]{1,0:T(8,128)(2,1)}, bf16[2048,768]{1,0:T(8,128)(2,1)}, bf16[2048,768]{1,0:T(8,128)(2,1)}, bf16[1024,768]{1,0:T(8,128)(2,1)}, bf16[2...) custom-call(s32[8]{0:T(128)} %stack.44.count, bf16[1024,128]{1,0:T(8,128)(2,1)} %get-tuple-element.83.x_query.xq, ...), custom_call_target="tpu_custom_call" | custom-call | flops 12000000000 | bytes 1048576 | tf_op jit(solution)/shard_map/project/pallas_call | solution.py:340
  133.1 14.7 %attend.1 = (bf16[1024,768]{1,0:T(8,128)(2,1)}, f32[6,8,1024]{2,1,0:T(8,128)}) custom-call(s32[8]{0:T(128)} %stack.44.count, bf16[1024,768]{1,0:T(8,128)(2,1)} %get-tuple-element.86.q_ref, bf16[2048,768]{1,0:T(8,128)(2,1)} %get-tuple-element.87.k_ref, bf16[2048,768]{1,0:T(8,128)(2,1)} %get-tuple-element.88.v_ref), custom_call_target="tpu_custom_call" | custom-call | flops 35000000512 | bytes 1048576 | tf_op jit(solution)/shard_map/attend/pallas_call | solution.py:452
  147.8 18.6 %feed.1 = (f32[1024,768]{1,0:T(8,128)}, bf16[1024,768]{1,0:T(8,128)(2,1)}, bf16[1024,3072]{1,0:T(8,128)(2,1)}, bf16[1024,3072]{1,0:T(8,128)(2,1)}, f32[1024,768]...) custom-call(s32[8]{0:T(128)} %stack.44.count, bf16[1024,768]{1,0:T(8,128)(2,1)} %get-tuple-element.89.o_ref.o_any, ...), custom_call_target="tpu_custom_call" | custom-call | flops 20000000000 | bytes 1048576 | tf_op jit(solution)/shard_map/feed/pallas_call | solution.py:640
  167.6 2.9 all-gather.5.cloned.1.call-done.weight_any
  170.5 24.1 %head.1 = (bf16[768,5120]{1,0:T(8,128)(2,1)}, f32[1024,768]{1,0:T(8,128)}, f32[8,128]{1,0:T(8,128)}) custom-call(s32[8]{0:T(128)} %stack.44.count, bf16[1024,768]{1,0:T(8,128)(2,1)} %get-tuple-element.92.f_ref, f32[1024,128]{1,0:T(8,128)} %get-tuple-element.93.t_ref, f32[1,128]{1,0:T(1,128)} %slice_add_fusion.rows_all, ...), custom_call_target="tpu_custom_call" | custom-call | flops 35000000512 | bytes 1048576 | tf_op jit(solution)/shard_map/head/pallas_call | solution.py:779
  194.5 9.4 %down_back.1 = (bf16[16,192,384]{2,1,0:T(8,128)(2,1)}, bf16[16,192,384]{2,1,0:T(8,128)(2,1)}, f32[1024,768]{1,0:T(8,128)}, bf16[1024,768]{1,0:T(8,128)(2,1)}, f32[8,768]{1,0:T(8,128)}) custom-call(s32[8]{0:T(128)} %stack.44.count, f32[1024,768]{1,0:T(8,128)} %get-tuple-element.97.df_any, f32[1024,768]{1,0:T(8,128)} %get-tuple-element.98.h2_any, ...), custom_call_target="tpu_custom_call" | custom-call | flops 10000000000 | bytes 1048576 | tf_op jit(solution)/shard_map/down_back/pallas_call | solution.py:865
  204.4 23.8 %feed_back.1 = (bf16[16,48,1920]{2,1,0:T(8,128)(2,1)}, bf16[16,48,1920]{2,1,0:T(8,128)(2,1)}, f32[1024,768]{1,0:T(8,128)}, bf16[1024,768]{1,0:T(8,128)(2,1)}, f32[8,768]{1,0:T(8,128)}) custom-call(s32[8]{0:T(128)} %stack.44.count, f32[1024,768]{1,0:T(8,128)} %get-tuple-element.100.dh2_ref, bf16[1024,768]{1,0:T(8,128)(2,1)} %get-tuple-element.101.dm_ref, ...), custom_call_target="tpu_custom_call" | custom-call | flops 24999999488 | bytes 1048576 | tf_op jit(solution)/shard_map/feed_back/pallas_call | solution.py:988
  228.5 1.4 copy-done.2
  229.9 4.2 add_convert_fusion.2
  234.7 21.7 %attend_back.1 = (bf16[1024,768]{1,0:T(8,128)(2,1)}, bf16[2048,768]{1,0:T(8,128)(2,1)}, bf16[2048,768]{1,0:T(8,128)(2,1)}) custom-call(s32[8]{0:T(128)} %stack.44.count, bf16[1024,768]{1,0:T(8,128)(2,1)} %get-tuple-element.86.q_ref, bf16[2048,768]{1,0:T(8,128)(2,1)} %get-tuple-element.87.k_ref, bf16[2048,768]{1,0:T(8,128)(2,1)} %get-tuple-element.88.v_ref, ...), custom_call_target="tpu_custom_call" | custom-call | flops 35000000512 | bytes 1048576 | tf_op jit(solution)/shard_map/attend_back/pallas_call | solution.py:531
  256.5 4.5 %add_convert_fusion = (bf16[8,48,1920]{2,1,0:T(8,128)(2,1)}, bf16[8,48,1920]{2,1,0:T(8,128)(2,1)S(1)}) fusion(bf16[16,48,1920]{2,1,0:T(8,128)(2,1)} %collective-permute-done.13, bf16[16,48,1920]{2,1,0:T(8,128)(2,1)} %get-tuple-element.116), kind=kLoop, calls=%fused_computation | loop fusion | flops 5898240 | bytes 8847360 | tf_op jit(solution)/shard_map/convert_element_type | solution.py:227
  261.0 1.5 collective-permute-start.26
  262.5 15.8 %collective-permute-done.14 = bf16[8,192,384]{2,1,0:T(8,128)(2,1)} collective-permute-done((bf16[8,192,384]{2,1,0:T(8,128)(2,1)}, bf16[8,192,384]{2,1,0:T(8,128)(2,1)}, u32[]{:S(2)}, u32[]{:S(2)}) %collective-permute-start.14) | collective-permute-done | bytes 1179680 | tf_op jit(solution)/shard_map/ppermute | solution.py:207
  278.3 2.3 add_convert_fusion.6
  280.7 25.2 %project_back.1 = (bf16[16,48,640]{2,1,0:T(8,128)(2,1)}, bf16[16,48,640]{2,1,0:T(8,128)(2,1)}, bf16[16,48,640]{2,1,0:T(8,128)(2,1)}, bf16[16,48,640]{2,1,0:T(8,128)(2,1)}) custom-call(s32[8]{0:T(128)} %stack.44.count, bf16[1024,768]{1,0:T(8,128)(2,1)} %get-tuple-element.120.dq, bf16[1024,768]{1,0:T(8,128)(2,1)} %get-tuple-element.121.aq, ...), custom_call_target="tpu_custom_call" | custom-call | flops 20000000000 | bytes 1048576 | tf_op jit(solution)/shard_map/project_back/pallas_call | solution.py:1098
  306.0 1.8 collective-permute-start.27
  309.6 12.1 %collective-permute-done.27 = bf16[4,192,384]{2,1,0:T(8,128)(2,1)S(1)} collective-permute-done((bf16[4,192,384]{2,1,0:T(8,128)(2,1)S(1)}, bf16[4,192,384]{2,1,0:T(8,128)(2,1)S(1)}, u32[]{:S(2)}, u32[]{:S(2)}) %collective-permute-start.27) | collective-permute-done | bytes 589856 | tf_op jit(solution)/shard_map/ppermute | solution.py:206
  321.9 2.0 collective-permute-start.31
  323.8 1.5 add_convert_fusion.9
  325.8 1.4 add_convert_fusion.11
  327.2 1.5 collective-permute-start.16
  328.7 6.8 %collective-permute-done.31 = bf16[2,192,384]{2,1,0:T(8,128)(2,1)S(1)} collective-permute-done((bf16[2,192,384]{2,1,0:T(8,128)(2,1)S(1)}, bf16[2,192,384]{2,1,0:T(8,128)(2,1)S(1)}, u32[]{:S(2)}, u32[]{:S(2)}) %collective-permute-start.31) | collective-permute-done | bytes 294944 | tf_op jit(solution)/shard_map/ppermute | solution.py:207
  335.5 6.1 %collective-permute-start.32 = (bf16[1,192,384]{2,1,0:T(8,128)(2,1)S(1)}, bf16[1,192,384]{2,1,0:T(8,128)(2,1)S(1)}, u32[]{:S(2)}, u32[]{:S(2)}) collective-permute-start(bf16[1,192,384]{2,1,0:T(8,128)(2,1)S(1)} %add_convert_fusion.24), channel_id=1, source_target_pairs={{0,8},{1,9},{2,10},{3,11},{4,12},{5,13},{6,14},{7,15},{8,0},{9,1},... | collective-permute-start | bytes 442376 | tf_op jit(solution)/shard_map/ppermute | solution.py:207
  342.1 1.7 add_convert_fusion.5
  343.8 1.7 collective-permute-start.28
  345.5 2.3 collective-permute-done.32
  350.1 1.6 collective-permute-start.17
  351.7 2.2 collective-permute-done.24
  353.9 9.3 %collective-permute-start.25 = (bf16[1,48,640]{2,1,0:T(8,128)(2,1)S(1)}, bf16[1,48,640]{2,1,0:T(8,128)(2,1)S(1)}, u32[]{:S(2)}, u32[]{:S(2)}) collective-permute-start(bf16[1,48,640]{2,1,0:T(8,128)(2,1)S(1)} %add_convert_fusion.31), channel_id=1, source_target_pairs={{0,8},{1,9},{2,10},{3,11},{4,12},{5,13},{6,14},{7,15},{8,0},{9,1},... | collective-permute-start | bytes 184328 | tf_op jit(solution)/shard_map/ppermute | solution.py:207
  363.5 1.7 collective-permute-start.29
  367.6 4.4 %collective-permute-done.29 = bf16[2,48,1920]{2,1,0:T(8,128)(2,1)S(1)} collective-permute-done((bf16[2,48,1920]{2,1,0:T(8,128)(2,1)S(1)}, bf16[2,48,1920]{2,1,0:T(8,128)(2,1)S(1)}, u32[]{:S(2)}, u32[]{:S(2)}) %collective-permute-start.29) | collective-permute-done | bytes 368672 | tf_op jit(solution)/shard_map/ppermute | solution.py:207
  372.1 8.8 %collective-permute-start.30 = (bf16[1,48,1920]{2,1,0:T(8,128)(2,1)S(1)}, bf16[1,48,1920]{2,1,0:T(8,128)(2,1)S(1)}, u32[]{:S(2)}, u32[]{:S(2)}) collective-permute-start(bf16[1,48,1920]{2,1,0:T(8,128)(2,1)S(1)} %add_convert_fusion.21), channel_id=1, source_target_pairs={{0,8},{1,9},{2,10},{3,11},{4,12},{5,13},{6,14},{7,15},{8,0},{9,1},... | collective-permute-start | bytes 552968 | tf_op jit(solution)/shard_map/ppermute | solution.py:207
  380.8 1.6 collective-permute-start.18
  382.6 2.9 collective-permute-done.30
  386.1 1.5 collective-permute-done.20
  388.3 1.6 collective-permute-done.18
  394.8 1.6 collective-permute-start.39
  396.5 2.7 collective-permute-done.39
  399.3 1.6 collective-permute-start.40
  401.5 4.8 %collective-permute-done.40 = bf16[48,1920]{1,0:T(8,128)(2,1)S(1)} collective-permute-done((bf16[48,1920]{1,0:T(8,128)(2,1)S(1)}, bf16[48,1920]{1,0:T(8,128)(2,1)S(1)}, u32[]{:S(2)}, u32[]{:S(2)}) %collective-permute-start.40) | collective-permute-done | bytes 184352 | tf_op jit(solution)/shard_map/ppermute | solution.py:206
  406.5 1.8 collective-permute-start.36
  408.3 1.8 collective-permute-done.36
  410.1 1.6 collective-permute-start.37
  411.7 2.0 collective-permute-done.37
  418.3 2.3 add_multiply_fusion.3
  420.7 1.4 add_multiply_fusion.1
  425.5 1.9 add_multiply_fusion
  (214 shorter events, 38.0 us)
Async XLA Ops:
  7.2 6.3 %copy-start.13 = (f32[48,768]{1,0:T(8,128)S(1)}, f32[48,768]{1,0:T(8,128)}, u32[]{:S(2)}) copy-start(f32[48,768]{1,0:T(8,128)} %param.31) | copy-start | bytes 442372
  7.2 6.4 %copy-start.29 = (f32[4,48]{1,0:T(4,128)S(1)}, f32[4,48]{1,0:T(4,128)}, u32[]{:S(2)}) copy-start(f32[4,48]{1,0:T(4,128)} %param.35) | copy-start | bytes 2308
  7.2 6.5 %copy-start.23 = (f32[100,48]{0,1:T(8,128)S(1)}, f32[100,48]{0,1:T(8,128)}, u32[]{:S(2)}) copy-start(f32[100,48]{0,1:T(8,128)} %param.29) | copy-start | bytes 57604
  7.2 108.1 %all-gather.3.cloned.1.call-start = ((), (), s32[]{:S(2)}) async-start(), calls=%async_computation.1 | async-start | bytes 10444800 | tf_op jit(solution)/shard_map/all_gather | solution.py:1218
  14.9 155.6 %all-gather.5.cloned.1.call-start = ((), (), s32[]{:S(2)}) async-start(), calls=%async_computation.2 | async-start | bytes 5849088 | tf_op jit(solution)/shard_map/all_gather | solution.py:1251
  15.7 11.0 %collective-permute-start.1 = (bf16[1,192,384]{2,1,0:T(8,128)(2,1)S(1)}, bf16[1,192,384]{2,1,0:T(8,128)(2,1)S(1)}, u32[]{:S(2)}, u32[]{:S(2)}) collective-permute-start(bf16[1,192,384]{2,1,0:T(8,128)(2,1)S(1)} %get-tuple-element.273), channel_id=1, source_target_pairs={{0,8},{1,9},{2,10},{3,11},{4,12},{5,13},{6,14},{7,15},{8,0},{9,1},... | collective-permute-start | bytes 442376 | tf_op jit(solution)/shard_map/ppermute | solution.py:207
  21.6 7.8 %collective-permute-start = (bf16[1024,128]{1,0:T(8,128)(2,1)S(1)}, bf16[1024,128]{1,0:T(8,128)(2,1)S(1)}, u32[]{:S(2)}, u32[]{:S(2)}) collective-permute-start(bf16[1024,128]{1,0:T(8,128)(2,1)S(1)} %concatenate.60), channel_id=1, source_target_pairs={{0,16},{16,0},{1,17},{17,1},{2,18},{18,2},{3,19},{19,3},{4,20},{20... | collective-permute-start | bytes 786440 | tf_op jit(solution)/shard_map/ppermute | solution.py:206
  26.7 22.9 %collective-permute-start.2 = (bf16[2,192,384]{2,1,0:T(8,128)(2,1)S(1)}, bf16[2,192,384]{2,1,0:T(8,128)(2,1)S(1)}, u32[]{:S(2)}, u32[]{:S(2)}) collective-permute-start(bf16[2,192,384]{2,1,0:T(8,128)(2,1)S(1)} %pad_maximum_fusion.4), channel_id=1, source_target_pairs={{0,4},{1,5},{2,6},{3,7},{4,0},{5,1},{6,2},{7,3},{8,12},{9,13},{10,... | collective-permute-start | bytes 884744 | tf_op jit(solution)/shard_map/ppermute | solution.py:207
  49.7 12.8 %collective-permute-start.3 = (bf16[4,192,384]{2,1,0:T(8,128)(2,1)S(1)}, bf16[4,192,384]{2,1,0:T(8,128)(2,1)S(1)}, u32[]{:S(2)}, u32[]{:S(2)}) collective-permute-start(bf16[4,192,384]{2,1,0:T(8,128)(2,1)S(1)} %pad_maximum_fusion.2), channel_id=1, source_target_pairs={{0,2},{1,3},{2,0},{3,1},{4,6},{5,7},{6,4},{7,5},{8,10},{9,11},{10,... | collective-permute-start | bytes 1769480 | tf_op jit(solution)/shard_map/ppermute | solution.py:207
  59.3 307.0 %reduce-scatter.2.cloned.1.call-start = ((), (), s32[]{:S(2)}) async-start(), calls=%async_computation.3 | async-start | bytes 8355840 | tf_op jit(solution)/shard_map/reduce_scatter | solution.py:1273
  59.4 21.4 %copy-start.27 = (bf16[16,192,384]{2,1,0:T(8,128)(2,1)S(1)}, bf16[16,192,384]{2,1,0:T(8,128)(2,1)}, u32[]{:S(2)}) copy-start(bf16[16,192,384]{2,1,0:T(8,128)(2,1)} %get-tuple-element.272) | copy-start | bytes 7077892
  62.6 24.5 %collective-permute-start.4 = (bf16[8,192,384]{2,1,0:T(8,128)(2,1)S(1)}, bf16[8,192,384]{2,1,0:T(8,128)(2,1)S(1)}, u32[]{:S(2)}, u32[]{:S(2)}) collective-permute-start(bf16[8,192,384]{2,1,0:T(8,128)(2,1)S(1)} %pad_maximum_fusion), channel_id=1, source_target_pairs={{0,16},{16,0},{1,17},{17,1},{2,18},{18,2},{3,19},{19,3},{4,20},{20... | collective-permute-start | bytes 3538952 | tf_op jit(solution)/shard_map/ppermute | solution.py:206
  63.0 15.4 %collective-permute-start.6 = (bf16[1,48,768]{2,1,0:T(8,128)(2,1)S(1)}, bf16[1,48,768]{2,1,0:T(8,128)(2,1)S(1)}, u32[]{:S(2)}, u32[]{:S(2)}) collective-permute-start(bf16[1,48,768]{2,1,0:T(8,128)(2,1)S(1)} %get-tuple-element.271), channel_id=1, source_target_pairs={{0,8},{1,9},{2,10},{3,11},{4,12},{5,13},{6,14},{7,15},{8,0},{9,1},... | collective-permute-start | bytes 221192 | tf_op jit(solution)/shard_map/ppermute | solution.py:207
  78.4 15.4 %collective-permute-start.7 = (bf16[2,48,768]{2,1,0:T(8,128)(2,1)S(1)}, bf16[2,48,768]{2,1,0:T(8,128)(2,1)S(1)}, u32[]{:S(2)}, u32[]{:S(2)}) collective-permute-start(bf16[2,48,768]{2,1,0:T(8,128)(2,1)S(1)} %pad_maximum_fusion.8), channel_id=1, source_target_pairs={{0,4},{1,5},{2,6},{3,7},{4,0},{5,1},{6,2},{7,3},{8,12},{9,13},{10,... | collective-permute-start | bytes 442376 | tf_op jit(solution)/shard_map/ppermute | solution.py:207
  87.3 25.0 %copy-start.28 = (bf16[16,192,384]{2,1,0:T(8,128)(2,1)}, bf16[16,192,384]{2,1,0:T(8,128)(2,1)S(1)}, u32[]{:S(2)}) copy-start(bf16[16,192,384]{2,1,0:T(8,128)(2,1)S(1)} %constant_dynamic-update-slice_fusion.rest_1_) | copy-start | bytes 7077892
  87.3 28.0 %collective-permute-start.5 = (bf16[16,192,384]{2,1,0:T(8,128)(2,1)S(1)}, bf16[16,192,384]{2,1,0:T(8,128)(2,1)}, u32[]{:S(2)}, u32[]{:S(2)}) collective-permute-start(bf16[16,192,384]{2,1,0:T(8,128)(2,1)S(1)} %constant_dynamic-update-slice_fusion.rest_1_), channel_id=1, source_target_pairs={{0,1},{1,0},{2,3},{3,2},{4,5},{5,4},{6,7},{7,6},{8,9},{9,8},{10,11... | collective-permute-start | bytes 7077896 | tf_op jit(solution)/shard_map/ppermute | solution.py:207
  93.8 6.8 %collective-permute-start.8 = (bf16[4,48,768]{2,1,0:T(8,128)(2,1)S(1)}, bf16[4,48,768]{2,1,0:T(8,128)(2,1)S(1)}, u32[]{:S(2)}, u32[]{:S(2)}) collective-permute-start(bf16[4,48,768]{2,1,0:T(8,128)(2,1)S(1)} %pad_maximum_fusion.5), channel_id=1, source_target_pairs={{0,2},{1,3},{2,0},{3,1},{4,6},{5,7},{6,4},{7,5},{8,10},{9,11},{10,... | collective-permute-start | bytes 884744 | tf_op jit(solution)/shard_map/ppermute | solution.py:207
  100.7 11.6 %collective-permute-start.9 = (bf16[8,48,768]{2,1,0:T(8,128)(2,1)S(1)}, bf16[8,48,768]{2,1,0:T(8,128)(2,1)S(1)}, u32[]{:S(2)}, u32[]{:S(2)}) collective-permute-start(bf16[8,48,768]{2,1,0:T(8,128)(2,1)S(1)} %pad_maximum_fusion.3), channel_id=1, source_target_pairs={{0,16},{16,0},{1,17},{17,1},{2,18},{18,2},{3,19},{19,3},{4,20},{20... | collective-permute-start | bytes 1769480 | tf_op jit(solution)/shard_map/ppermute | solution.py:206
  112.4 18.9 %copy-start.31 = (bf16[16,48,768]{2,1,0:T(8,128)(2,1)}, bf16[16,48,768]{2,1,0:T(8,128)(2,1)S(1)}, u32[]{:S(2)}) copy-start(bf16[16,48,768]{2,1,0:T(8,128)(2,1)S(1)} %constant_dynamic-update-slice_fusion.5.rest_0_) | copy-start | bytes 3538948
  112.4 2.9 collective-permute-start.10
  115.3 15.9 %copy-start.36 = (bf16[16,48,768]{2,1,0:T(8,128)(2,1)}, bf16[16,48,768]{2,1,0:T(8,128)(2,1)S(1)}, u32[]{:S(2)}) copy-start(bf16[16,48,768]{2,1,0:T(8,128)(2,1)S(1)} %collective-permute-done.10.rest_1_) | copy-start | bytes 3538948
  131.9 34.4 %collective-permute-start.11 = (f32[1,128]{1,0:T(1,128)S(1)}, f32[1,128]{1,0:T(1,128)S(1)}, u32[]{:S(2)}, u32[]{:S(2)}) collective-permute-start(f32[1,128]{1,0:T(1,128)S(1)} %slice.267), channel_id=1, source_target_pairs={{0,16},{16,0},{1,17},{17,1},{2,18},{18,2},{3,19},{19,3},{4,20},{20... | collective-permute-start | bytes 1544 | tf_op jit(solution)/shard_map/ppermute | solution.py:206
  204.0 24.5 %collective-permute-start.12 = (bf16[16,192,384]{2,1,0:T(8,128)(2,1)}, bf16[16,192,384]{2,1,0:T(8,128)(2,1)S(1)}, u32[]{:S(2)}, u32[]{:S(2)}) collective-permute-start(bf16[16,192,384]{2,1,0:T(8,128)(2,1)} %get-tuple-element.108), channel_id=1, source_target_pairs={{0,1},{1,0},{2,3},{3,2},{4,5},{5,4},{6,7},{7,6},{8,9},{9,8},{10,11... | collective-permute-start | bytes 7077896 | tf_op jit(solution)/shard_map/ppermute | solution.py:207
  228.2 28.3 %collective-permute-start.13 = (bf16[16,48,1920]{2,1,0:T(8,128)(2,1)}, bf16[16,48,1920]{2,1,0:T(8,128)(2,1)}, u32[]{:S(2)}, u32[]{:S(2)}) collective-permute-start(bf16[16,48,1920]{2,1,0:T(8,128)(2,1)} %get-tuple-element.115), channel_id=1, source_target_pairs={{0,1},{1,0},{2,3},{3,2},{4,5},{5,4},{6,7},{7,6},{8,9},{9,8},{10,11... | collective-permute-start | bytes 8847368 | tf_op jit(solution)/shard_map/ppermute | solution.py:207
  234.1 44.2 %collective-permute-start.14 = (bf16[8,192,384]{2,1,0:T(8,128)(2,1)}, bf16[8,192,384]{2,1,0:T(8,128)(2,1)}, u32[]{:S(2)}, u32[]{:S(2)}) collective-permute-start(bf16[8,192,384]{2,1,0:T(8,128)(2,1)} %get-tuple-element.276), channel_id=1, source_target_pairs={{0,2},{1,3},{2,0},{3,1},{4,6},{5,7},{6,4},{7,5},{8,10},{9,11},{10,... | collective-permute-start | bytes 3538952 | tf_op jit(solution)/shard_map/ppermute | solution.py:207
  261.0 60.7 %collective-permute-start.26 = (bf16[8,48,1920]{2,1,0:T(8,128)(2,1)}, bf16[8,48,1920]{2,1,0:T(8,128)(2,1)}, u32[]{:S(2)}, u32[]{:S(2)}) collective-permute-start(bf16[8,48,1920]{2,1,0:T(8,128)(2,1)} %get-tuple-element.274), channel_id=1, source_target_pairs={{0,16},{16,0},{1,17},{17,1},{2,18},{18,2},{3,19},{19,3},{4,20},{20... | collective-permute-start | bytes 4423688 | tf_op jit(solution)/shard_map/ppermute | solution.py:206
  280.6 25.3 %copy-start.12 = (bf16[4,192,384]{2,1,0:T(8,128)(2,1)S(1)}, bf16[4,192,384]{2,1,0:T(8,128)(2,1)}, u32[]{:S(2)}) copy-start(bf16[4,192,384]{2,1,0:T(8,128)(2,1)} %get-tuple-element.280) | copy-start | bytes 1769476
  280.6 27.3 %copy-start.30 = (f32[4,48]{1,0:T(4,128)S(1)}, f32[4,48]{1,0:T(4,128)}, u32[]{:S(2)}) copy-start(f32[4,48]{1,0:T(4,128)} %param.35) | copy-start | bytes 2308
  280.6 27.4 %copy-start.33 = (f32[4,48]{1,0:T(4,128)S(1)}, f32[4,48]{1,0:T(4,128)}, u32[]{:S(2)}) copy-start(f32[4,48]{1,0:T(4,128)} %param.42) | copy-start | bytes 2308
  280.6 27.5 %copy-start.34 = (f32[4,48]{1,0:T(4,128)S(1)}, f32[4,48]{1,0:T(4,128)}, u32[]{:S(2)}) copy-start(f32[4,48]{1,0:T(4,128)} %param.49) | copy-start | bytes 2308
  280.6 27.6 %copy-start.35 = (f32[8,128]{1,0:T(8,128)S(1)}, f32[8,128]{1,0:T(8,128)}, u32[]{:S(2)}) copy-start(f32[8,128]{1,0:T(8,128)} %get-tuple-element.96) | copy-start | bytes 12292
  305.9 18.0 %collective-permute-start.21 = (bf16[16,48,640]{2,1,0:T(8,128)(2,1)}, bf16[16,48,640]{2,1,0:T(8,128)(2,1)}, u32[]{:S(2)}, u32[]{:S(2)}) collective-permute-start(bf16[16,48,640]{2,1,0:T(8,128)(2,1)} %get-tuple-element.134), channel_id=1, source_target_pairs={{0,1},{1,0},{2,3},{3,2},{4,5},{5,4},{6,7},{7,6},{8,9},{9,8},{10,11... | collective-permute-start | bytes 2949128 | tf_op jit(solution)/shard_map/ppermute | solution.py:207
  306.0 15.7 %collective-permute-start.27 = (bf16[4,192,384]{2,1,0:T(8,128)(2,1)S(1)}, bf16[4,192,384]{2,1,0:T(8,128)(2,1)S(1)}, u32[]{:S(2)}, u32[]{:S(2)}) collective-permute-start(bf16[4,192,384]{2,1,0:T(8,128)(2,1)S(1)} %copy-done.12), channel_id=1, source_target_pairs={{0,16},{16,0},{1,17},{17,1},{2,18},{18,2},{3,19},{19,3},{4,20},{20... | collective-permute-start | bytes 1769480 | tf_op jit(solution)/shard_map/ppermute | solution.py:206
  307.8 18.0 %collective-permute-start.15 = (bf16[16,48,640]{2,1,0:T(8,128)(2,1)}, bf16[16,48,640]{2,1,0:T(8,128)(2,1)}, u32[]{:S(2)}, u32[]{:S(2)}) collective-permute-start(bf16[16,48,640]{2,1,0:T(8,128)(2,1)} %get-tuple-element.128), channel_id=1, source_target_pairs={{0,1},{1,0},{2,3},{3,2},{4,5},{5,4},{6,7},{7,6},{8,9},{9,8},{10,11... | collective-permute-start | bytes 2949128 | tf_op jit(solution)/shard_map/ppermute | solution.py:207
  308.4 15.5 %copy-start.11 = (bf16[16,48,640]{2,1,0:T(8,128)(2,1)S(1)}, bf16[16,48,640]{2,1,0:T(8,128)(2,1)}, u32[]{:S(2)}) copy-start(bf16[16,48,640]{2,1,0:T(8,128)(2,1)} %get-tuple-element.133) | copy-start | bytes 2949124
  321.9 13.6 %collective-permute-start.31 = (bf16[2,192,384]{2,1,0:T(8,128)(2,1)S(1)}, bf16[2,192,384]{2,1,0:T(8,128)(2,1)S(1)}, u32[]{:S(2)}, u32[]{:S(2)}) collective-permute-start(bf16[2,192,384]{2,1,0:T(8,128)(2,1)S(1)} %get-tuple-element.289), channel_id=1, source_target_pairs={{0,4},{1,5},{2,6},{3,7},{4,0},{5,1},{6,2},{7,3},{8,12},{9,13},{10,... | collective-permute-start | bytes 884744 | tf_op jit(solution)/shard_map/ppermute | solution.py:207
  325.3 16.3 %collective-permute-start.22 = (bf16[8,48,640]{2,1,0:T(8,128)(2,1)S(1)}, bf16[8,48,640]{2,1,0:T(8,128)(2,1)S(1)}, u32[]{:S(2)}, u32[]{:S(2)}) collective-permute-start(bf16[8,48,640]{2,1,0:T(8,128)(2,1)S(1)} %get-tuple-element.283), channel_id=1, source_target_pairs={{0,2},{1,3},{2,0},{3,1},{4,6},{5,7},{6,4},{7,5},{8,10},{9,11},{10,... | collective-permute-start | bytes 1474568 | tf_op jit(solution)/shard_map/ppermute | solution.py:207
  327.2 22.8 %collective-permute-start.16 = (bf16[8,48,640]{2,1,0:T(8,128)(2,1)S(1)}, bf16[8,48,640]{2,1,0:T(8,128)(2,1)S(1)}, u32[]{:S(2)}, u32[]{:S(2)}) collective-permute-start(bf16[8,48,640]{2,1,0:T(8,128)(2,1)S(1)} %get-tuple-element.285), channel_id=1, source_target_pairs={{0,16},{16,0},{1,17},{17,1},{2,18},{18,2},{3,19},{19,3},{4,20},{20... | collective-permute-start | bytes 1474568 | tf_op jit(solution)/shard_map/ppermute | solution.py:206
  335.5 12.3 %collective-permute-start.32 = (bf16[1,192,384]{2,1,0:T(8,128)(2,1)S(1)}, bf16[1,192,384]{2,1,0:T(8,128)(2,1)S(1)}, u32[]{:S(2)}, u32[]{:S(2)}) collective-permute-start(bf16[1,192,384]{2,1,0:T(8,128)(2,1)S(1)} %add_convert_fusion.24), channel_id=1, source_target_pairs={{0,8},{1,9},{2,10},{3,11},{4,12},{5,13},{6,14},{7,15},{8,0},{9,1},... | collective-permute-start | bytes 442376 | tf_op jit(solution)/shard_map/ppermute | solution.py:207
  341.7 7.2 %collective-permute-start.23 = (bf16[4,48,640]{2,1,0:T(8,128)(2,1)S(1)}, bf16[4,48,640]{2,1,0:T(8,128)(2,1)S(1)}, u32[]{:S(2)}, u32[]{:S(2)}) collective-permute-start(bf16[4,48,640]{2,1,0:T(8,128)(2,1)S(1)} %get-tuple-element.291), channel_id=1, source_target_pairs={{0,16},{16,0},{1,17},{17,1},{2,18},{18,2},{3,19},{19,3},{4,20},{20... | collective-permute-start | bytes 737288 | tf_op jit(solution)/shard_map/ppermute | solution.py:206
  343.8 19.5 %collective-permute-start.28 = (bf16[4,48,1920]{2,1,0:T(8,128)(2,1)S(1)}, bf16[4,48,1920]{2,1,0:T(8,128)(2,1)S(1)}, u32[]{:S(2)}, u32[]{:S(2)}) collective-permute-start(bf16[4,48,1920]{2,1,0:T(8,128)(2,1)S(1)} %get-tuple-element.279), channel_id=1, source_target_pairs={{0,2},{1,3},{2,0},{3,1},{4,6},{5,7},{6,4},{7,5},{8,10},{9,11},{10,... | collective-permute-start | bytes 2211848 | tf_op jit(solution)/shard_map/ppermute | solution.py:207
  348.5 46.3 %collective-permute-start.41 = (bf16[192,384]{1,0:T(8,128)(2,1)S(1)}, bf16[192,384]{1,0:T(8,128)(2,1)S(1)}, u32[]{:S(2)}, u32[]{:S(2)}) collective-permute-start(bf16[192,384]{1,0:T(8,128)(2,1)S(1)} %get-tuple-element.263), channel_id=1, source_target_pairs={{0,16},{16,0},{1,17},{17,1},{2,18},{18,2},{3,19},{19,3},{4,20},{20... | collective-permute-start | bytes 442376 | tf_op jit(solution)/shard_map/ppermute | solution.py:206
  349.0 4.9 %collective-permute-start.24 = (bf16[2,48,640]{2,1,0:T(8,128)(2,1)S(1)}, bf16[2,48,640]{2,1,0:T(8,128)(2,1)S(1)}, u32[]{:S(2)}, u32[]{:S(2)}) collective-permute-start(bf16[2,48,640]{2,1,0:T(8,128)(2,1)S(1)} %get-tuple-element.299), channel_id=1, source_target_pairs={{0,4},{1,5},{2,6},{3,7},{4,0},{5,1},{6,2},{7,3},{8,12},{9,13},{10,... | collective-permute-start | bytes 368648 | tf_op jit(solution)/shard_map/ppermute | solution.py:207
  350.1 16.3 %collective-permute-start.17 = (bf16[4,48,640]{2,1,0:T(8,128)(2,1)S(1)}, bf16[4,48,640]{2,1,0:T(8,128)(2,1)S(1)}, u32[]{:S(2)}, u32[]{:S(2)}) collective-permute-start(bf16[4,48,640]{2,1,0:T(8,128)(2,1)S(1)} %get-tuple-element.292), channel_id=1, source_target_pairs={{0,2},{1,3},{2,0},{3,1},{4,6},{5,7},{6,4},{7,5},{8,10},{9,11},{10,... | collective-permute-start | bytes 737288 | tf_op jit(solution)/shard_map/ppermute | solution.py:207
  353.9 11.8 %collective-permute-start.25 = (bf16[1,48,640]{2,1,0:T(8,128)(2,1)S(1)}, bf16[1,48,640]{2,1,0:T(8,128)(2,1)S(1)}, u32[]{:S(2)}, u32[]{:S(2)}) collective-permute-start(bf16[1,48,640]{2,1,0:T(8,128)(2,1)S(1)} %add_convert_fusion.31), channel_id=1, source_target_pairs={{0,8},{1,9},{2,10},{3,11},{4,12},{5,13},{6,14},{7,15},{8,0},{9,1},... | collective-permute-start | bytes 184328 | tf_op jit(solution)/shard_map/ppermute | solution.py:207
  363.5 8.5 %collective-permute-start.29 = (bf16[2,48,1920]{2,1,0:T(8,128)(2,1)S(1)}, bf16[2,48,1920]{2,1,0:T(8,128)(2,1)S(1)}, u32[]{:S(2)}, u32[]{:S(2)}) collective-permute-start(bf16[2,48,1920]{2,1,0:T(8,128)(2,1)S(1)} %get-tuple-element.287), channel_id=1, source_target_pairs={{0,4},{1,5},{2,6},{3,7},{4,0},{5,1},{6,2},{7,3},{8,12},{9,13},{10,... | collective-permute-start | bytes 1105928 | tf_op jit(solution)/shard_map/ppermute | solution.py:207
  366.3 23.5 %copy-start.4 = (bf16[48,5120]{1,0:T(8,128)(2,1)S(1)}, bf16[48,5120]{1,0:T(8,128)(2,1)}, u32[]{:S(2)}) copy-start(bf16[48,5120]{1,0:T(8,128)(2,1)} %reduce-scatter.2.cloned.1.call-done) | copy-start | bytes 1474564
  366.4 16.0 %collective-permute-start.19 = (bf16[2,48,640]{2,1,0:T(8,128)(2,1)S(1)}, bf16[2,48,640]{2,1,0:T(8,128)(2,1)S(1)}, u32[]{:S(2)}, u32[]{:S(2)}) collective-permute-start(bf16[2,48,640]{2,1,0:T(8,128)(2,1)S(1)} %get-tuple-element.301), channel_id=1, source_target_pairs={{0,4},{1,5},{2,6},{3,7},{4,0},{5,1},{6,2},{7,3},{8,12},{9,13},{10,... | collective-permute-start | bytes 368648 | tf_op jit(solution)/shard_map/ppermute | solution.py:207
  372.1 13.4 %collective-permute-start.30 = (bf16[1,48,1920]{2,1,0:T(8,128)(2,1)S(1)}, bf16[1,48,1920]{2,1,0:T(8,128)(2,1)S(1)}, u32[]{:S(2)}, u32[]{:S(2)}) collective-permute-start(bf16[1,48,1920]{2,1,0:T(8,128)(2,1)S(1)} %add_convert_fusion.21), channel_id=1, source_target_pairs={{0,8},{1,9},{2,10},{3,11},{4,12},{5,13},{6,14},{7,15},{8,0},{9,1},... | collective-permute-start | bytes 552968 | tf_op jit(solution)/shard_map/ppermute | solution.py:207
  380.8 9.0 %collective-permute-start.18 = (bf16[48,5000]{1,0:T(8,128)(2,1)}, bf16[48,5000]{1,0:T(8,128)(2,1)S(1)}, u32[]{:S(2)}, u32[]{:S(2)}) collective-permute-start(bf16[48,5000]{1,0:T(8,128)(2,1)} %bitcast.73), channel_id=1, source_target_pairs={{0,16},{16,0},{1,17},{17,1},{2,18},{18,2},{3,19},{19,3},{4,20},{20... | collective-permute-start | bytes 1440008 | tf_op jit(solution)/shard_map/ppermute | solution.py:206
  382.4 5.2 %collective-permute-start.20 = (bf16[1,48,640]{2,1,0:T(8,128)(2,1)S(1)}, bf16[1,48,640]{2,1,0:T(8,128)(2,1)S(1)}, u32[]{:S(2)}, u32[]{:S(2)}) collective-permute-start(bf16[1,48,640]{2,1,0:T(8,128)(2,1)S(1)} %add_convert_fusion.34), channel_id=1, source_target_pairs={{0,8},{1,9},{2,10},{3,11},{4,12},{5,13},{6,14},{7,15},{8,0},{9,1},... | collective-permute-start | bytes 184328 | tf_op jit(solution)/shard_map/ppermute | solution.py:207
  394.7 1.7 collective-permute-start.33
  394.8 4.5 %collective-permute-start.39 = (bf16[48,640]{1,0:T(8,128)(2,1)S(1)}, bf16[48,640]{1,0:T(8,128)(2,1)S(1)}, u32[]{:S(2)}, u32[]{:S(2)}) collective-permute-start(bf16[48,640]{1,0:T(8,128)(2,1)S(1)} %get-tuple-element.267), channel_id=1, source_target_pairs={{0,16},{16,0},{1,17},{17,1},{2,18},{18,2},{3,19},{19,3},{4,20},{20... | collective-permute-start | bytes 184328 | tf_op jit(solution)/shard_map/ppermute | solution.py:206
  396.5 5.0 %collective-permute-start.34 = (f32[8,128]{1,0:T(8,128)S(1)}, f32[8,128]{1,0:T(8,128)S(1)}, u32[]{:S(2)}, u32[]{:S(2)}) collective-permute-start(f32[8,128]{1,0:T(8,128)S(1)} %broadcast_add_fusion), channel_id=1, source_target_pairs={{0,8},{1,9},{2,10},{3,11},{4,12},{5,13},{6,14},{7,15},{8,0},{9,1},... | collective-permute-start | bytes 12296 | tf_op jit(solution)/shard_map/ppermute | solution.py:207
  399.3 18.3 %copy-start.24 = (f32[100,48]{0,1:T(8,128)S(1)}, f32[100,48]{0,1:T(8,128)}, u32[]{:S(2)}) copy-start(f32[100,48]{0,1:T(8,128)} %param.29) | copy-start | bytes 57604
  399.3 18.3 %copy-start.25 = (f32[100,48]{0,1:T(8,128)S(1)}, f32[100,48]{0,1:T(8,128)}, u32[]{:S(2)}) copy-start(f32[100,48]{0,1:T(8,128)} %param.43) | copy-start | bytes 57604
  399.3 18.3 %copy-start.26 = (f32[100,48]{0,1:T(8,128)S(1)}, f32[100,48]{0,1:T(8,128)}, u32[]{:S(2)}) copy-start(f32[100,48]{0,1:T(8,128)} %param.36) | copy-start | bytes 57604
  399.3 7.0 %collective-permute-start.40 = (bf16[48,1920]{1,0:T(8,128)(2,1)S(1)}, bf16[48,1920]{1,0:T(8,128)(2,1)S(1)}, u32[]{:S(2)}, u32[]{:S(2)}) collective-permute-start(bf16[48,1920]{1,0:T(8,128)(2,1)S(1)} %get-tuple-element.265), channel_id=1, source_target_pairs={{0,16},{16,0},{1,17},{17,1},{2,18},{18,2},{3,19},{19,3},{4,20},{20... | collective-permute-start | bytes 552968 | tf_op jit(solution)/shard_map/ppermute | solution.py:206
  401.0 7.3 %collective-permute-start.38 = (bf16[48,640]{1,0:T(8,128)(2,1)S(1)}, bf16[48,640]{1,0:T(8,128)(2,1)S(1)}, u32[]{:S(2)}, u32[]{:S(2)}) collective-permute-start(bf16[48,640]{1,0:T(8,128)(2,1)S(1)} %get-tuple-element.269), channel_id=1, source_target_pairs={{0,16},{16,0},{1,17},{17,1},{2,18},{18,2},{3,19},{19,3},{4,20},{20... | collective-permute-start | bytes 184328 | tf_op jit(solution)/shard_map/ppermute | solution.py:206
  401.4 16.8 %copy-start.5 = (f32[48,2304]{1,0:T(8,128)S(1)}, f32[48,2304]{1,0:T(8,128)}, u32[]{:S(2)}) copy-start(f32[48,2304]{1,0:T(8,128)} %param.30) | copy-start | bytes 1327108
  401.4 16.8 %copy-start.19 = (f32[48,2304]{1,0:T(8,128)S(1)}, f32[48,2304]{1,0:T(8,128)}, u32[]{:S(2)}) copy-start(f32[48,2304]{1,0:T(8,128)} %param.44) | copy-start | bytes 1327108
  401.5 5.0 %collective-permute-start.35 = (f32[8,128]{1,0:T(8,128)S(1)}, f32[8,128]{1,0:T(8,128)S(1)}, u32[]{:S(2)}, u32[]{:S(2)}) collective-permute-start(f32[8,128]{1,0:T(8,128)S(1)} %fusion.46), channel_id=1, source_target_pairs={{0,4},{1,5},{2,6},{3,7},{4,0},{5,1},{6,2},{7,3},{8,12},{9,13},{10,... | collective-permute-start | bytes 12296 | tf_op jit(solution)/shard_map/ppermute | solution.py:207
  406.5 3.7 collective-permute-start.36
  410.1 3.6 collective-permute-start.37
  (18 other events, 47.2 us)
Sparse Core Ops, SparseCore 0:
  15.0 94.1 all-gather.2
  112.1 58.3 all-gather.4
  204.5 127.8 reduce-scatter.1

commit v4 on v3

--- a/solution.py
+++ b/solution.py
@@ -1192,7 +1192,7 @@
     gather_h = Group(x_last, rows, [((bins - plain) // 2, 1)], count_fsdp)
     groups_b = [
         Group(x_last, rows, [(half, 1), (hidden_half, 1)], count_fsdp),
-        Group(y_last, down_weight.shape[0], [(half, 1)], count_fsdp),
+        Group(x_last, down_weight.shape[0], [(half, 1)], count_fsdp),
     ]
 
     def side_of(weight, width):

time: 441 us -> 429 us (0.973)
  waiting for transfers between devices: 127 us -> 113 us
    ppermute x14, waiting for transfers between devices: 41.6 us -> 29.4 us  [swap(): return lax.ppermute(value, 'tab', [(0, 1), (1, 0)])]
  transfers between devices with their start and end apart: 45 -> 45, of which waited for: 26 -> 25; matrix products, arithmetic and copies ran while one was open for 7% -> 7% of each run, Pallas kernels for 29% -> 30%
where the time goes in v4:
time: 429 us; the launch traced here: 424 us
  Pallas kernels  162 us (38%)
  waiting for transfers between devices  113 us (26%)
  starting transfers between devices  74.8 us (17%)
  other arithmetic  37.9 us (9%)
  between operations  24.2 us (6%)
  local copies, waits for them, and re-layouts  12.6 us (3%)
    ppermute x28, waiting for transfers between devices, swap(): return lax.ppermute(value, 'fsdp', [(i, i ^ step) for i in range(count)])  80.3 us
    ppermute x28, starting transfers between devices, swap(): return lax.ppermute(value, 'fsdp', [(i, i ^ step) for i in range(count)])  59.1 us
    ppermute x14, waiting for transfers between devices, swap(): return lax.ppermute(value, 'tab', [(0, 1), (1, 0)])  29.4 us
    pallas_call x1, Pallas kernels, project_back_call(): pl.pallas_call(functools.partial(project_back, groups, blocks_q), grid_sp...  25.1 us
    pallas_call x1, Pallas kernels, head_call(): pl.pallas_call(functools.partial(head, group), out_shape=(shape((model, b...  24.1 us
    pallas_call x1, Pallas kernels, feed_back_call(): pl.pallas_call(functools.partial(feed_back, down_group, group), grid_spec...  23.8 us
    pallas_call x1, Pallas kernels, attend_back_call(): pl.pallas_call(functools.partial(attend_back, size), grid_spec=pltpu.Pref...  21.7 us
    pallas_call x1, Pallas kernels, feed_call(): pl.pallas_call(functools.partial(feed, down_group), grid_spec=pltpu.Prefe...  18.6 us
  transfers between devices with their start and end apart: 45, of which 25 were waited for; matrix products, arithmetic and copies ran while one was open for 7% of the time, Pallas kernels for 30%

profile of v4, /device:TPU:0, one launch (start us, length us, event | category | flops | bytes accessed | tf_op | source)
XLA Modules:
  0.0 423.7 jit_solution(16159118714223200934)
XLA Ops:
  7.3 1.4 fusion.45
  15.7 4.0 collective-permute-start.1
  21.6 1.6 collective-permute-start
  24.5 2.2 collective-permute-done.1
  27.5 1.9 collective-permute-done
  32.7 16.9 %collective-permute-done.2 = bf16[2,192,384]{2,1,0:T(8,128)(2,1)S(1)} collective-permute-done((bf16[2,192,384]{2,1,0:T(8,128)(2,1)S(1)}, bf16[2,192,384]{2,1,0:T(8,128)(2,1)S(1)}, u32[]{:S(2)}, u32[]{:S(2)}) %collective-permute-start.2) | collective-permute-done | bytes 294944 | tf_op jit(solution)/shard_map/ppermute | solution.py:207
  49.7 1.3 collective-permute-start.3
  51.0 8.3 %sort_rows.1 = (bf16[1024,128]{1,0:T(8,128)(2,1)}, f32[1024,128]{1,0:T(8,128)}, bf16[2048,128]{1,0:T(8,128)(2,1)}, f32[2048,128]{1,0:T(8,128)}) custom-call(s32[8]{0:T(128)} %stack.44.count, bf16[2048,128]{1,0:T(8,128)(2,1)} %pad_maximum_fusion.1.table, f32[16,128]{1,0:T(8,128)} %bitcast.76), custom_call_target="tpu_custom_call" | custom-call | flops 7000000000 | bytes 1048576 | tf_op jit(solution)/shard_map/sort_rows/pallas_call | solution.py:279
  59.4 3.0 collective-permute-done.3
  63.0 7.2 %collective-permute-start.6 = (bf16[1,48,768]{2,1,0:T(8,128)(2,1)S(1)}, bf16[1,48,768]{2,1,0:T(8,128)(2,1)S(1)}, u32[]{:S(2)}, u32[]{:S(2)}) collective-permute-start(bf16[1,48,768]{2,1,0:T(8,128)(2,1)S(1)} %get-tuple-element.271), channel_id=1, source_target_pairs={{0,8},{1,9},{2,10},{3,11},{4,12},{5,13},{6,14},{7,15},{8,0},{9,1},... | collective-permute-start | bytes 221192 | tf_op jit(solution)/shard_map/ppermute | solution.py:207
  70.2 8.2 %collective-permute-done.6 = bf16[1,48,768]{2,1,0:T(8,128)(2,1)S(1)} collective-permute-done((bf16[1,48,768]{2,1,0:T(8,128)(2,1)S(1)}, bf16[1,48,768]{2,1,0:T(8,128)(2,1)S(1)}, u32[]{:S(2)}, u32[]{:S(2)}) %collective-permute-start.6) | collective-permute-done | bytes 73760 | tf_op jit(solution)/shard_map/ppermute | solution.py:207
  78.4 2.3 collective-permute-start.7
  81.0 6.1 %collective-permute-done.4 = bf16[8,192,384]{2,1,0:T(8,128)(2,1)S(1)} collective-permute-done((bf16[8,192,384]{2,1,0:T(8,128)(2,1)S(1)}, bf16[8,192,384]{2,1,0:T(8,128)(2,1)S(1)}, u32[]{:S(2)}, u32[]{:S(2)}) %collective-permute-start.4) | collective-permute-done | bytes 1179680 | tf_op jit(solution)/shard_map/ppermute | solution.py:206
  87.4 6.4 %collective-permute-done.7 = bf16[2,48,768]{2,1,0:T(8,128)(2,1)S(1)} collective-permute-done((bf16[2,48,768]{2,1,0:T(8,128)(2,1)S(1)}, bf16[2,48,768]{2,1,0:T(8,128)(2,1)S(1)}, u32[]{:S(2)}, u32[]{:S(2)}) %collective-permute-start.7) | collective-permute-done | bytes 147488 | tf_op jit(solution)/shard_map/ppermute | solution.py:207
  93.8 1.7 collective-permute-start.8
  95.5 5.1 %collective-permute-done.8 = bf16[4,48,768]{2,1,0:T(8,128)(2,1)S(1)} collective-permute-done((bf16[4,48,768]{2,1,0:T(8,128)(2,1)S(1)}, bf16[4,48,768]{2,1,0:T(8,128)(2,1)S(1)}, u32[]{:S(2)}, u32[]{:S(2)}) %collective-permute-start.8) | collective-permute-done | bytes 294944 | tf_op jit(solution)/shard_map/ppermute | solution.py:207
  101.9 10.4 %collective-permute-done.9 = bf16[8,48,768]{2,1,0:T(8,128)(2,1)S(1)} collective-permute-done((bf16[8,48,768]{2,1,0:T(8,128)(2,1)S(1)}, bf16[8,48,768]{2,1,0:T(8,128)(2,1)S(1)}, u32[]{:S(2)}, u32[]{:S(2)}) %collective-permute-start.9) | collective-permute-done | bytes 589856 | tf_op jit(solution)/shard_map/ppermute | solution.py:206
  112.4 2.8 collective-permute-done.10.rest_1_
  115.3 15.9 %project.1 = (bf16[1024,768]{1,0:T(8,128)(2,1)}, bf16[2048,768]{1,0:T(8,128)(2,1)}, bf16[2048,768]{1,0:T(8,128)(2,1)}, bf16[1024,768]{1,0:T(8,128)(2,1)}, bf16[2...) custom-call(s32[8]{0:T(128)} %stack.44.count, bf16[1024,128]{1,0:T(8,128)(2,1)} %get-tuple-element.83.x_query.xq, ...), custom_call_target="tpu_custom_call" | custom-call | flops 12000000000 | bytes 1048576 | tf_op jit(solution)/shard_map/project/pallas_call | solution.py:340
  133.1 14.7 %attend.1 = (bf16[1024,768]{1,0:T(8,128)(2,1)}, f32[6,8,1024]{2,1,0:T(8,128)}) custom-call(s32[8]{0:T(128)} %stack.44.count, bf16[1024,768]{1,0:T(8,128)(2,1)} %get-tuple-element.86.q_ref, bf16[2048,768]{1,0:T(8,128)(2,1)} %get-tuple-element.87.k_ref, bf16[2048,768]{1,0:T(8,128)(2,1)} %get-tuple-element.88.v_ref), custom_call_target="tpu_custom_call" | custom-call | flops 35000000512 | bytes 1048576 | tf_op jit(solution)/shard_map/attend/pallas_call | solution.py:452
  147.8 18.6 %feed.1 = (f32[1024,768]{1,0:T(8,128)}, bf16[1024,768]{1,0:T(8,128)(2,1)}, bf16[1024,3072]{1,0:T(8,128)(2,1)}, bf16[1024,3072]{1,0:T(8,128)(2,1)}, f32[1024,768]...) custom-call(s32[8]{0:T(128)} %stack.44.count, bf16[1024,768]{1,0:T(8,128)(2,1)} %get-tuple-element.89.o_ref.o_any, ...), custom_call_target="tpu_custom_call" | custom-call | flops 20000000000 | bytes 1048576 | tf_op jit(solution)/shard_map/feed/pallas_call | solution.py:640
  167.6 2.9 all-gather.5.cloned.1.call-done.weight_any
  170.5 24.1 %head.1 = (bf16[768,5120]{1,0:T(8,128)(2,1)}, f32[1024,768]{1,0:T(8,128)}, f32[8,128]{1,0:T(8,128)}) custom-call(s32[8]{0:T(128)} %stack.44.count, bf16[1024,768]{1,0:T(8,128)(2,1)} %get-tuple-element.92.f_ref, f32[1024,128]{1,0:T(8,128)} %get-tuple-element.93.t_ref, f32[1,128]{1,0:T(1,128)} %slice_add_fusion.rows_all, ...), custom_call_target="tpu_custom_call" | custom-call | flops 35000000512 | bytes 1048576 | tf_op jit(solution)/shard_map/head/pallas_call | solution.py:779
  194.5 9.5 %down_back.1 = (bf16[16,192,384]{2,1,0:T(8,128)(2,1)}, bf16[16,192,384]{2,1,0:T(8,128)(2,1)}, f32[1024,768]{1,0:T(8,128)}, bf16[1024,768]{1,0:T(8,128)(2,1)}, f32[8,768]{1,0:T(8,128)}) custom-call(s32[8]{0:T(128)} %stack.44.count, f32[1024,768]{1,0:T(8,128)} %get-tuple-element.97.df_any, f32[1024,768]{1,0:T(8,128)} %get-tuple-element.98.h2_any, ...), custom_call_target="tpu_custom_call" | custom-call | flops 10000000000 | bytes 1048576 | tf_op jit(solution)/shard_map/down_back/pallas_call | solution.py:865
  204.4 23.8 %feed_back.1 = (bf16[16,48,1920]{2,1,0:T(8,128)(2,1)}, bf16[16,48,1920]{2,1,0:T(8,128)(2,1)}, f32[1024,768]{1,0:T(8,128)}, bf16[1024,768]{1,0:T(8,128)(2,1)}, f32[8,768]{1,0:T(8,128)}) custom-call(s32[8]{0:T(128)} %stack.44.count, f32[1024,768]{1,0:T(8,128)} %get-tuple-element.100.dh2_ref, bf16[1024,768]{1,0:T(8,128)(2,1)} %get-tuple-element.101.dm_ref, ...), custom_call_target="tpu_custom_call" | custom-call | flops 24999999488 | bytes 1048576 | tf_op jit(solution)/shard_map/feed_back/pallas_call | solution.py:988
  228.5 1.4 copy-done.2
  229.9 4.2 add_convert_fusion.2
  234.1 1.6 collective-permute-start.14
  235.7 21.7 %attend_back.1 = (bf16[1024,768]{1,0:T(8,128)(2,1)}, bf16[2048,768]{1,0:T(8,128)(2,1)}, bf16[2048,768]{1,0:T(8,128)(2,1)}) custom-call(s32[8]{0:T(128)} %stack.44.count, bf16[1024,768]{1,0:T(8,128)(2,1)} %get-tuple-element.86.q_ref, bf16[2048,768]{1,0:T(8,128)(2,1)} %get-tuple-element.87.k_ref, bf16[2048,768]{1,0:T(8,128)(2,1)} %get-tuple-element.88.v_ref, ...), custom_call_target="tpu_custom_call" | custom-call | flops 35000000512 | bytes 1048576 | tf_op jit(solution)/shard_map/attend_back/pallas_call | solution.py:531
  257.4 4.5 %add_convert_fusion = (bf16[8,48,1920]{2,1,0:T(8,128)(2,1)}, bf16[8,48,1920]{2,1,0:T(8,128)(2,1)S(1)}) fusion(bf16[16,48,1920]{2,1,0:T(8,128)(2,1)} %collective-permute-done.13, bf16[16,48,1920]{2,1,0:T(8,128)(2,1)} %get-tuple-element.116), kind=kLoop, calls=%fused_computation | loop fusion | flops 5898240 | bytes 8847360 | tf_op jit(solution)/shard_map/convert_element_type | solution.py:227
  262.6 2.3 add_convert_fusion.6
  264.9 25.1 %project_back.1 = (bf16[16,48,640]{2,1,0:T(8,128)(2,1)}, bf16[16,48,640]{2,1,0:T(8,128)(2,1)}, bf16[16,48,640]{2,1,0:T(8,128)(2,1)}, bf16[16,48,640]{2,1,0:T(8,128)(2,1)}) custom-call(s32[8]{0:T(128)} %stack.44.count, bf16[1024,768]{1,0:T(8,128)(2,1)} %get-tuple-element.120.dq, bf16[1024,768]{1,0:T(8,128)(2,1)} %get-tuple-element.121.aq, ...), custom_call_target="tpu_custom_call" | custom-call | flops 20000000000 | bytes 1048576 | tf_op jit(solution)/shard_map/project_back/pallas_call | solution.py:1098
  292.7 17.4 %collective-permute-done.27 = bf16[4,192,384]{2,1,0:T(8,128)(2,1)S(1)} collective-permute-done((bf16[4,192,384]{2,1,0:T(8,128)(2,1)S(1)}, bf16[4,192,384]{2,1,0:T(8,128)(2,1)S(1)}, u32[]{:S(2)}, u32[]{:S(2)}) %collective-permute-start.27) | collective-permute-done | bytes 589856 | tf_op jit(solution)/shard_map/ppermute | solution.py:207
  310.3 1.6 collective-permute-start.31
  311.8 1.4 add_convert_fusion.9
  313.9 1.4 add_convert_fusion.11
  315.3 1.5 collective-permute-start.16
  316.9 2.3 collective-permute-done.31
  319.2 10.6 %collective-permute-start.32 = (bf16[1,192,384]{2,1,0:T(8,128)(2,1)S(1)}, bf16[1,192,384]{2,1,0:T(8,128)(2,1)S(1)}, u32[]{:S(2)}, u32[]{:S(2)}) collective-permute-start(bf16[1,192,384]{2,1,0:T(8,128)(2,1)S(1)} %add_convert_fusion.24), channel_id=1, source_target_pairs={{0,8},{1,9},{2,10},{3,11},{4,12},{5,13},{6,14},{7,15},{8,0},{9,1},... | collective-permute-start | bytes 442376 | tf_op jit(solution)/shard_map/ppermute | solution.py:207
  330.2 1.7 add_convert_fusion.5
  331.9 1.5 collective-permute-start.28
  333.4 2.6 collective-permute-done.32
  338.3 1.7 collective-permute-start.17
  340.0 2.0 collective-permute-done.24
  342.0 9.6 %collective-permute-start.25 = (bf16[1,48,640]{2,1,0:T(8,128)(2,1)S(1)}, bf16[1,48,640]{2,1,0:T(8,128)(2,1)S(1)}, u32[]{:S(2)}, u32[]{:S(2)}) collective-permute-start(bf16[1,48,640]{2,1,0:T(8,128)(2,1)S(1)} %add_convert_fusion.31), channel_id=1, source_target_pairs={{0,8},{1,9},{2,10},{3,11},{4,12},{5,13},{6,14},{7,15},{8,0},{9,1},... | collective-permute-start | bytes 184328 | tf_op jit(solution)/shard_map/ppermute | solution.py:207
  351.8 1.5 collective-permute-start.29
  355.8 4.5 %collective-permute-done.29 = bf16[2,48,1920]{2,1,0:T(8,128)(2,1)S(1)} collective-permute-done((bf16[2,48,1920]{2,1,0:T(8,128)(2,1)S(1)}, bf16[2,48,1920]{2,1,0:T(8,128)(2,1)S(1)}, u32[]{:S(2)}, u32[]{:S(2)}) %collective-permute-start.29) | collective-permute-done | bytes 368672 | tf_op jit(solution)/shard_map/ppermute | solution.py:207
  360.3 8.7 %collective-permute-start.30 = (bf16[1,48,1920]{2,1,0:T(8,128)(2,1)S(1)}, bf16[1,48,1920]{2,1,0:T(8,128)(2,1)S(1)}, u32[]{:S(2)}, u32[]{:S(2)}) collective-permute-start(bf16[1,48,1920]{2,1,0:T(8,128)(2,1)S(1)} %add_convert_fusion.21), channel_id=1, source_target_pairs={{0,8},{1,9},{2,10},{3,11},{4,12},{5,13},{6,14},{7,15},{8,0},{9,1},... | collective-permute-start | bytes 552968 | tf_op jit(solution)/shard_map/ppermute | solution.py:207
  369.0 1.7 collective-permute-start.18
  370.8 2.8 collective-permute-done.30
  374.3 1.6 collective-permute-done.20
  376.5 1.5 collective-permute-done.18
  383.0 1.7 collective-permute-start.39
  384.8 2.6 collective-permute-done.39
  387.5 1.7 collective-permute-start.40
  389.7 4.8 %collective-permute-done.40 = bf16[48,1920]{1,0:T(8,128)(2,1)S(1)} collective-permute-done((bf16[48,1920]{1,0:T(8,128)(2,1)S(1)}, bf16[48,1920]{1,0:T(8,128)(2,1)S(1)}, u32[]{:S(2)}, u32[]{:S(2)}) %collective-permute-start.40) | collective-permute-done | bytes 184352 | tf_op jit(solution)/shard_map/ppermute | solution.py:206
  394.6 1.8 collective-permute-start.36
  396.5 1.8 collective-permute-done.36
  398.3 1.7 collective-permute-start.37
  400.0 1.9 collective-permute-done.37
  406.4 2.3 add_multiply_fusion.3
  408.8 1.4 add_multiply_fusion.1
  410.9 1.4 add_multiply_fusion.2
  413.7 1.9 add_multiply_fusion
  (214 shorter events, 36.0 us)
Async XLA Ops:
  7.2 6.3 %copy-start.13 = (f32[48,768]{1,0:T(8,128)S(1)}, f32[48,768]{1,0:T(8,128)}, u32[]{:S(2)}) copy-start(f32[48,768]{1,0:T(8,128)} %param.31) | copy-start | bytes 442372
  7.2 6.4 %copy-start.29 = (f32[4,48]{1,0:T(4,128)S(1)}, f32[4,48]{1,0:T(4,128)}, u32[]{:S(2)}) copy-start(f32[4,48]{1,0:T(4,128)} %param.35) | copy-start | bytes 2308
  7.2 6.5 %copy-start.23 = (f32[100,48]{0,1:T(8,128)S(1)}, f32[100,48]{0,1:T(8,128)}, u32[]{:S(2)}) copy-start(f32[100,48]{0,1:T(8,128)} %param.29) | copy-start | bytes 57604
  7.2 108.1 %all-gather.3.cloned.1.call-start = ((), (), s32[]{:S(2)}) async-start(), calls=%async_computation.1 | async-start | bytes 10444800 | tf_op jit(solution)/shard_map/all_gather | solution.py:1218
  14.9 155.6 %all-gather.5.cloned.1.call-start = ((), (), s32[]{:S(2)}) async-start(), calls=%async_computation.2 | async-start | bytes 5849088 | tf_op jit(solution)/shard_map/all_gather | solution.py:1251
  15.7 11.0 %collective-permute-start.1 = (bf16[1,192,384]{2,1,0:T(8,128)(2,1)S(1)}, bf16[1,192,384]{2,1,0:T(8,128)(2,1)S(1)}, u32[]{:S(2)}, u32[]{:S(2)}) collective-permute-start(bf16[1,192,384]{2,1,0:T(8,128)(2,1)S(1)} %get-tuple-element.273), channel_id=1, source_target_pairs={{0,8},{1,9},{2,10},{3,11},{4,12},{5,13},{6,14},{7,15},{8,0},{9,1},... | collective-permute-start | bytes 442376 | tf_op jit(solution)/shard_map/ppermute | solution.py:207
  21.6 7.8 %collective-permute-start = (bf16[1024,128]{1,0:T(8,128)(2,1)S(1)}, bf16[1024,128]{1,0:T(8,128)(2,1)S(1)}, u32[]{:S(2)}, u32[]{:S(2)}) collective-permute-start(bf16[1024,128]{1,0:T(8,128)(2,1)S(1)} %concatenate.60), channel_id=1, source_target_pairs={{0,16},{16,0},{1,17},{17,1},{2,18},{18,2},{3,19},{19,3},{4,20},{20... | collective-permute-start | bytes 786440 | tf_op jit(solution)/shard_map/ppermute | solution.py:206
  26.7 22.9 %collective-permute-start.2 = (bf16[2,192,384]{2,1,0:T(8,128)(2,1)S(1)}, bf16[2,192,384]{2,1,0:T(8,128)(2,1)S(1)}, u32[]{:S(2)}, u32[]{:S(2)}) collective-permute-start(bf16[2,192,384]{2,1,0:T(8,128)(2,1)S(1)} %pad_maximum_fusion.4), channel_id=1, source_target_pairs={{0,4},{1,5},{2,6},{3,7},{4,0},{5,1},{6,2},{7,3},{8,12},{9,13},{10,... | collective-permute-start | bytes 884744 | tf_op jit(solution)/shard_map/ppermute | solution.py:207
  49.7 12.8 %collective-permute-start.3 = (bf16[4,192,384]{2,1,0:T(8,128)(2,1)S(1)}, bf16[4,192,384]{2,1,0:T(8,128)(2,1)S(1)}, u32[]{:S(2)}, u32[]{:S(2)}) collective-permute-start(bf16[4,192,384]{2,1,0:T(8,128)(2,1)S(1)} %pad_maximum_fusion.2), channel_id=1, source_target_pairs={{0,2},{1,3},{2,0},{3,1},{4,6},{5,7},{6,4},{7,5},{8,10},{9,11},{10,... | collective-permute-start | bytes 1769480 | tf_op jit(solution)/shard_map/ppermute | solution.py:207
  59.3 295.4 %reduce-scatter.2.cloned.1.call-start = ((), (), s32[]{:S(2)}) async-start(), calls=%async_computation.3 | async-start | bytes 8355840 | tf_op jit(solution)/shard_map/reduce_scatter | solution.py:1273
  59.4 21.4 %copy-start.27 = (bf16[16,192,384]{2,1,0:T(8,128)(2,1)S(1)}, bf16[16,192,384]{2,1,0:T(8,128)(2,1)}, u32[]{:S(2)}) copy-start(bf16[16,192,384]{2,1,0:T(8,128)(2,1)} %get-tuple-element.272) | copy-start | bytes 7077892
  62.6 24.5 %collective-permute-start.4 = (bf16[8,192,384]{2,1,0:T(8,128)(2,1)S(1)}, bf16[8,192,384]{2,1,0:T(8,128)(2,1)S(1)}, u32[]{:S(2)}, u32[]{:S(2)}) collective-permute-start(bf16[8,192,384]{2,1,0:T(8,128)(2,1)S(1)} %pad_maximum_fusion), channel_id=1, source_target_pairs={{0,16},{16,0},{1,17},{17,1},{2,18},{18,2},{3,19},{19,3},{4,20},{20... | collective-permute-start | bytes 3538952 | tf_op jit(solution)/shard_map/ppermute | solution.py:206
  63.0 15.4 %collective-permute-start.6 = (bf16[1,48,768]{2,1,0:T(8,128)(2,1)S(1)}, bf16[1,48,768]{2,1,0:T(8,128)(2,1)S(1)}, u32[]{:S(2)}, u32[]{:S(2)}) collective-permute-start(bf16[1,48,768]{2,1,0:T(8,128)(2,1)S(1)} %get-tuple-element.271), channel_id=1, source_target_pairs={{0,8},{1,9},{2,10},{3,11},{4,12},{5,13},{6,14},{7,15},{8,0},{9,1},... | collective-permute-start | bytes 221192 | tf_op jit(solution)/shard_map/ppermute | solution.py:207
  78.4 15.4 %collective-permute-start.7 = (bf16[2,48,768]{2,1,0:T(8,128)(2,1)S(1)}, bf16[2,48,768]{2,1,0:T(8,128)(2,1)S(1)}, u32[]{:S(2)}, u32[]{:S(2)}) collective-permute-start(bf16[2,48,768]{2,1,0:T(8,128)(2,1)S(1)} %pad_maximum_fusion.8), channel_id=1, source_target_pairs={{0,4},{1,5},{2,6},{3,7},{4,0},{5,1},{6,2},{7,3},{8,12},{9,13},{10,... | collective-permute-start | bytes 442376 | tf_op jit(solution)/shard_map/ppermute | solution.py:207
  87.3 25.0 %copy-start.28 = (bf16[16,192,384]{2,1,0:T(8,128)(2,1)}, bf16[16,192,384]{2,1,0:T(8,128)(2,1)S(1)}, u32[]{:S(2)}) copy-start(bf16[16,192,384]{2,1,0:T(8,128)(2,1)S(1)} %constant_dynamic-update-slice_fusion.rest_1_) | copy-start | bytes 7077892
  87.3 28.0 %collective-permute-start.5 = (bf16[16,192,384]{2,1,0:T(8,128)(2,1)S(1)}, bf16[16,192,384]{2,1,0:T(8,128)(2,1)}, u32[]{:S(2)}, u32[]{:S(2)}) collective-permute-start(bf16[16,192,384]{2,1,0:T(8,128)(2,1)S(1)} %constant_dynamic-update-slice_fusion.rest_1_), channel_id=1, source_target_pairs={{0,1},{1,0},{2,3},{3,2},{4,5},{5,4},{6,7},{7,6},{8,9},{9,8},{10,11... | collective-permute-start | bytes 7077896 | tf_op jit(solution)/shard_map/ppermute | solution.py:207
  93.8 6.8 %collective-permute-start.8 = (bf16[4,48,768]{2,1,0:T(8,128)(2,1)S(1)}, bf16[4,48,768]{2,1,0:T(8,128)(2,1)S(1)}, u32[]{:S(2)}, u32[]{:S(2)}) collective-permute-start(bf16[4,48,768]{2,1,0:T(8,128)(2,1)S(1)} %pad_maximum_fusion.5), channel_id=1, source_target_pairs={{0,2},{1,3},{2,0},{3,1},{4,6},{5,7},{6,4},{7,5},{8,10},{9,11},{10,... | collective-permute-start | bytes 884744 | tf_op jit(solution)/shard_map/ppermute | solution.py:207
  100.7 11.6 %collective-permute-start.9 = (bf16[8,48,768]{2,1,0:T(8,128)(2,1)S(1)}, bf16[8,48,768]{2,1,0:T(8,128)(2,1)S(1)}, u32[]{:S(2)}, u32[]{:S(2)}) collective-permute-start(bf16[8,48,768]{2,1,0:T(8,128)(2,1)S(1)} %pad_maximum_fusion.3), channel_id=1, source_target_pairs={{0,16},{16,0},{1,17},{17,1},{2,18},{18,2},{3,19},{19,3},{4,20},{20... | collective-permute-start | bytes 1769480 | tf_op jit(solution)/shard_map/ppermute | solution.py:206
  112.4 18.9 %copy-start.31 = (bf16[16,48,768]{2,1,0:T(8,128)(2,1)}, bf16[16,48,768]{2,1,0:T(8,128)(2,1)S(1)}, u32[]{:S(2)}) copy-start(bf16[16,48,768]{2,1,0:T(8,128)(2,1)S(1)} %constant_dynamic-update-slice_fusion.5.rest_0_) | copy-start | bytes 3538948
  112.4 2.9 collective-permute-start.10
  115.3 15.9 %copy-start.36 = (bf16[16,48,768]{2,1,0:T(8,128)(2,1)}, bf16[16,48,768]{2,1,0:T(8,128)(2,1)S(1)}, u32[]{:S(2)}) copy-start(bf16[16,48,768]{2,1,0:T(8,128)(2,1)S(1)} %collective-permute-done.10.rest_1_) | copy-start | bytes 3538948
  131.9 34.4 %collective-permute-start.11 = (f32[1,128]{1,0:T(1,128)S(1)}, f32[1,128]{1,0:T(1,128)S(1)}, u32[]{:S(2)}, u32[]{:S(2)}) collective-permute-start(f32[1,128]{1,0:T(1,128)S(1)} %slice.267), channel_id=1, source_target_pairs={{0,16},{16,0},{1,17},{17,1},{2,18},{18,2},{3,19},{19,3},{4,20},{20... | collective-permute-start | bytes 1544 | tf_op jit(solution)/shard_map/ppermute | solution.py:206
  204.0 24.4 %collective-permute-start.12 = (bf16[16,192,384]{2,1,0:T(8,128)(2,1)}, bf16[16,192,384]{2,1,0:T(8,128)(2,1)S(1)}, u32[]{:S(2)}, u32[]{:S(2)}) collective-permute-start(bf16[16,192,384]{2,1,0:T(8,128)(2,1)} %get-tuple-element.108), channel_id=1, source_target_pairs={{0,1},{1,0},{2,3},{3,2},{4,5},{5,4},{6,7},{7,6},{8,9},{9,8},{10,11... | collective-permute-start | bytes 7077896 | tf_op jit(solution)/shard_map/ppermute | solution.py:207
  228.2 29.2 %collective-permute-start.13 = (bf16[16,48,1920]{2,1,0:T(8,128)(2,1)}, bf16[16,48,1920]{2,1,0:T(8,128)(2,1)}, u32[]{:S(2)}, u32[]{:S(2)}) collective-permute-start(bf16[16,48,1920]{2,1,0:T(8,128)(2,1)} %get-tuple-element.115), channel_id=1, source_target_pairs={{0,1},{1,0},{2,3},{3,2},{4,5},{5,4},{6,7},{7,6},{8,9},{9,8},{10,11... | collective-permute-start | bytes 8847368 | tf_op jit(solution)/shard_map/ppermute | solution.py:207
  234.1 28.5 %collective-permute-start.14 = (bf16[8,192,384]{2,1,0:T(8,128)(2,1)}, bf16[8,192,384]{2,1,0:T(8,128)(2,1)}, u32[]{:S(2)}, u32[]{:S(2)}) collective-permute-start(bf16[8,192,384]{2,1,0:T(8,128)(2,1)} %get-tuple-element.276), channel_id=1, source_target_pairs={{0,16},{16,0},{1,17},{17,1},{2,18},{18,2},{3,19},{19,3},{4,20},{20... | collective-permute-start | bytes 3538952 | tf_op jit(solution)/shard_map/ppermute | solution.py:206
  261.9 48.2 %collective-permute-start.26 = (bf16[8,48,1920]{2,1,0:T(8,128)(2,1)}, bf16[8,48,1920]{2,1,0:T(8,128)(2,1)}, u32[]{:S(2)}, u32[]{:S(2)}) collective-permute-start(bf16[8,48,1920]{2,1,0:T(8,128)(2,1)} %get-tuple-element.274), channel_id=1, source_target_pairs={{0,16},{16,0},{1,17},{17,1},{2,18},{18,2},{3,19},{19,3},{4,20},{20... | collective-permute-start | bytes 4423688 | tf_op jit(solution)/shard_map/ppermute | solution.py:206
  264.9 25.2 %copy-start.12 = (bf16[4,192,384]{2,1,0:T(8,128)(2,1)S(1)}, bf16[4,192,384]{2,1,0:T(8,128)(2,1)}, u32[]{:S(2)}) copy-start(bf16[4,192,384]{2,1,0:T(8,128)(2,1)} %get-tuple-element.280) | copy-start | bytes 1769476
  264.9 26.1 %copy-start.30 = (f32[4,48]{1,0:T(4,128)S(1)}, f32[4,48]{1,0:T(4,128)}, u32[]{:S(2)}) copy-start(f32[4,48]{1,0:T(4,128)} %param.35) | copy-start | bytes 2308
  264.9 26.2 %copy-start.33 = (f32[4,48]{1,0:T(4,128)S(1)}, f32[4,48]{1,0:T(4,128)}, u32[]{:S(2)}) copy-start(f32[4,48]{1,0:T(4,128)} %param.42) | copy-start | bytes 2308
  264.9 26.3 %copy-start.34 = (f32[4,48]{1,0:T(4,128)S(1)}, f32[4,48]{1,0:T(4,128)}, u32[]{:S(2)}) copy-start(f32[4,48]{1,0:T(4,128)} %param.49) | copy-start | bytes 2308
  264.9 26.4 %copy-start.35 = (f32[8,128]{1,0:T(8,128)S(1)}, f32[8,128]{1,0:T(8,128)}, u32[]{:S(2)}) copy-start(f32[8,128]{1,0:T(8,128)} %get-tuple-element.96) | copy-start | bytes 12292
  290.0 21.8 %collective-permute-start.21 = (bf16[16,48,640]{2,1,0:T(8,128)(2,1)}, bf16[16,48,640]{2,1,0:T(8,128)(2,1)}, u32[]{:S(2)}, u32[]{:S(2)}) collective-permute-start(bf16[16,48,640]{2,1,0:T(8,128)(2,1)} %get-tuple-element.134), channel_id=1, source_target_pairs={{0,1},{1,0},{2,3},{3,2},{4,5},{5,4},{6,7},{7,6},{8,9},{9,8},{10,11... | collective-permute-start | bytes 2949128 | tf_op jit(solution)/shard_map/ppermute | solution.py:207
  290.1 20.0 %collective-permute-start.27 = (bf16[4,192,384]{2,1,0:T(8,128)(2,1)S(1)}, bf16[4,192,384]{2,1,0:T(8,128)(2,1)S(1)}, u32[]{:S(2)}, u32[]{:S(2)}) collective-permute-start(bf16[4,192,384]{2,1,0:T(8,128)(2,1)S(1)} %copy-done.12), channel_id=1, source_target_pairs={{0,2},{1,3},{2,0},{3,1},{4,6},{5,7},{6,4},{7,5},{8,10},{9,11},{10,... | collective-permute-start | bytes 1769480 | tf_op jit(solution)/shard_map/ppermute | solution.py:207
  290.9 23.0 %collective-permute-start.15 = (bf16[16,48,640]{2,1,0:T(8,128)(2,1)}, bf16[16,48,640]{2,1,0:T(8,128)(2,1)}, u32[]{:S(2)}, u32[]{:S(2)}) collective-permute-start(bf16[16,48,640]{2,1,0:T(8,128)(2,1)} %get-tuple-element.128), channel_id=1, source_target_pairs={{0,1},{1,0},{2,3},{3,2},{4,5},{5,4},{6,7},{7,6},{8,9},{9,8},{10,11... | collective-permute-start | bytes 2949128 | tf_op jit(solution)/shard_map/ppermute | solution.py:207
  291.5 20.4 %copy-start.11 = (bf16[16,48,640]{2,1,0:T(8,128)(2,1)S(1)}, bf16[16,48,640]{2,1,0:T(8,128)(2,1)}, u32[]{:S(2)}) copy-start(bf16[16,48,640]{2,1,0:T(8,128)(2,1)} %get-tuple-element.133) | copy-start | bytes 2949124
  310.3 8.9 %collective-permute-start.31 = (bf16[2,192,384]{2,1,0:T(8,128)(2,1)S(1)}, bf16[2,192,384]{2,1,0:T(8,128)(2,1)S(1)}, u32[]{:S(2)}, u32[]{:S(2)}) collective-permute-start(bf16[2,192,384]{2,1,0:T(8,128)(2,1)S(1)} %get-tuple-element.289), channel_id=1, source_target_pairs={{0,4},{1,5},{2,6},{3,7},{4,0},{5,1},{6,2},{7,3},{8,12},{9,13},{10,... | collective-permute-start | bytes 884744 | tf_op jit(solution)/shard_map/ppermute | solution.py:207
  313.3 16.5 %collective-permute-start.22 = (bf16[8,48,640]{2,1,0:T(8,128)(2,1)S(1)}, bf16[8,48,640]{2,1,0:T(8,128)(2,1)S(1)}, u32[]{:S(2)}, u32[]{:S(2)}) collective-permute-start(bf16[8,48,640]{2,1,0:T(8,128)(2,1)S(1)} %get-tuple-element.283), channel_id=1, source_target_pairs={{0,2},{1,3},{2,0},{3,1},{4,6},{5,7},{6,4},{7,5},{8,10},{9,11},{10,... | collective-permute-start | bytes 1474568 | tf_op jit(solution)/shard_map/ppermute | solution.py:207
  315.3 22.9 %collective-permute-start.16 = (bf16[8,48,640]{2,1,0:T(8,128)(2,1)S(1)}, bf16[8,48,640]{2,1,0:T(8,128)(2,1)S(1)}, u32[]{:S(2)}, u32[]{:S(2)}) collective-permute-start(bf16[8,48,640]{2,1,0:T(8,128)(2,1)S(1)} %get-tuple-element.285), channel_id=1, source_target_pairs={{0,16},{16,0},{1,17},{17,1},{2,18},{18,2},{3,19},{19,3},{4,20},{20... | collective-permute-start | bytes 1474568 | tf_op jit(solution)/shard_map/ppermute | solution.py:206
  319.2 16.8 %collective-permute-start.32 = (bf16[1,192,384]{2,1,0:T(8,128)(2,1)S(1)}, bf16[1,192,384]{2,1,0:T(8,128)(2,1)S(1)}, u32[]{:S(2)}, u32[]{:S(2)}) collective-permute-start(bf16[1,192,384]{2,1,0:T(8,128)(2,1)S(1)} %add_convert_fusion.24), channel_id=1, source_target_pairs={{0,8},{1,9},{2,10},{3,11},{4,12},{5,13},{6,14},{7,15},{8,0},{9,1},... | collective-permute-start | bytes 442376 | tf_op jit(solution)/shard_map/ppermute | solution.py:207
  329.9 7.0 %collective-permute-start.23 = (bf16[4,48,640]{2,1,0:T(8,128)(2,1)S(1)}, bf16[4,48,640]{2,1,0:T(8,128)(2,1)S(1)}, u32[]{:S(2)}, u32[]{:S(2)}) collective-permute-start(bf16[4,48,640]{2,1,0:T(8,128)(2,1)S(1)} %get-tuple-element.291), channel_id=1, source_target_pairs={{0,16},{16,0},{1,17},{17,1},{2,18},{18,2},{3,19},{19,3},{4,20},{20... | collective-permute-start | bytes 737288 | tf_op jit(solution)/shard_map/ppermute | solution.py:206
  331.9 19.7 %collective-permute-start.28 = (bf16[4,48,1920]{2,1,0:T(8,128)(2,1)S(1)}, bf16[4,48,1920]{2,1,0:T(8,128)(2,1)S(1)}, u32[]{:S(2)}, u32[]{:S(2)}) collective-permute-start(bf16[4,48,1920]{2,1,0:T(8,128)(2,1)S(1)} %get-tuple-element.279), channel_id=1, source_target_pairs={{0,2},{1,3},{2,0},{3,1},{4,6},{5,7},{6,4},{7,5},{8,10},{9,11},{10,... | collective-permute-start | bytes 2211848 | tf_op jit(solution)/shard_map/ppermute | solution.py:207
  336.7 46.2 %collective-permute-start.41 = (bf16[192,384]{1,0:T(8,128)(2,1)S(1)}, bf16[192,384]{1,0:T(8,128)(2,1)S(1)}, u32[]{:S(2)}, u32[]{:S(2)}) collective-permute-start(bf16[192,384]{1,0:T(8,128)(2,1)S(1)} %get-tuple-element.263), channel_id=1, source_target_pairs={{0,16},{16,0},{1,17},{17,1},{2,18},{18,2},{3,19},{19,3},{4,20},{20... | collective-permute-start | bytes 442376 | tf_op jit(solution)/shard_map/ppermute | solution.py:206
  337.0 4.9 %collective-permute-start.24 = (bf16[2,48,640]{2,1,0:T(8,128)(2,1)S(1)}, bf16[2,48,640]{2,1,0:T(8,128)(2,1)S(1)}, u32[]{:S(2)}, u32[]{:S(2)}) collective-permute-start(bf16[2,48,640]{2,1,0:T(8,128)(2,1)S(1)} %get-tuple-element.299), channel_id=1, source_target_pairs={{0,4},{1,5},{2,6},{3,7},{4,0},{5,1},{6,2},{7,3},{8,12},{9,13},{10,... | collective-permute-start | bytes 368648 | tf_op jit(solution)/shard_map/ppermute | solution.py:207
  338.3 16.4 %collective-permute-start.17 = (bf16[4,48,640]{2,1,0:T(8,128)(2,1)S(1)}, bf16[4,48,640]{2,1,0:T(8,128)(2,1)S(1)}, u32[]{:S(2)}, u32[]{:S(2)}) collective-permute-start(bf16[4,48,640]{2,1,0:T(8,128)(2,1)S(1)} %get-tuple-element.292), channel_id=1, source_target_pairs={{0,2},{1,3},{2,0},{3,1},{4,6},{5,7},{6,4},{7,5},{8,10},{9,11},{10,... | collective-permute-start | bytes 737288 | tf_op jit(solution)/shard_map/ppermute | solution.py:207
  342.0 12.1 %collective-permute-start.25 = (bf16[1,48,640]{2,1,0:T(8,128)(2,1)S(1)}, bf16[1,48,640]{2,1,0:T(8,128)(2,1)S(1)}, u32[]{:S(2)}, u32[]{:S(2)}) collective-permute-start(bf16[1,48,640]{2,1,0:T(8,128)(2,1)S(1)} %add_convert_fusion.31), channel_id=1, source_target_pairs={{0,8},{1,9},{2,10},{3,11},{4,12},{5,13},{6,14},{7,15},{8,0},{9,1},... | collective-permute-start | bytes 184328 | tf_op jit(solution)/shard_map/ppermute | solution.py:207
  351.8 8.5 %collective-permute-start.29 = (bf16[2,48,1920]{2,1,0:T(8,128)(2,1)S(1)}, bf16[2,48,1920]{2,1,0:T(8,128)(2,1)S(1)}, u32[]{:S(2)}, u32[]{:S(2)}) collective-permute-start(bf16[2,48,1920]{2,1,0:T(8,128)(2,1)S(1)} %get-tuple-element.287), channel_id=1, source_target_pairs={{0,4},{1,5},{2,6},{3,7},{4,0},{5,1},{6,2},{7,3},{8,12},{9,13},{10,... | collective-permute-start | bytes 1105928 | tf_op jit(solution)/shard_map/ppermute | solution.py:207
  354.7 23.3 %copy-start.4 = (bf16[48,5120]{1,0:T(8,128)(2,1)S(1)}, bf16[48,5120]{1,0:T(8,128)(2,1)}, u32[]{:S(2)}) copy-start(bf16[48,5120]{1,0:T(8,128)(2,1)} %reduce-scatter.2.cloned.1.call-done) | copy-start | bytes 1474564
  354.8 15.9 %collective-permute-start.19 = (bf16[2,48,640]{2,1,0:T(8,128)(2,1)S(1)}, bf16[2,48,640]{2,1,0:T(8,128)(2,1)S(1)}, u32[]{:S(2)}, u32[]{:S(2)}) collective-permute-start(bf16[2,48,640]{2,1,0:T(8,128)(2,1)S(1)} %get-tuple-element.301), channel_id=1, source_target_pairs={{0,4},{1,5},{2,6},{3,7},{4,0},{5,1},{6,2},{7,3},{8,12},{9,13},{10,... | collective-permute-start | bytes 368648 | tf_op jit(solution)/shard_map/ppermute | solution.py:207
  360.3 13.3 %collective-permute-start.30 = (bf16[1,48,1920]{2,1,0:T(8,128)(2,1)S(1)}, bf16[1,48,1920]{2,1,0:T(8,128)(2,1)S(1)}, u32[]{:S(2)}, u32[]{:S(2)}) collective-permute-start(bf16[1,48,1920]{2,1,0:T(8,128)(2,1)S(1)} %add_convert_fusion.21), channel_id=1, source_target_pairs={{0,8},{1,9},{2,10},{3,11},{4,12},{5,13},{6,14},{7,15},{8,0},{9,1},... | collective-permute-start | bytes 552968 | tf_op jit(solution)/shard_map/ppermute | solution.py:207
  369.0 9.0 %collective-permute-start.18 = (bf16[48,5000]{1,0:T(8,128)(2,1)}, bf16[48,5000]{1,0:T(8,128)(2,1)S(1)}, u32[]{:S(2)}, u32[]{:S(2)}) collective-permute-start(bf16[48,5000]{1,0:T(8,128)(2,1)} %bitcast.73), channel_id=1, source_target_pairs={{0,16},{16,0},{1,17},{17,1},{2,18},{18,2},{3,19},{19,3},{4,20},{20... | collective-permute-start | bytes 1440008 | tf_op jit(solution)/shard_map/ppermute | solution.py:206
  370.7 5.2 %collective-permute-start.20 = (bf16[1,48,640]{2,1,0:T(8,128)(2,1)S(1)}, bf16[1,48,640]{2,1,0:T(8,128)(2,1)S(1)}, u32[]{:S(2)}, u32[]{:S(2)}) collective-permute-start(bf16[1,48,640]{2,1,0:T(8,128)(2,1)S(1)} %add_convert_fusion.34), channel_id=1, source_target_pairs={{0,8},{1,9},{2,10},{3,11},{4,12},{5,13},{6,14},{7,15},{8,0},{9,1},... | collective-permute-start | bytes 184328 | tf_op jit(solution)/shard_map/ppermute | solution.py:207
  382.9 1.8 collective-permute-start.33
  383.0 4.5 %collective-permute-start.39 = (bf16[48,640]{1,0:T(8,128)(2,1)S(1)}, bf16[48,640]{1,0:T(8,128)(2,1)S(1)}, u32[]{:S(2)}, u32[]{:S(2)}) collective-permute-start(bf16[48,640]{1,0:T(8,128)(2,1)S(1)} %get-tuple-element.267), channel_id=1, source_target_pairs={{0,16},{16,0},{1,17},{17,1},{2,18},{18,2},{3,19},{19,3},{4,20},{20... | collective-permute-start | bytes 184328 | tf_op jit(solution)/shard_map/ppermute | solution.py:206
  384.7 4.9 %collective-permute-start.34 = (f32[8,128]{1,0:T(8,128)S(1)}, f32[8,128]{1,0:T(8,128)S(1)}, u32[]{:S(2)}, u32[]{:S(2)}) collective-permute-start(f32[8,128]{1,0:T(8,128)S(1)} %broadcast_add_fusion), channel_id=1, source_target_pairs={{0,8},{1,9},{2,10},{3,11},{4,12},{5,13},{6,14},{7,15},{8,0},{9,1},... | collective-permute-start | bytes 12296 | tf_op jit(solution)/shard_map/ppermute | solution.py:207
  387.4 18.3 %copy-start.24 = (f32[100,48]{0,1:T(8,128)S(1)}, f32[100,48]{0,1:T(8,128)}, u32[]{:S(2)}) copy-start(f32[100,48]{0,1:T(8,128)} %param.29) | copy-start | bytes 57604
  387.5 18.3 %copy-start.25 = (f32[100,48]{0,1:T(8,128)S(1)}, f32[100,48]{0,1:T(8,128)}, u32[]{:S(2)}) copy-start(f32[100,48]{0,1:T(8,128)} %param.43) | copy-start | bytes 57604
  387.5 18.3 %copy-start.26 = (f32[100,48]{0,1:T(8,128)S(1)}, f32[100,48]{0,1:T(8,128)}, u32[]{:S(2)}) copy-start(f32[100,48]{0,1:T(8,128)} %param.36) | copy-start | bytes 57604
  387.5 7.0 %collective-permute-start.40 = (bf16[48,1920]{1,0:T(8,128)(2,1)S(1)}, bf16[48,1920]{1,0:T(8,128)(2,1)S(1)}, u32[]{:S(2)}, u32[]{:S(2)}) collective-permute-start(bf16[48,1920]{1,0:T(8,128)(2,1)S(1)} %get-tuple-element.265), channel_id=1, source_target_pairs={{0,16},{16,0},{1,17},{17,1},{2,18},{18,2},{3,19},{19,3},{4,20},{20... | collective-permute-start | bytes 552968 | tf_op jit(solution)/shard_map/ppermute | solution.py:206
  389.2 7.2 %collective-permute-start.38 = (bf16[48,640]{1,0:T(8,128)(2,1)S(1)}, bf16[48,640]{1,0:T(8,128)(2,1)S(1)}, u32[]{:S(2)}, u32[]{:S(2)}) collective-permute-start(bf16[48,640]{1,0:T(8,128)(2,1)S(1)} %get-tuple-element.269), channel_id=1, source_target_pairs={{0,16},{16,0},{1,17},{17,1},{2,18},{18,2},{3,19},{19,3},{4,20},{20... | collective-permute-start | bytes 184328 | tf_op jit(solution)/shard_map/ppermute | solution.py:206
  389.6 16.8 %copy-start.5 = (f32[48,2304]{1,0:T(8,128)S(1)}, f32[48,2304]{1,0:T(8,128)}, u32[]{:S(2)}) copy-start(f32[48,2304]{1,0:T(8,128)} %param.30) | copy-start | bytes 1327108
  389.6 16.8 %copy-start.19 = (f32[48,2304]{1,0:T(8,128)S(1)}, f32[48,2304]{1,0:T(8,128)}, u32[]{:S(2)}) copy-start(f32[48,2304]{1,0:T(8,128)} %param.44) | copy-start | bytes 1327108
  389.6 5.0 %collective-permute-start.35 = (f32[8,128]{1,0:T(8,128)S(1)}, f32[8,128]{1,0:T(8,128)S(1)}, u32[]{:S(2)}, u32[]{:S(2)}) collective-permute-start(f32[8,128]{1,0:T(8,128)S(1)} %fusion.46), channel_id=1, source_target_pairs={{0,4},{1,5},{2,6},{3,7},{4,0},{5,1},{6,2},{7,3},{8,12},{9,13},{10,... | collective-permute-start | bytes 12296 | tf_op jit(solution)/shard_map/ppermute | solution.py:207
  394.6 3.7 collective-permute-start.36
  398.3 3.6 collective-permute-start.37
  (18 other events, 47.0 us)
Sparse Core Ops, SparseCore 0:
  15.0 94.1 all-gather.2
  112.1 58.3 all-gather.4
  204.5 106.3 reduce-scatter.1
